TPU v7x, 128 devices: a whole 4x4x4 slice. The times are simulated.
128 devices in a mesh: dp: 32 (over x, y_lo, z), outer: 4 (over y_hi, core).
Axes of the slice: x: 4, y: 4 (y_hi: 2, y_lo: 2; y = y_hi * 2 + y_lo), z: 4, core: 2. Of those that a mesh axis runs over, the one named last changes fastest.
Arguments:
- tokens: bfloat16 [65536, 4096], P(('dp', 'outer')), may hold values from -6 to 6
- grad_out: bfloat16 [65536, 11008], P(('dp', 'outer')), may hold values from -0.0234375 to 0.0234375
- projection_basis: bfloat16 [4096, 512], replicated, may hold values from -0.09375 to 0.09375
- first_moment: float32 [512, 11008], P(('dp', 'outer')), may hold values from -3 to 3
- second_moment: float32 [512, 11008], P(('dp', 'outer')), may hold values from 0.2 to 4
Outputs:
- weight_update: float32 [4096, 11008], P('dp')
- new_first: float32 [512, 11008], P(('dp', 'outer'))
- new_second: float32 [512, 11008], P(('dp', 'outer'))
All inputs are finite; a program needn't handle non-finite values.
Results may differ from a plain program's by a relative error of at most 0.003.
Values may be sent and summed in bfloat16 or wider, within the bound.
No kernel may reach another device: no remote copies, remote signals or barrier semaphores. Data moves between devices by JAX's collectives and lax.ppermute only.
A program may use at most 192 MiB of HBM per device.

v0:
```python
import jax
import jax.numpy as jnp
from jax import lax
from jax.sharding import PartitionSpec as P

STEP = 100


beta_first = 0.9
beta_second = 0.999
epsilon = 1e-08
galore_scale = 0.25


def term_rows(columns, grad_out):
    return lax.dot_general(
        columns, grad_out, (((0,), (0,)), ((), ())), preferred_element_type=jnp.float32
    )


def shards(tokens, grad_out, projection_basis, first_moment, second_moment):
    replicas = lax.axis_size("dp")
    projected = jnp.dot(tokens, projection_basis, preferred_element_type=jnp.float32).astype(
        jnp.bfloat16
    )
    owned_grad = lax.psum_scatter(
        term_rows(projected, grad_out), ("dp", "outer"), scatter_dimension=0, tiled=True
    )
    new_first = beta_first * first_moment + (1.0 - beta_first) * owned_grad
    new_second = beta_second * second_moment + (1.0 - beta_second) * owned_grad * owned_grad
    first_bias = 1.0 - beta_first**STEP
    second_bias = 1.0 - beta_second**STEP
    low_update = (new_first / first_bias / (jnp.sqrt(new_second / second_bias) + epsilon)).astype(
        jnp.bfloat16
    )
    local_width = projection_basis.shape[0] // replicas
    basis_rows = lax.dynamic_slice_in_dim(
        projection_basis, lax.axis_index("dp") * local_width, local_width, 0
    )
    expanded = jnp.dot(
        basis_rows,
        lax.all_gather(low_update, ("dp", "outer"), axis=0, tiled=True),
        preferred_element_type=jnp.float32,
    )
    weight_update = -galore_scale * expanded
    return (weight_update, new_first, new_second)


def solution(mesh):
    in_specs = (
        P(("dp", "outer"), None),
        P(("dp", "outer"), None),
        P(),
        P(("dp", "outer"), None),
        P(("dp", "outer"), None),
    )
    out_specs = (P("dp", None), P(("dp", "outer"), None), P(("dp", "outer"), None))
    return jax.shard_map(shards, mesh=mesh, in_specs=in_specs, out_specs=out_specs, check_vma=False)
```

profile of v0, /device:TPU:1, one launch (start us, length us, event | category | flops | bytes accessed | tf_op | source)
XLA Modules:
  0.0 496.2 jit_solution(15750251676325471300)
XLA Ops:
  7.2 0.0 all-reduce.3.cloned.1.call-start
  7.2 0.0 copy-start
  7.2 5.9 %convolution_convert_fusion = bf16[512,512]{1,0:T(8,128)(2,1)S(1)} fusion(bf16[512,4096]{1,0:T(8,128)(2,1)} %param.5, bf16[4096,512]{1,0:T(8,128)(2,1)} %param.7), kind=kOutput, calls=%fused_computation.1 | convolution fusion | flops 2147745792 | bytes 8912896 | tf_op jit(solution)/shard_map/dot_general | solution.py:23
  13.1 0.7 copy-done
  13.9 10.8 %fusion.6 = f32[512,11008]{1,0:T(8,128)} fusion(bf16[512,512]{1,0:T(8,128)(2,1)S(1)} %convolution_convert_fusion, bf16[512,11008]{1,0:T(8,128)(2,1)S(1)} %copy-done), kind=kOutput, calls=%fused_computation.10 | convolution fusion | flops 5771362304 | bytes 34340864 | tf_op jit(solution)/shard_map/dot_general | solution.py:16
  24.7 0.0 copy-start.1
  24.7 0.0 copy-start.2
  24.7 0.0 all-reduce.3.cloned.1.call-update
  24.7 0.0 all-gather.3.cloned.1.call-start
  24.8 229.9 %all-reduce.3.cloned.1.call-done = f32[512,11008]{1,0:T(8,128)} async-done(((f32[512,11008]{1,0:T(8,128)}), f32[512,11008]{1,0:T(8,128)}) %all-reduce.3.cloned.1.call-update) | async-done | bytes 22544400
  254.7 0.0 copy-done.1
  254.7 0.0 copy-done.2
  254.7 2.0 fusion.3
  256.7 0.0 all-gather.3.cloned.1.call-update
  256.7 205.8 %all-gather.3.cloned.1.call-done = bf16[128,4,11008]{2,1,0:T(4,128)(2,1)} async-done(((bf16[1,4,11008]{2,1,0:T(4,128)(2,1)}), bf16[128,4,11008]{2,1,0:T(4,128)(2,1)}) %all-gather.3.cloned.1.call-update) | async-done | bytes 11272208 | tf_op jit(solution)/shard_map/all_gather | solution.py:42
  462.5 18.4 %reshape.7 = bf16[512,11008]{1,0:T(8,128)(2,1)} reshape(bf16[128,4,11008]{2,1,0:T(4,128)(2,1)} %all-gather.3.cloned.1.call-done) | data formatting | bytes 22544384
  480.9 8.4 %convolution_multiply_fusion = f32[128,11008]{1,0:T(8,128)} fusion(bf16[512,11008]{1,0:T(8,128)(2,1)} %reshape.7, bf16[4096,512]{1,0:T(8,128)(2,1)} %param.7, s32[]{:T(128)S(6)} %select_n.3), kind=kOutput, calls=%fused_computation | convolution fusion | flops 1444249600 | bytes 17039364 | tf_op jit(solution)/shard_map/dot_general | solution.py:40
Async XLA Ops:
  7.2 247.6 %all-reduce.3.cloned.1.call-start = ((), (), s32[]{:S(2)}) async-start(), calls=%async_computation.1 | async-start | bytes 45088768
  7.2 6.7 %copy-start = (bf16[512,11008]{1,0:T(8,128)(2,1)S(1)}, bf16[512,11008]{1,0:T(8,128)(2,1)}, u32[]{:S(2)}) copy-start(bf16[512,11008]{1,0:T(8,128)(2,1)} %param.6) | copy-start | bytes 33816580
  24.7 230.0 %copy-start.1 = (f32[4,11008]{1,0:T(4,128)S(1)}, f32[4,11008]{1,0:T(4,128)}, u32[]{:S(2)}) copy-start(f32[4,11008]{1,0:T(4,128)} %param.8) | copy-start | bytes 528388
  24.7 230.0 %copy-start.2 = (f32[4,11008]{1,0:T(4,128)S(1)}, f32[4,11008]{1,0:T(4,128)}, u32[]{:S(2)}) copy-start(f32[4,11008]{1,0:T(4,128)} %param.9) | copy-start | bytes 528388
  24.7 437.8 %all-gather.3.cloned.1.call-start = ((), (), s32[]{:S(2)}) async-start(), calls=%async_computation | async-start | bytes 11360256 | tf_op jit(solution)/shard_map/all_gather | solution.py:42
Sparse Core Ops, SparseCore 0:
  24.9 229.8 all-reduce.2
  257.1 205.3 all-gather.2
where the time goes:
time: 497 us; the launch traced here: 496 us
  waiting for transfers between devices  436 us (88%)
  matrix products  25.2 us (5%)
  local copies, waits for them, and re-layouts  19.1 us (4%)
  between operations  14.1 us (3%)
    unnamed x3, waiting for transfers between devices  230 us
    all_gather x1, waiting for transfers between devices, shards(): lax.all_gather(low_update, ('dp', 'outer'), axis=0, tiled=True)  206 us
    unnamed x7, local copies, waits for them, and re-layouts  19.1 us
    dot_general x1, matrix products, term_rows(): lax.dot_general(columns, grad_out, (((0,), (0,)), ((), ())), preferred_el...  10.8 us
  transfers between devices with their start and end apart: 2, of which 2 were waited for; matrix products, arithmetic and copies ran while one was open for 0% of the time, Pallas kernels for 0%

commit v1 on v0

v1 whole, which is shorter than its diff:
```python
import itertools

import jax
import jax.numpy as jnp
from jax import lax
from jax.experimental import pallas as pl
from jax.experimental.pallas import tpu as pltpu
from jax.sharding import PartitionSpec as P

STEP = 100

beta_first = 0.9
beta_second = 0.999
epsilon = 1e-08
galore_scale = 0.25

AXES = ("dp", "outer")
WIDTH = 1280
PIECES = ((0, 3840), (3840, 3840), (7680, 3328))
ORDERS = ((0, 1, 2), (1, 2, 0), (2, 0, 1))


def linear(x, y, z, core):
    return ((((x % 4) * 2 + y % 2) * 4 + z % 4) * 2 + (y % 4) // 2) * 2 + core


def ring(axis, sign):
    pairs = []
    for x, y, z, core in itertools.product(range(4), range(4), range(4), range(2)):
        there = [x, y, z]
        there[axis] += sign * (1 - 2 * core)
        pairs.append((linear(x, y, z, core), linear(*there, core)))
    return pairs


SWAP = [(2 * i + core, 2 * i + 1 - core) for i in range(64) for core in range(2)]
UP = [ring(axis, 1) for axis in range(3)]
DOWN = [ring(axis, -1) for axis in range(3)]


def send(value, pairs):
    return lax.ppermute(value, AXES, pairs)


def rank_order(order, dp, outer):
    here = (dp // 8, (outer // 2) * 2 + (dp // 4) % 2, dp % 4)
    place = lax.iota(jnp.int32, 512)
    hops = (place // 128, (place // 16) % 4, (place // 4) % 4)
    core = (outer % 2 + (place // 64) % 2) % 2
    there = [None, None, None]
    for hop, axis in zip(hops, order):
        there[axis] = (here[axis] + 4 + (1 - 2 * core) * hop) % 4
    return linear(*there, core) * 4 + place % 4


def term_kernel(projected_ref, grad_ref, own_ref, other_ref):
    total = jnp.dot(projected_ref[...], grad_ref[...], preferred_element_type=jnp.float32)
    own_ref[...] = total[:64].astype(jnp.bfloat16)
    other_ref[...] = total[64:].astype(jnp.bfloat16)


def term_rows(projected, grad_out, hop):
    tokens, width = grad_out.shape
    shape = jax.ShapeDtypeStruct((64, width), jnp.bfloat16)
    block = pl.BlockSpec((64, WIDTH), lambda j: (0, j))
    return pl.pallas_call(
        term_kernel,
        grid=(pl.cdiv(width, WIDTH),),
        in_specs=[
            pl.BlockSpec((128, tokens), lambda j: (j // 3 * 4 + hop, 0)),
            pl.BlockSpec((tokens, WIDTH), lambda j: (0, j)),
        ],
        out_specs=[block, block],
        out_shape=[shape, shape],
        cost_estimate=pl.CostEstimate(
            flops=2 * 128 * tokens * width,
            bytes_accessed=2 * (tokens + 128) * width,
            transcendentals=0,
        ),
        name="terms",
    )(projected, grad_out)


def expand_kernel(basis_ref, *refs):
    out_ref = refs[-1]
    step = pl.program_id(0)
    for piece in range(3):

        @pl.when(step // 3 == piece)
        def _(piece=piece):
            low = jnp.concatenate([ref[...] for ref in refs[8 * piece : 8 * piece + 8]], axis=0)
            out_ref[...] = -galore_scale * jnp.dot(
                basis_ref[...], low, preferred_element_type=jnp.float32
            )


def expand(basis_rows, blocks, width):
    rows = basis_rows.shape[0]
    specs = []
    for piece in range(3):
        spec = pl.BlockSpec((64, WIDTH), lambda j, piece=piece: (0, jnp.clip(j - 3 * piece, 0, 2)))
        specs += [spec] * 8
    return pl.pallas_call(
        expand_kernel,
        grid=(pl.cdiv(width, WIDTH),),
        in_specs=[pl.BlockSpec((rows, 512), lambda j: (0, j // 3))] + specs,
        out_specs=pl.BlockSpec((rows, WIDTH), lambda j: (0, j)),
        out_shape=jax.ShapeDtypeStruct((rows, width), jnp.float32),
        cost_estimate=pl.CostEstimate(
            flops=2 * rows * 512 * width,
            bytes_accessed=(2 * 512 + 4 * rows) * width,
            transcendentals=0,
        ),
        compiler_params=pltpu.CompilerParams(vmem_limit_bytes=48 * 1024 * 1024),
        name="expand",
    )(basis_rows, *itertools.chain(*blocks))


def shards(tokens, grad_out, projection_basis, first_moment, second_moment):
    width = grad_out.shape[1]
    dp, outer = lax.axis_index("dp"), lax.axis_index("outer")
    f32, bf16 = jnp.float32, jnp.bfloat16

    places = jnp.concatenate([rank_order(order, dp, outer) for order in ORDERS])
    picks = (lax.broadcasted_iota(jnp.int32, (512, 1536), 0) == places[None, :]).astype(bf16)

    projected = jnp.dot(tokens, projection_basis, preferred_element_type=f32).astype(bf16)
    projected = lax.dot_general(
        picks, projected, (((0,), (1,)), ((), ())), preferred_element_type=f32
    ).astype(bf16)
    local_width = projection_basis.shape[0] // 32
    basis_rows = lax.dynamic_slice_in_dim(projection_basis, dp * local_width, local_width, 0)
    basis_rows = jnp.dot(basis_rows, picks, preferred_element_type=f32).astype(bf16)

    sums = [None] * 3
    for hop in (3, 2, 1, 0):
        own, other = term_rows(projected, grad_out, hop)
        other = send(other, SWAP)
        for piece, (start, size) in enumerate(PIECES):
            total = own[:, start : start + size].astype(f32) + other[:, start : start + size].astype(f32)
            if hop < 3:
                total = total + send(sums[piece], UP[ORDERS[piece][0]]).astype(f32)
            sums[piece] = total.astype(bf16) if hop else total
    for stage, rows, kind in ((1, 16, bf16), (2, 4, f32)):
        held = sums
        sums = [h[3 * rows :].astype(kind) for h in held]
        for hop in (2, 1, 0):
            for piece in range(3):
                total = held[piece][hop * rows : (hop + 1) * rows] + send(
                    sums[piece], UP[ORDERS[piece][stage]]
                ).astype(f32)
                sums[piece] = total.astype(kind) if hop else total
    owned_grad = jnp.concatenate(sums, axis=1)

    new_first = beta_first * first_moment + (1.0 - beta_first) * owned_grad
    new_second = beta_second * second_moment + (1.0 - beta_second) * owned_grad * owned_grad
    first_bias = 1.0 - beta_first**STEP
    second_bias = 1.0 - beta_second**STEP
    low_update = (new_first / first_bias / (jnp.sqrt(new_second / second_bias) + epsilon)).astype(bf16)

    low = [low_update[:, start : start + size] for start, size in PIECES]
    for stage in (2, 1, 0):
        parts = [[value] for value in low]
        for _ in range(3):
            for piece in range(3):
                parts[piece].append(send(parts[piece][-1], DOWN[ORDERS[piece][stage]]))
        if stage:
            low = [jnp.concatenate(p, axis=0) for p in parts]
    blocks = [
        [block for part in parts[piece] for block in (part, send(part, SWAP))] for piece in range(3)
    ]
    weight_update = expand(basis_rows, blocks, width)
    return (weight_update, new_first, new_second)


def solution(mesh):
    in_specs = (
        P(("dp", "outer"), None),
        P(("dp", "outer"), None),
        P(),
        P(("dp", "outer"), None),
        P(("dp", "outer"), None),
    )
    out_specs = (P("dp", None), P(("dp", "outer"), None), P(("dp", "outer"), None))
    return jax.shard_map(shards, mesh=mesh, in_specs=in_specs, out_specs=out_specs, check_vma=False)
```

time: 497 us -> 239 us (0.48)
  waiting for transfers between devices: 436 us -> 65.1 us
  starting transfers between devices: 0.08 us -> 100 us
  Pallas kernels: 0 us -> 49.5 us
  local copies, waits for them, and re-layouts: 19.1 us -> 2.83 us
  matrix products: 25.2 us -> 9.63 us
  between operations: 14.1 us -> 1.34 us
  other arithmetic: 1.96 us -> 9.11 us
    unnamed x3 -> x0, waiting for transfers between devices: 230 us -> none
    all_gather x1 -> x0, waiting for transfers between devices: 206 us -> none  [shards(): lax.all_gather(low_update, ('dp', 'outer'), axis=0, tiled=True)]
    ppermute x0 -> x70, starting transfers between devices: none -> 100 us  [send(): return lax.ppermute(value, AXES, pairs)]
    ppermute x0 -> x70, waiting for transfers between devices: none -> 65.1 us  [send(): return lax.ppermute(value, AXES, pairs)]
    pallas_call x0 -> x5, Pallas kernels: none -> 49.5 us  [the longest x4 39.2 us: term_rows(): pl.pallas_call(term_kernel, grid=(pl.cdiv(width, WIDTH),), in_specs=[pl.B...]
    unnamed x7 -> x32, local copies, waits for them, and re-layouts: 19.1 us -> 2.37 us
    dot_general x3 -> x2, matrix products: 25.2 us -> 9.63 us  [the longest x1 7.88 us: shards(): lax.dot_general(picks, projected, (((0,), (1,)), ((), ())), preferred_ele...]
    convert_element_type x0 -> x13, other arithmetic: none -> 8.06 us  [the longest x6 6.92 us: shards(): sums[piece] = total.astype(bf16) if hop else total]
  transfers between devices with their start and end apart: 2 -> 70, of which waited for: 2 -> 29; matrix products, arithmetic and copies ran while one was open for 0% -> 4% of each run, Pallas kernels for 0% -> 12%
where the time goes in v1:
time: 239 us; the launch traced here: 238 us
  starting transfers between devices  100 us (42%)
  waiting for transfers between devices  65.1 us (27%)
  Pallas kernels  49.5 us (21%)
  matrix products  9.63 us (4%)
  other arithmetic  9.11 us (4%)
  local copies, waits for them, and re-layouts  2.83 us (1%)
    ppermute x70, starting transfers between devices, send(): return lax.ppermute(value, AXES, pairs)  100 us
    ppermute x70, waiting for transfers between devices, send(): return lax.ppermute(value, AXES, pairs)  65.1 us
    pallas_call x4, Pallas kernels, term_rows(): pl.pallas_call(term_kernel, grid=(pl.cdiv(width, WIDTH),), in_specs=[pl.B...  39.2 us
    pallas_call x1, Pallas kernels, expand(): pl.pallas_call(expand_kernel, grid=(pl.cdiv(width, WIDTH),), in_specs=[pl...  10.3 us
    dot_general x1, matrix products, shards(): lax.dot_general(picks, projected, (((0,), (1,)), ((), ())), preferred_ele...  7.88 us
    convert_element_type x6, other arithmetic, shards(): sums[piece] = total.astype(bf16) if hop else total  6.92 us
  transfers between devices with their start and end apart: 70, of which 29 were waited for; matrix products, arithmetic and copies ran while one was open for 4% of the time, Pallas kernels for 12%

profile of v1, /device:TPU:1, one launch (start us, length us, event | category | flops | bytes accessed | tf_op | source)
XLA Modules:
  0.0 237.7 jit_solution(13686371141123936970)
XLA Ops:
  0.8 7.9 %convolution_convert_fusion.projected_ref = bf16[1536,512]{1,0:T(8,128)(2,1)} fusion(s32[1536]{0:T(1024)S(1)} %pad_add_fusion, bf16[512,4096]{1,0:T(8,128)(2,1)} %param.5, bf16[4096,512]{1,0:T(8,128)(2,1)} %param.7), kind=kOutput, calls=%fused_computation.3 | convolution fusion | flops 2955411456 | bytes 9967616 | tf_op jit(solution)/shard_map/dot_general | solution.py:128
  8.7 9.8 %terms.7 = (bf16[64,11008]{1,0:T(8,128)(2,1)}, bf16[64,11008]{1,0:T(8,128)(2,1)}) custom-call(bf16[1536,512]{1,0:T(8,128)(2,1)} %convolution_convert_fusion.projected_ref, bf16[512,11008]{1,0:T(8,128)(2,1)} %grad_ref.7), custom_call_target="tpu_custom_call" | custom-call | flops 1442840576 | bytes 14090240 | tf_op jit(solution)/shard_map/terms/pallas_call | solution.py:66
  19.9 9.8 %terms.6 = (bf16[64,11008]{1,0:T(8,128)(2,1)}, bf16[64,11008]{1,0:T(8,128)(2,1)}) custom-call(bf16[1536,512]{1,0:T(8,128)(2,1)} %convolution_convert_fusion.projected_ref, bf16[512,11008]{1,0:T(8,128)(2,1)} %grad_ref.7), custom_call_target="tpu_custom_call" | custom-call | flops 1442840576 | bytes 14090240 | tf_op jit(solution)/shard_map/terms/pallas_call | solution.py:66
  30.0 3.9 %collective-permute-start.22 = (bf16[64,3328]{1,0:T(8,128)(2,1)S(1)}, bf16[64,3328]{1,0:T(8,128)(2,1)}, u32[]{:S(2)}, u32[]{:S(2)}) collective-permute-start(bf16[64,3328]{1,0:T(8,128)(2,1)S(1)} %add_convert_fusion.8), channel_id=1, source_target_pairs={{0,4},{1,13},{4,8},{5,1},{8,12},{9,5},{12,0},{13,9},{16,20},{17,29... | collective-permute-start | bytes 1277960 | tf_op jit(solution)/shard_map/ppermute | solution.py:42
  33.9 9.8 %terms.5 = (bf16[64,11008]{1,0:T(8,128)(2,1)}, bf16[64,11008]{1,0:T(8,128)(2,1)}) custom-call(bf16[1536,512]{1,0:T(8,128)(2,1)} %convolution_convert_fusion.projected_ref, bf16[512,11008]{1,0:T(8,128)(2,1)} %grad_ref.7), custom_call_target="tpu_custom_call" | custom-call | flops 1442840576 | bytes 14090240 | tf_op jit(solution)/shard_map/terms/pallas_call | solution.py:66
  46.3 9.8 %terms.4 = (bf16[64,11008]{1,0:T(8,128)(2,1)}, bf16[64,11008]{1,0:T(8,128)(2,1)}) custom-call(bf16[1536,512]{1,0:T(8,128)(2,1)} %convolution_convert_fusion.projected_ref, bf16[512,11008]{1,0:T(8,128)(2,1)} %grad_ref.7), custom_call_target="tpu_custom_call" | custom-call | flops 1442840576 | bytes 14090240 | tf_op jit(solution)/shard_map/terms/pallas_call | solution.py:66
  57.5 3.0 %collective-permute-start.24 = (bf16[64,3328]{1,0:T(8,128)(2,1)S(1)}, bf16[64,3328]{1,0:T(8,128)(2,1)S(1)}, u32[]{:S(2)}, u32[]{:S(2)}) collective-permute-start(bf16[64,3328]{1,0:T(8,128)(2,1)S(1)} %add_convert_fusion.6), channel_id=1, source_target_pairs={{0,4},{1,13},{4,8},{5,1},{8,12},{9,5},{12,0},{13,9},{16,20},{17,29... | collective-permute-start | bytes 1277960 | tf_op jit(solution)/shard_map/ppermute | solution.py:42
  60.8 2.6 %collective-permute-start.4 = (bf16[64,3840]{1,0:T(8,128)(2,1)S(1)}, bf16[64,3840]{1,0:T(8,128)(2,1)S(1)}, u32[]{:S(2)}, u32[]{:S(2)}) collective-permute-start(bf16[64,3840]{1,0:T(8,128)(2,1)S(1)} %get-tuple-element.28), channel_id=1, source_target_pairs={{0,32},{1,97},{4,36},{5,101},{8,40},{9,105},{12,44},{13,109},{16,4... | collective-permute-start | bytes 1474568 | tf_op jit(solution)/shard_map/ppermute | solution.py:42
  63.3 2.7 %collective-permute-start.13 = (bf16[64,3840]{1,0:T(8,128)(2,1)S(1)}, bf16[64,3840]{1,0:T(8,128)(2,1)S(1)}, u32[]{:S(2)}, u32[]{:S(2)}) collective-permute-start(bf16[64,3840]{1,0:T(8,128)(2,1)S(1)} %get-tuple-element.29), channel_id=1, source_target_pairs={{0,16},{1,19},{4,20},{5,23},{8,24},{9,27},{12,28},{13,31},{16,2},{... | collective-permute-start | bytes 1474568 | tf_op jit(solution)/shard_map/ppermute | solution.py:42
  69.1 2.7 %collective-permute-done.13 = bf16[64,3840]{1,0:T(8,128)(2,1)S(1)} collective-permute-done((bf16[64,3840]{1,0:T(8,128)(2,1)S(1)}, bf16[64,3840]{1,0:T(8,128)(2,1)S(1)}, u32[]{:S(2)}, u32[]{:S(2)}) %collective-permute-start.13) | collective-permute-done | bytes 491552 | tf_op jit(solution)/shard_map/ppermute | solution.py:42
  74.0 3.1 %collective-permute-start.14 = (bf16[64,3840]{1,0:T(8,128)(2,1)S(1)}, bf16[64,3840]{1,0:T(8,128)(2,1)S(1)}, u32[]{:S(2)}, u32[]{:S(2)}) collective-permute-start(bf16[64,3840]{1,0:T(8,128)(2,1)S(1)} %get-tuple-element.27), channel_id=1, source_target_pairs={{0,16},{1,19},{4,20},{5,23},{8,24},{9,27},{12,28},{13,31},{16,2},{... | collective-permute-start | bytes 1474568 | tf_op jit(solution)/shard_map/ppermute | solution.py:42
  77.4 4.0 %collective-permute-done.5 = bf16[64,3840]{1,0:T(8,128)(2,1)S(1)} collective-permute-done((bf16[64,3840]{1,0:T(8,128)(2,1)S(1)}, bf16[64,3840]{1,0:T(8,128)(2,1)S(1)}, u32[]{:S(2)}, u32[]{:S(2)}) %collective-permute-start.5) | collective-permute-done | bytes 491552 | tf_op jit(solution)/shard_map/ppermute | solution.py:42
  84.8 3.1 %collective-permute-start.15 = (bf16[64,3840]{1,0:T(8,128)(2,1)S(1)}, bf16[64,3840]{1,0:T(8,128)(2,1)S(1)}, u32[]{:S(2)}, u32[]{:S(2)}) collective-permute-start(bf16[64,3840]{1,0:T(8,128)(2,1)S(1)} %get-tuple-element.25), channel_id=1, source_target_pairs={{0,16},{1,19},{4,20},{5,23},{8,24},{9,27},{12,28},{13,31},{16,2},{... | collective-permute-start | bytes 1474568 | tf_op jit(solution)/shard_map/ppermute | solution.py:42
  88.2 4.2 %collective-permute-done.6 = bf16[64,3840]{1,0:T(8,128)(2,1)S(1)} collective-permute-done((bf16[64,3840]{1,0:T(8,128)(2,1)S(1)}, bf16[64,3840]{1,0:T(8,128)(2,1)S(1)}, u32[]{:S(2)}, u32[]{:S(2)}) %collective-permute-start.6) | collective-permute-done | bytes 491552 | tf_op jit(solution)/shard_map/ppermute | solution.py:42
  94.4 3.4 %collective-permute-start.7 = (bf16[16,3840]{1,0:T(8,128)(2,1)S(1)}, bf16[16,3840]{1,0:T(8,128)(2,1)S(1)}, u32[]{:S(2)}, u32[]{:S(2)}) collective-permute-start(bf16[16,3840]{1,0:T(8,128)(2,1)S(1)} %slice.304), channel_id=1, source_target_pairs={{0,16},{1,19},{4,20},{5,23},{8,24},{9,27},{12,28},{13,31},{16,2},{... | collective-permute-start | bytes 368648 | tf_op jit(solution)/shard_map/ppermute | solution.py:42
  100.9 2.5 %collective-permute-start.29 = (f32[4,3328]{1,0:T(4,128)S(1)}, f32[4,3328]{1,0:T(4,128)S(1)}, u32[]{:S(2)}, u32[]{:S(2)}) collective-permute-start(f32[4,3328]{1,0:T(4,128)S(1)} %slice_add_fusion.15), channel_id=1, source_target_pairs={{0,16},{1,19},{4,20},{5,23},{8,24},{9,27},{12,28},{13,31},{16,2},{... | collective-permute-start | bytes 159752 | tf_op jit(solution)/shard_map/ppermute | solution.py:42
  104.7 3.3 %collective-permute-start.30 = (f32[4,3328]{1,0:T(4,128)S(1)}, f32[4,3328]{1,0:T(4,128)S(1)}, u32[]{:S(2)}, u32[]{:S(2)}) collective-permute-start(f32[4,3328]{1,0:T(4,128)S(1)} %slice_add_fusion.16), channel_id=1, source_target_pairs={{0,16},{1,19},{4,20},{5,23},{8,24},{9,27},{12,28},{13,31},{16,2},{... | collective-permute-start | bytes 159752 | tf_op jit(solution)/shard_map/ppermute | solution.py:42
  109.2 2.6 %collective-permute-done.18 = bf16[16,3840]{1,0:T(8,128)(2,1)S(1)} collective-permute-done((bf16[16,3840]{1,0:T(8,128)(2,1)S(1)}, bf16[16,3840]{1,0:T(8,128)(2,1)S(1)}, u32[]{:S(2)}, u32[]{:S(2)}) %collective-permute-start.18) | collective-permute-done | bytes 122912 | tf_op jit(solution)/shard_map/ppermute | solution.py:42
  125.5 4.2 %collective-permute-done.57 = bf16[4,3328]{1,0:T(4,128)(2,1)S(1)} collective-permute-done((bf16[4,3328]{1,0:T(4,128)(2,1)S(1)}, bf16[4,3328]{1,0:T(4,128)(2,1)S(1)}, u32[]{:S(2)}, u32[]{:S(2)}) %collective-permute-start.57) | collective-permute-done | bytes 26656 | tf_op jit(solution)/shard_map/ppermute | solution.py:42
  129.7 3.9 %collective-permute-done.58 = bf16[4,3328]{1,0:T(4,128)(2,1)S(1)} collective-permute-done((bf16[4,3328]{1,0:T(4,128)(2,1)S(1)}, bf16[4,3328]{1,0:T(4,128)(2,1)S(1)}, u32[]{:S(2)}, u32[]{:S(2)}) %collective-permute-start.58) | collective-permute-done | bytes 26656 | tf_op jit(solution)/shard_map/ppermute | solution.py:42
  133.7 3.9 %collective-permute-done.59 = bf16[4,3328]{1,0:T(4,128)(2,1)S(1)} collective-permute-done((bf16[4,3328]{1,0:T(4,128)(2,1)S(1)}, bf16[4,3328]{1,0:T(4,128)(2,1)S(1)}, u32[]{:S(2)}, u32[]{:S(2)}) %collective-permute-start.59) | collective-permute-done | bytes 26656 | tf_op jit(solution)/shard_map/ppermute | solution.py:42
  139.5 3.4 %collective-permute-done.31 = bf16[4,3840]{1,0:T(4,128)(2,1)S(1)} collective-permute-done((bf16[4,3840]{1,0:T(4,128)(2,1)S(1)}, bf16[4,3840]{1,0:T(4,128)(2,1)S(1)}, u32[]{:S(2)}, u32[]{:S(2)}) %collective-permute-start.31) | collective-permute-done | bytes 30752 | tf_op jit(solution)/shard_map/ppermute | solution.py:42
  143.7 3.2 %collective-permute-done.32 = bf16[4,3840]{1,0:T(4,128)(2,1)S(1)} collective-permute-done((bf16[4,3840]{1,0:T(4,128)(2,1)S(1)}, bf16[4,3840]{1,0:T(4,128)(2,1)S(1)}, u32[]{:S(2)}, u32[]{:S(2)}) %collective-permute-start.32) | collective-permute-done | bytes 30752 | tf_op jit(solution)/shard_map/ppermute | solution.py:42
  153.2 3.9 %collective-permute-done.62 = bf16[16,3328]{1,0:T(8,128)(2,1)S(1)} collective-permute-done((bf16[16,3328]{1,0:T(8,128)(2,1)S(1)}, bf16[16,3328]{1,0:T(8,128)(2,1)S(1)}, u32[]{:S(2)}, u32[]{:S(2)}) %collective-permute-start.62) | collective-permute-done | bytes 106528 | tf_op jit(solution)/shard_map/ppermute | solution.py:42
  160.7 2.5 %collective-permute-done.35 = bf16[16,3840]{1,0:T(8,128)(2,1)S(1)} collective-permute-done((bf16[16,3840]{1,0:T(8,128)(2,1)S(1)}, bf16[16,3840]{1,0:T(8,128)(2,1)S(1)}, u32[]{:S(2)}, u32[]{:S(2)}) %collective-permute-start.35) | collective-permute-done | bytes 122912 | tf_op jit(solution)/shard_map/ppermute | solution.py:42
  163.2 3.9 %collective-permute-done.48 = bf16[16,3840]{1,0:T(8,128)(2,1)S(1)} collective-permute-done((bf16[16,3840]{1,0:T(8,128)(2,1)S(1)}, bf16[16,3840]{1,0:T(8,128)(2,1)S(1)}, u32[]{:S(2)}, u32[]{:S(2)}) %collective-permute-start.48) | collective-permute-done | bytes 122912 | tf_op jit(solution)/shard_map/ppermute | solution.py:42
  168.3 3.7 %collective-permute-done.49 = bf16[16,3840]{1,0:T(8,128)(2,1)S(1)} collective-permute-done((bf16[16,3840]{1,0:T(8,128)(2,1)S(1)}, bf16[16,3840]{1,0:T(8,128)(2,1)S(1)}, u32[]{:S(2)}, u32[]{:S(2)}) %collective-permute-start.49) | collective-permute-done | bytes 122912 | tf_op jit(solution)/shard_map/ppermute | solution.py:42
  172.2 20.9 %collective-permute-start.63 = (bf16[64,3328]{1,0:T(8,128)(2,1)S(1)}, bf16[64,3328]{1,0:T(8,128)(2,1)S(1)}, u32[]{:S(2)}, u32[]{:S(2)}) collective-permute-start(bf16[64,3328]{1,0:T(8,128)(2,1)S(1)} %concatenate.34.refs_16_), channel_id=1, source_target_pairs={{0,1},{1,0},{2,3},{3,2},{4,5},{5,4},{6,7},{7,6},{8,9},{9,8},{10,11... | collective-permute-start | bytes 1277960 | tf_op jit(solution)/shard_map/ppermute | solution.py:42
  196.0 8.8 %collective-permute-start.65 = (bf16[64,3328]{1,0:T(8,128)(2,1)S(1)}, bf16[64,3328]{1,0:T(8,128)(2,1)S(1)}, u32[]{:S(2)}, u32[]{:S(2)}) collective-permute-start(bf16[64,3328]{1,0:T(8,128)(2,1)S(1)} %collective-permute-done.64.refs_18_), channel_id=1, source_target_pairs={{0,1},{1,0},{2,3},{3,2},{4,5},{5,4},{6,7},{7,6},{8,9},{9,8},{10,11... | collective-permute-start | bytes 1277960 | tf_op jit(solution)/shard_map/ppermute | solution.py:42
  204.9 6.4 %collective-permute-start.52 = (bf16[64,3840]{1,0:T(8,128)(2,1)S(1)}, bf16[64,3840]{1,0:T(8,128)(2,1)S(1)}, u32[]{:S(2)}, u32[]{:S(2)}) collective-permute-start(bf16[64,3840]{1,0:T(8,128)(2,1)S(1)} %collective-permute-done.51.refs_10_), channel_id=1, source_target_pairs={{0,1},{1,0},{2,3},{3,2},{4,5},{5,4},{6,7},{7,6},{8,9},{9,8},{10,11... | collective-permute-start | bytes 1474568 | tf_op jit(solution)/shard_map/ppermute | solution.py:42
  213.6 4.1 %collective-permute-start.67 = (bf16[64,3328]{1,0:T(8,128)(2,1)S(1)}, bf16[64,3328]{1,0:T(8,128)(2,1)S(1)}, u32[]{:S(2)}, u32[]{:S(2)}) collective-permute-start(bf16[64,3328]{1,0:T(8,128)(2,1)S(1)} %collective-permute-done.66.refs_20_), channel_id=1, source_target_pairs={{0,1},{1,0},{2,3},{3,2},{4,5},{5,4},{6,7},{7,6},{8,9},{9,8},{10,11... | collective-permute-start | bytes 1277960 | tf_op jit(solution)/shard_map/ppermute | solution.py:42
  227.2 10.3 %expand.1 = f32[128,11008]{1,0:T(8,128)} custom-call(bf16[128,1536]{1,0:T(8,128)(2,1)S(1)} %fusion.2.basis_ref, bf16[64,3840]{1,0:T(8,128)(2,1)S(1)} %concatenate.30.refs_0_, bf16[64,3840]{1,0:T(8,128)(2,1)S(1)} %collective-permute-done.37.refs_1_, bf16[64,3840]{1,0:T(8,128)(2,1)S(1)} %collective-permute-done.38.refs_2_, ...), custom_call_target="tpu_custom_call" | custom-call | flops 1442840576 | bytes 16908288 | tf_op jit(solution)/shard_map/expand/pallas_call | solution.py:103
  (191 shorter events, 65.2 us)
Async XLA Ops:
  18.5 11.4 %collective-permute-start.3 = (bf16[64,11008]{1,0:T(8,128)(2,1)}, bf16[64,11008]{1,0:T(8,128)(2,1)S(1)}, u32[]{:S(2)}, u32[]{:S(2)}) collective-permute-start(bf16[64,11008]{1,0:T(8,128)(2,1)} %get-tuple-element.18), channel_id=1, source_target_pairs={{0,1},{1,0},{2,3},{3,2},{4,5},{5,4},{6,7},{7,6},{8,9},{9,8},{10,11... | collective-permute-start | bytes 4227080 | tf_op jit(solution)/shard_map/ppermute | solution.py:42
  29.7 13.9 %collective-permute-start.2 = (bf16[64,11008]{1,0:T(8,128)(2,1)}, bf16[64,11008]{1,0:T(8,128)(2,1)}, u32[]{:S(2)}, u32[]{:S(2)}) collective-permute-start(bf16[64,11008]{1,0:T(8,128)(2,1)} %get-tuple-element.16), channel_id=1, source_target_pairs={{0,1},{1,0},{2,3},{3,2},{4,5},{5,4},{6,7},{7,6},{8,9},{9,8},{10,11... | collective-permute-start | bytes 4227080 | tf_op jit(solution)/shard_map/ppermute | solution.py:42
  30.0 13.7 %collective-permute-start.22 = (bf16[64,3328]{1,0:T(8,128)(2,1)S(1)}, bf16[64,3328]{1,0:T(8,128)(2,1)}, u32[]{:S(2)}, u32[]{:S(2)}) collective-permute-start(bf16[64,3328]{1,0:T(8,128)(2,1)S(1)} %add_convert_fusion.8), channel_id=1, source_target_pairs={{0,4},{1,13},{4,8},{5,1},{8,12},{9,5},{12,0},{13,9},{16,20},{17,29... | collective-permute-start | bytes 1277960 | tf_op jit(solution)/shard_map/ppermute | solution.py:42
  43.7 12.5 %collective-permute-start.1 = (bf16[64,11008]{1,0:T(8,128)(2,1)}, bf16[64,11008]{1,0:T(8,128)(2,1)}, u32[]{:S(2)}, u32[]{:S(2)}) collective-permute-start(bf16[64,11008]{1,0:T(8,128)(2,1)} %get-tuple-element.14), channel_id=1, source_target_pairs={{0,1},{1,0},{2,3},{3,2},{4,5},{5,4},{6,7},{7,6},{8,9},{9,8},{10,11... | collective-permute-start | bytes 4227080 | tf_op jit(solution)/shard_map/ppermute | solution.py:42
  45.9 10.3 %collective-permute-start.23 = (bf16[64,3328]{1,0:T(8,128)(2,1)}, bf16[64,3328]{1,0:T(8,128)(2,1)S(1)}, u32[]{:S(2)}, u32[]{:S(2)}) collective-permute-start(bf16[64,3328]{1,0:T(8,128)(2,1)} %add_convert_fusion.7), channel_id=1, source_target_pairs={{0,4},{1,13},{4,8},{5,1},{8,12},{9,5},{12,0},{13,9},{16,20},{17,29... | collective-permute-start | bytes 1277960 | tf_op jit(solution)/shard_map/ppermute | solution.py:42
  56.1 9.9 %collective-permute-start = (bf16[64,11008]{1,0:T(8,128)(2,1)}, bf16[64,11008]{1,0:T(8,128)(2,1)S(1)}, u32[]{:S(2)}, u32[]{:S(2)}) collective-permute-start(bf16[64,11008]{1,0:T(8,128)(2,1)} %get-tuple-element.12), channel_id=1, source_target_pairs={{0,1},{1,0},{2,3},{3,2},{4,5},{5,4},{6,7},{7,6},{8,9},{9,8},{10,11... | collective-permute-start | bytes 4227080 | tf_op jit(solution)/shard_map/ppermute | solution.py:42
  57.5 8.5 %collective-permute-start.24 = (bf16[64,3328]{1,0:T(8,128)(2,1)S(1)}, bf16[64,3328]{1,0:T(8,128)(2,1)S(1)}, u32[]{:S(2)}, u32[]{:S(2)}) collective-permute-start(bf16[64,3328]{1,0:T(8,128)(2,1)S(1)} %add_convert_fusion.6), channel_id=1, source_target_pairs={{0,4},{1,13},{4,8},{5,1},{8,12},{9,5},{12,0},{13,9},{16,20},{17,29... | collective-permute-start | bytes 1277960 | tf_op jit(solution)/shard_map/ppermute | solution.py:42
  63.3 8.5 %collective-permute-start.13 = (bf16[64,3840]{1,0:T(8,128)(2,1)S(1)}, bf16[64,3840]{1,0:T(8,128)(2,1)S(1)}, u32[]{:S(2)}, u32[]{:S(2)}) collective-permute-start(bf16[64,3840]{1,0:T(8,128)(2,1)S(1)} %get-tuple-element.29), channel_id=1, source_target_pairs={{0,16},{1,19},{4,20},{5,23},{8,24},{9,27},{12,28},{13,31},{16,2},{... | collective-permute-start | bytes 1474568 | tf_op jit(solution)/shard_map/ppermute | solution.py:42
  66.2 10.9 %collective-permute-start.25 = (bf16[16,3328]{1,0:T(8,128)(2,1)S(1)}, bf16[16,3328]{1,0:T(8,128)(2,1)S(1)}, u32[]{:S(2)}, u32[]{:S(2)}) collective-permute-start(bf16[16,3328]{1,0:T(8,128)(2,1)S(1)} %slice.305), channel_id=1, source_target_pairs={{0,32},{1,97},{4,36},{5,101},{8,40},{9,105},{12,44},{13,109},{16,4... | collective-permute-start | bytes 319496 | tf_op jit(solution)/shard_map/ppermute | solution.py:42
  74.0 8.9 %collective-permute-start.14 = (bf16[64,3840]{1,0:T(8,128)(2,1)S(1)}, bf16[64,3840]{1,0:T(8,128)(2,1)S(1)}, u32[]{:S(2)}, u32[]{:S(2)}) collective-permute-start(bf16[64,3840]{1,0:T(8,128)(2,1)S(1)} %get-tuple-element.27), channel_id=1, source_target_pairs={{0,16},{1,19},{4,20},{5,23},{8,24},{9,27},{12,28},{13,31},{16,2},{... | collective-permute-start | bytes 1474568 | tf_op jit(solution)/shard_map/ppermute | solution.py:42
  77.1 10.8 %collective-permute-start.26 = (bf16[16,3328]{1,0:T(8,128)(2,1)S(1)}, bf16[16,3328]{1,0:T(8,128)(2,1)S(1)}, u32[]{:S(2)}, u32[]{:S(2)}) collective-permute-start(bf16[16,3328]{1,0:T(8,128)(2,1)S(1)} %fusion.10), channel_id=1, source_target_pairs={{0,32},{1,97},{4,36},{5,101},{8,40},{9,105},{12,44},{13,109},{16,4... | collective-permute-start | bytes 319496 | tf_op jit(solution)/shard_map/ppermute | solution.py:42
  84.8 8.8 %collective-permute-start.15 = (bf16[64,3840]{1,0:T(8,128)(2,1)S(1)}, bf16[64,3840]{1,0:T(8,128)(2,1)S(1)}, u32[]{:S(2)}, u32[]{:S(2)}) collective-permute-start(bf16[64,3840]{1,0:T(8,128)(2,1)S(1)} %get-tuple-element.25), channel_id=1, source_target_pairs={{0,16},{1,19},{4,20},{5,23},{8,24},{9,27},{12,28},{13,31},{16,2},{... | collective-permute-start | bytes 1474568 | tf_op jit(solution)/shard_map/ppermute | solution.py:42
  87.9 9.9 %collective-permute-start.27 = (bf16[16,3328]{1,0:T(8,128)(2,1)S(1)}, bf16[16,3328]{1,0:T(8,128)(2,1)S(1)}, u32[]{:S(2)}, u32[]{:S(2)}) collective-permute-start(bf16[16,3328]{1,0:T(8,128)(2,1)S(1)} %fusion.11), channel_id=1, source_target_pairs={{0,32},{1,97},{4,36},{5,101},{8,40},{9,105},{12,44},{13,109},{16,4... | collective-permute-start | bytes 319496 | tf_op jit(solution)/shard_map/ppermute | solution.py:42
  94.4 9.0 %collective-permute-start.7 = (bf16[16,3840]{1,0:T(8,128)(2,1)S(1)}, bf16[16,3840]{1,0:T(8,128)(2,1)S(1)}, u32[]{:S(2)}, u32[]{:S(2)}) collective-permute-start(bf16[16,3840]{1,0:T(8,128)(2,1)S(1)} %slice.304), channel_id=1, source_target_pairs={{0,16},{1,19},{4,20},{5,23},{8,24},{9,27},{12,28},{13,31},{16,2},{... | collective-permute-start | bytes 368648 | tf_op jit(solution)/shard_map/ppermute | solution.py:42
  98.0 10.0 %collective-permute-start.17 = (bf16[16,3840]{1,0:T(8,128)(2,1)S(1)}, bf16[16,3840]{1,0:T(8,128)(2,1)S(1)}, u32[]{:S(2)}, u32[]{:S(2)}) collective-permute-start(bf16[16,3840]{1,0:T(8,128)(2,1)S(1)} %fusion.6), channel_id=1, source_target_pairs={{0,4},{1,13},{4,8},{5,1},{8,12},{9,5},{12,0},{13,9},{16,20},{17,29... | collective-permute-start | bytes 368648 | tf_op jit(solution)/shard_map/ppermute | solution.py:42
  137.6 10.0 %collective-permute-start.60 = (bf16[16,3328]{1,0:T(8,128)(2,1)S(1)}, bf16[16,3328]{1,0:T(8,128)(2,1)S(1)}, u32[]{:S(2)}, u32[]{:S(2)}) collective-permute-start(bf16[16,3328]{1,0:T(8,128)(2,1)S(1)} %pad_maximum_fusion.3), channel_id=1, source_target_pairs={{0,96},{1,33},{4,100},{5,37},{8,104},{9,41},{12,108},{13,45},{16,1... | collective-permute-start | bytes 319496 | tf_op jit(solution)/shard_map/ppermute | solution.py:42
  157.3 35.8 %collective-permute-start.64 = (bf16[64,3328]{1,0:T(8,128)(2,1)S(1)}, bf16[64,3328]{1,0:T(8,128)(2,1)S(1)}, u32[]{:S(2)}, u32[]{:S(2)}) collective-permute-start(bf16[64,3328]{1,0:T(8,128)(2,1)S(1)} %concatenate.34.refs_16_), channel_id=1, source_target_pairs={{0,12},{1,5},{4,0},{5,9},{8,4},{9,13},{12,8},{13,1},{16,28},{17,21... | collective-permute-start | bytes 1277960 | tf_op jit(solution)/shard_map/ppermute | solution.py:42
  158.3 8.8 %collective-permute-start.48 = (bf16[16,3840]{1,0:T(8,128)(2,1)S(1)}, bf16[16,3840]{1,0:T(8,128)(2,1)S(1)}, u32[]{:S(2)}, u32[]{:S(2)}) collective-permute-start(bf16[16,3840]{1,0:T(8,128)(2,1)S(1)} %collective-permute-done.47), channel_id=1, source_target_pairs={{0,12},{1,5},{4,0},{5,9},{8,4},{9,13},{12,8},{13,1},{16,28},{17,21... | collective-permute-start | bytes 368648 | tf_op jit(solution)/shard_map/ppermute | solution.py:42
  168.3 25.4 %collective-permute-start.38 = (bf16[64,3840]{1,0:T(8,128)(2,1)S(1)}, bf16[64,3840]{1,0:T(8,128)(2,1)S(1)}, u32[]{:S(2)}, u32[]{:S(2)}) collective-permute-start(bf16[64,3840]{1,0:T(8,128)(2,1)S(1)} %concatenate.30.refs_0_), channel_id=1, source_target_pairs={{0,96},{1,33},{4,100},{5,37},{8,104},{9,41},{12,108},{13,45},{16,1... | collective-permute-start | bytes 1474568 | tf_op jit(solution)/shard_map/ppermute | solution.py:42
  172.1 21.5 %collective-permute-start.51 = (bf16[64,3840]{1,0:T(8,128)(2,1)S(1)}, bf16[64,3840]{1,0:T(8,128)(2,1)S(1)}, u32[]{:S(2)}, u32[]{:S(2)}) collective-permute-start(bf16[64,3840]{1,0:T(8,128)(2,1)S(1)} %concatenate.32.refs_8_), channel_id=1, source_target_pairs={{0,18},{1,17},{4,22},{5,21},{8,26},{9,25},{12,30},{13,29},{16,0},{... | collective-permute-start | bytes 1474568 | tf_op jit(solution)/shard_map/ppermute | solution.py:42
  172.2 22.3 %collective-permute-start.63 = (bf16[64,3328]{1,0:T(8,128)(2,1)S(1)}, bf16[64,3328]{1,0:T(8,128)(2,1)S(1)}, u32[]{:S(2)}, u32[]{:S(2)}) collective-permute-start(bf16[64,3328]{1,0:T(8,128)(2,1)S(1)} %concatenate.34.refs_16_), channel_id=1, source_target_pairs={{0,1},{1,0},{2,3},{3,2},{4,5},{5,4},{6,7},{7,6},{8,9},{9,8},{10,11... | collective-permute-start | bytes 1277960 | tf_op jit(solution)/shard_map/ppermute | solution.py:42
  193.1 11.7 %collective-permute-start.50 = (bf16[64,3840]{1,0:T(8,128)(2,1)S(1)}, bf16[64,3840]{1,0:T(8,128)(2,1)S(1)}, u32[]{:S(2)}, u32[]{:S(2)}) collective-permute-start(bf16[64,3840]{1,0:T(8,128)(2,1)S(1)} %concatenate.32.refs_8_), channel_id=1, source_target_pairs={{0,1},{1,0},{2,3},{3,2},{4,5},{5,4},{6,7},{7,6},{8,9},{9,8},{10,11... | collective-permute-start | bytes 1474568 | tf_op jit(solution)/shard_map/ppermute | solution.py:42
  193.6 17.7 %collective-permute-start.40 = (bf16[64,3840]{1,0:T(8,128)(2,1)S(1)}, bf16[64,3840]{1,0:T(8,128)(2,1)}, u32[]{:S(2)}, u32[]{:S(2)}) collective-permute-start(bf16[64,3840]{1,0:T(8,128)(2,1)S(1)} %collective-permute-done.38.refs_2_), channel_id=1, source_target_pairs={{0,96},{1,33},{4,100},{5,37},{8,104},{9,41},{12,108},{13,45},{16,1... | collective-permute-start | bytes 1474568 | tf_op jit(solution)/shard_map/ppermute | solution.py:42
  193.6 17.6 %collective-permute-start.53 = (bf16[64,3840]{1,0:T(8,128)(2,1)S(1)}, bf16[64,3840]{1,0:T(8,128)(2,1)}, u32[]{:S(2)}, u32[]{:S(2)}) collective-permute-start(bf16[64,3840]{1,0:T(8,128)(2,1)S(1)} %collective-permute-done.51.refs_10_), channel_id=1, source_target_pairs={{0,18},{1,17},{4,22},{5,21},{8,26},{9,25},{12,30},{13,29},{16,0},{... | collective-permute-start | bytes 1474568 | tf_op jit(solution)/shard_map/ppermute | solution.py:42
  194.5 10.4 %collective-permute-start.66 = (bf16[64,3328]{1,0:T(8,128)(2,1)S(1)}, bf16[64,3328]{1,0:T(8,128)(2,1)S(1)}, u32[]{:S(2)}, u32[]{:S(2)}) collective-permute-start(bf16[64,3328]{1,0:T(8,128)(2,1)S(1)} %collective-permute-done.64.refs_18_), channel_id=1, source_target_pairs={{0,12},{1,5},{4,0},{5,9},{8,4},{9,13},{12,8},{13,1},{16,28},{17,21... | collective-permute-start | bytes 1277960 | tf_op jit(solution)/shard_map/ppermute | solution.py:42
  196.0 15.4 %collective-permute-start.65 = (bf16[64,3328]{1,0:T(8,128)(2,1)S(1)}, bf16[64,3328]{1,0:T(8,128)(2,1)S(1)}, u32[]{:S(2)}, u32[]{:S(2)}) collective-permute-start(bf16[64,3328]{1,0:T(8,128)(2,1)S(1)} %collective-permute-done.64.refs_18_), channel_id=1, source_target_pairs={{0,1},{1,0},{2,3},{3,2},{4,5},{5,4},{6,7},{7,6},{8,9},{9,8},{10,11... | collective-permute-start | bytes 1277960 | tf_op jit(solution)/shard_map/ppermute | solution.py:42
  204.8 8.8 %collective-permute-start.39 = (bf16[64,3840]{1,0:T(8,128)(2,1)S(1)}, bf16[64,3840]{1,0:T(8,128)(2,1)S(1)}, u32[]{:S(2)}, u32[]{:S(2)}) collective-permute-start(bf16[64,3840]{1,0:T(8,128)(2,1)S(1)} %collective-permute-done.38.refs_2_), channel_id=1, source_target_pairs={{0,1},{1,0},{2,3},{3,2},{4,5},{5,4},{6,7},{7,6},{8,9},{9,8},{10,11... | collective-permute-start | bytes 1474568 | tf_op jit(solution)/shard_map/ppermute | solution.py:42
  204.9 13.6 %collective-permute-start.52 = (bf16[64,3840]{1,0:T(8,128)(2,1)S(1)}, bf16[64,3840]{1,0:T(8,128)(2,1)S(1)}, u32[]{:S(2)}, u32[]{:S(2)}) collective-permute-start(bf16[64,3840]{1,0:T(8,128)(2,1)S(1)} %collective-permute-done.51.refs_10_), channel_id=1, source_target_pairs={{0,1},{1,0},{2,3},{3,2},{4,5},{5,4},{6,7},{7,6},{8,9},{9,8},{10,11... | collective-permute-start | bytes 1474568 | tf_op jit(solution)/shard_map/ppermute | solution.py:42
  211.3 12.1 %collective-permute-start.42 = (bf16[64,3840]{1,0:T(8,128)(2,1)}, bf16[64,3840]{1,0:T(8,128)(2,1)}, u32[]{:S(2)}, u32[]{:S(2)}) collective-permute-start(bf16[64,3840]{1,0:T(8,128)(2,1)} %collective-permute-done.40.refs_4_), channel_id=1, source_target_pairs={{0,96},{1,33},{4,100},{5,37},{8,104},{9,41},{12,108},{13,45},{16,1... | collective-permute-start | bytes 1474568 | tf_op jit(solution)/shard_map/ppermute | solution.py:42
  211.3 12.1 %collective-permute-start.55 = (bf16[64,3840]{1,0:T(8,128)(2,1)}, bf16[64,3840]{1,0:T(8,128)(2,1)}, u32[]{:S(2)}, u32[]{:S(2)}) collective-permute-start(bf16[64,3840]{1,0:T(8,128)(2,1)} %collective-permute-done.53.refs_12_), channel_id=1, source_target_pairs={{0,18},{1,17},{4,22},{5,21},{8,26},{9,25},{12,30},{13,29},{16,0},{... | collective-permute-start | bytes 1474568 | tf_op jit(solution)/shard_map/ppermute | solution.py:42
  212.1 8.8 %collective-permute-start.68 = (bf16[64,3328]{1,0:T(8,128)(2,1)S(1)}, bf16[64,3328]{1,0:T(8,128)(2,1)}, u32[]{:S(2)}, u32[]{:S(2)}) collective-permute-start(bf16[64,3328]{1,0:T(8,128)(2,1)S(1)} %collective-permute-done.66.refs_20_), channel_id=1, source_target_pairs={{0,12},{1,5},{4,0},{5,9},{8,4},{9,13},{12,8},{13,1},{16,28},{17,21... | collective-permute-start | bytes 1277960 | tf_op jit(solution)/shard_map/ppermute | solution.py:42
  213.6 10.3 %collective-permute-start.67 = (bf16[64,3328]{1,0:T(8,128)(2,1)S(1)}, bf16[64,3328]{1,0:T(8,128)(2,1)S(1)}, u32[]{:S(2)}, u32[]{:S(2)}) collective-permute-start(bf16[64,3328]{1,0:T(8,128)(2,1)S(1)} %collective-permute-done.66.refs_20_), channel_id=1, source_target_pairs={{0,1},{1,0},{2,3},{3,2},{4,5},{5,4},{6,7},{7,6},{8,9},{9,8},{10,11... | collective-permute-start | bytes 1277960 | tf_op jit(solution)/shard_map/ppermute | solution.py:42
  (54 other events, 354.3 us)

commit v2 on v0

v2 whole, which is shorter than its diff:
```python
import itertools

import jax
import jax.numpy as jnp
from jax import lax
from jax.experimental import pallas as pl
from jax.experimental.pallas import tpu as pltpu
from jax.sharding import PartitionSpec as P

STEP = 100

beta_first = 0.9
beta_second = 0.999
epsilon = 1e-08
galore_scale = 0.25

AXES = ("dp", "outer")
WIDTH = 1280
PIECES = ((0, 3840), (3840, 3840), (7680, 3328))
X, Y, Z = 0, 1, 2
BITS = (
    ((X, 0), (Z, 0), (Y, 0), (Z, 1)),
    ((Y, 0), (X, 0), (Z, 1), (Z, 0)),
    ((Z, 0), (Y, 0), (X, 0), (Z, 1)),
)
LAST = ((X, 1), (Y, 1))


def linear(x, y, z, core):
    return (((x * 2 + y % 2) * 4 + z) * 2 + y // 2) * 2 + core


def code(second, core):
    return 1 + 2 * ((second + core) % 2)


def exchange(*bits):
    pairs = []
    for x, y, z, core in itertools.product(range(4), range(4), range(4), range(2)):
        there = [x, y, z]
        for axis, second in bits:
            there[axis] ^= code(second, core)
        pairs.append((linear(x, y, z, core), linear(*there, core)))
    return pairs


SWAP = [(2 * i + core, 2 * i + 1 - core) for i in range(64) for core in range(2)]
QUAD = (exchange(LAST[1]), exchange(LAST[0]), exchange(*LAST))


def send(value, pairs):
    return lax.ppermute(value, AXES, pairs)


def send_pieces(values, level):
    values = lax.optimization_barrier(tuple(values))
    return lax.optimization_barrier(
        tuple(send(v, exchange(bits[level])) for v, bits in zip(values, BITS))
    )


def rank_order(bits, dp, outer):
    here = (dp // 8, (outer // 2) * 2 + (dp // 4) % 2, dp % 4)
    place = lax.iota(jnp.int32, 512)
    core = (outer + place // 256) % 2
    there = list(here)
    for level, (axis, second) in enumerate(bits + LAST):
        there[axis] = there[axis] ^ ((place // (128 >> level)) % 2 * code(second, core))
    return linear(*there, core) * 4 + place % 4


def expand_kernel(basis_ref, *refs):
    low = jnp.concatenate([ref[...] for ref in refs[:8]], axis=0)
    product = jnp.dot(basis_ref[...], low, preferred_element_type=jnp.float32)
    refs[-1][...] = -galore_scale * product


def expand(piece, basis_rows, blocks, width, *done):
    rows, (start, size) = basis_rows.shape[0], PIECES[piece]
    return pl.pallas_call(
        expand_kernel,
        grid=(pl.cdiv(size, WIDTH),),
        in_specs=[pl.BlockSpec((rows, 512), lambda j: (0, piece))]
        + [pl.BlockSpec((64, WIDTH), lambda j: (0, j))] * 8
        + [pl.BlockSpec(memory_space=pl.ANY)] * len(done),
        out_specs=pl.BlockSpec((rows, WIDTH), lambda j: (0, start // WIDTH + j)),
        out_shape=jax.ShapeDtypeStruct((rows, width), jnp.float32),
        input_output_aliases={9: 0} if done else {},
        cost_estimate=pl.CostEstimate(
            flops=2 * rows * 512 * size,
            bytes_accessed=(2 * 512 + 4 * rows) * size,
            transcendentals=0,
        ),
        compiler_params=pltpu.CompilerParams(vmem_limit_bytes=12 * 1024 * 1024),
        name="expand",
    )(basis_rows, *blocks, *done)


def shards(tokens, grad_out, projection_basis, first_moment, second_moment):
    dp, outer = lax.axis_index("dp"), lax.axis_index("outer")
    f32, bf16 = jnp.float32, jnp.bfloat16

    places = jnp.concatenate([rank_order(bits, dp, outer) for bits in BITS])
    picks = (lax.broadcasted_iota(jnp.int32, (512, 1536), 0) == places[None, :]).astype(bf16)

    projected = jnp.dot(tokens, projection_basis, preferred_element_type=f32).astype(bf16)
    projected = jnp.dot(projected, picks, preferred_element_type=f32).astype(bf16)
    local_width = projection_basis.shape[0] // 32
    basis_rows = lax.dynamic_slice_in_dim(projection_basis, dp * local_width, local_width, 0)
    basis_rows = jnp.dot(basis_rows, picks, preferred_element_type=f32).astype(bf16)

    own, other = [], []
    for piece, (start, size) in enumerate(PIECES):
        terms = lax.dot_general(
            projected[:, 512 * piece : 512 * piece + 512],
            grad_out[:, start : start + size],
            (((0,), (0,)), ((), ())),
            preferred_element_type=f32,
        ).astype(bf16)
        own.append(terms[:256])
        other.append(terms[256:])
    sent = [o[128:].astype(f32) + send(t[128:], SWAP).astype(f32) for o, t in zip(own, other)]
    held = [o[:128].astype(f32) + send(t[:128], SWAP).astype(f32) for o, t in zip(own, other)]
    for level in range(4):
        got = send_pieces([s.astype(bf16) for s in sent], level)
        held = [h + g.astype(f32) for h, g in zip(held, got)]
        half = held[0].shape[0] // 2
        if level < 3:
            sent, held = [h[half:] for h in held], [h[:half] for h in held]
    held = jnp.concatenate(held, axis=1)
    owned_grad = held[:4]
    for i, pairs in enumerate(QUAD):
        owned_grad = owned_grad + send(held[4 * i + 4 : 4 * i + 8], pairs)

    new_first = beta_first * first_moment + (1.0 - beta_first) * owned_grad
    new_second = beta_second * second_moment + (1.0 - beta_second) * owned_grad * owned_grad
    first_bias = 1.0 - beta_first**STEP
    second_bias = 1.0 - beta_second**STEP
    low_update = (new_first / first_bias / (jnp.sqrt(new_second / second_bias) + epsilon)).astype(bf16)

    low = jnp.concatenate([low_update] + [send(low_update, pairs) for pairs in QUAD], axis=0)
    low = [low[:, start : start + size] for start, size in PIECES]
    for level in (3, 2):
        got = send_pieces(low, level)
        low = [jnp.concatenate([mine, theirs], axis=0) for mine, theirs in zip(low, got)]
    blocks = [low, send_pieces(low, 1), send_pieces(low, 0)]
    blocks.append(send_pieces(blocks[1], 0))
    done = ()
    for piece in range(3):
        mine = [block[piece] for block in blocks]
        done = (expand(piece, basis_rows, mine + [send(m, SWAP) for m in mine], grad_out.shape[1], *done),)
    weight_update = done[0]
    return (weight_update, new_first, new_second)


def solution(mesh):
    in_specs = (
        P(("dp", "outer"), None),
        P(("dp", "outer"), None),
        P(),
        P(("dp", "outer"), None),
        P(("dp", "outer"), None),
    )
    out_specs = (P("dp", None), P(("dp", "outer"), None), P(("dp", "outer"), None))
    return jax.shard_map(shards, mesh=mesh, in_specs=in_specs, out_specs=out_specs, check_vma=False)
```

time: 497 us -> 164 us (0.33)
  waiting for transfers between devices: 436 us -> 52.1 us
  starting transfers between devices: 0.08 us -> 68 us
  between operations: 14.1 us -> 1.15 us
  Pallas kernels: 0 us -> 10.9 us
  local copies, waits for them, and re-layouts: 19.1 us -> 10.2 us
  matrix products: 25.2 us -> 17 us
    unnamed x3 -> x0, waiting for transfers between devices: 230 us -> none
    all_gather x1 -> x0, waiting for transfers between devices: 206 us -> none  [shards(): lax.all_gather(low_update, ('dp', 'outer'), axis=0, tiled=True)]
    ppermute x0 -> x51, starting transfers between devices: none -> 68 us  [send(): return lax.ppermute(value, AXES, pairs)]
    ppermute x0 -> x51, waiting for transfers between devices: none -> 52.1 us  [send(): return lax.ppermute(value, AXES, pairs)]
    pallas_call x0 -> x3, Pallas kernels: none -> 10.9 us  [expand(): pl.pallas_call(expand_kernel, grid=(pl.cdiv(size, WIDTH),), in_specs=[pl....]
    unnamed x7 -> x38, local copies, waits for them, and re-layouts: 19.1 us -> 9.46 us
    dot_general x3 -> x5, matrix products: 25.2 us -> 17 us  [the longest x3 8.76 us: shards(): lax.dot_general(projected[:, 512 * piece:512 * piece + 512], grad_out[:,...]
  transfers between devices with their start and end apart: 2 -> 51, of which waited for: 2 -> 19; matrix products, arithmetic and copies ran while one was open for 0% -> 5% of each run, Pallas kernels for 0% -> 4%
where the time goes in v2:
time: 164 us; the launch traced here: 163 us
  starting transfers between devices  68 us (41%)
  waiting for transfers between devices  52.1 us (32%)
  matrix products  17 us (10%)
  Pallas kernels  10.9 us (7%)
  local copies, waits for them, and re-layouts  10.2 us (6%)
  other arithmetic  3.76 us (2%)
    ppermute x51, starting transfers between devices, send(): return lax.ppermute(value, AXES, pairs)  68 us
    ppermute x51, waiting for transfers between devices, send(): return lax.ppermute(value, AXES, pairs)  52.1 us
    pallas_call x3, Pallas kernels, expand(): pl.pallas_call(expand_kernel, grid=(pl.cdiv(size, WIDTH),), in_specs=[pl....  10.9 us
    unnamed x38, local copies, waits for them, and re-layouts  9.46 us
    dot_general x3, matrix products, shards(): lax.dot_general(projected[:, 512 * piece:512 * piece + 512], grad_out[:,...  8.76 us
    dot_general x1, matrix products, shards(): jnp.dot(projected, picks, preferred_element_type=f32).astype(bf16)  6.63 us
  transfers between devices with their start and end apart: 51, of which 19 were waited for; matrix products, arithmetic and copies ran while one was open for 5% of the time, Pallas kernels for 4%

profile of v2, /device:TPU:1, one launch (start us, length us, event | category | flops | bytes accessed | tf_op | source)
XLA Modules:
  0.0 163.2 jit_solution(16319838271952789039)
XLA Ops:
  0.8 6.6 %fusion.5 = bf16[512,1536]{1,0:T(8,128)(2,1)S(1)} fusion(s32[1536]{0:T(1024)S(1)} %pad_add_fusion, bf16[512,4096]{1,0:T(8,128)(2,1)} %param.5, bf16[4096,512]{1,0:T(8,128)(2,1)} %param.7), kind=kOutput, calls=%fused_computation.9 | convolution fusion | flops 2954625024 | bytes 9967616 | tf_op jit(solution)/shard_map/dot_general | solution.py:107
  7.4 4.5 %convolution_convert_fusion.1 = bf16[512,3840]{1,0:T(8,128)(2,1)S(1)} fusion(bf16[512,11008]{1,0:T(8,128)(2,1)} %param.6, bf16[512,1536]{1,0:T(8,128)(2,1)S(1)} %fusion.5), kind=kOutput, calls=%fused_computation.1 | convolution fusion | flops 2015232000 | bytes 8388608 | tf_op jit(solution)/shard_map/dot_general | solution.py:114
  13.6 2.0 %convolution_convert_fusion = bf16[512,3328]{1,0:T(8,128)(2,1)S(1)} fusion(bf16[512,11008]{1,0:T(8,128)(2,1)S(1)} %copy-done.16, bf16[512,1536]{1,0:T(8,128)(2,1)S(1)} %fusion.5), kind=kOutput, calls=%fused_computation | convolution fusion | flops 1746534400 | bytes 7340032 | tf_op jit(solution)/shard_map/dot_general | solution.py:114
  16.4 2.3 %convolution_convert_fusion.2 = bf16[512,3840]{1,0:T(8,128)(2,1)S(1)} fusion(bf16[512,11008]{1,0:T(8,128)(2,1)S(1)} %copy-done.16, bf16[512,1536]{1,0:T(8,128)(2,1)S(1)} %fusion.5), kind=kOutput, calls=%fused_computation.2 | convolution fusion | flops 2015232000 | bytes 8388608 | tf_op jit(solution)/shard_map/dot_general | solution.py:114
  19.4 2.1 %collective-permute-done.1 = bf16[128,3840]{1,0:T(8,128)(2,1)S(1)} collective-permute-done((bf16[128,3840]{1,0:T(8,128)(2,1)S(1)}, bf16[128,3840]{1,0:T(8,128)(2,1)S(1)}, u32[]{:S(2)}, u32[]{:S(2)}) %collective-permute-start.1) | collective-permute-done | bytes 983072 | tf_op jit(solution)/shard_map/ppermute | solution.py:52
  21.7 2.6 %collective-permute-start.4 = (bf16[128,3840]{1,0:T(8,128)(2,1)S(1)}, bf16[128,3840]{1,0:T(8,128)(2,1)S(1)}, u32[]{:S(2)}, u32[]{:S(2)}) collective-permute-start(bf16[128,3840]{1,0:T(8,128)(2,1)S(1)} %add_convert_fusion.1), channel_id=1, source_target_pairs={{0,32},{1,97},{4,36},{5,101},{8,40},{9,105},{12,44},{13,109},{16,4... | collective-permute-start | bytes 2949128 | tf_op jit(solution)/shard_map/ppermute | solution.py:52
  24.4 2.7 %collective-permute-start.5 = (bf16[128,3840]{1,0:T(8,128)(2,1)S(1)}, bf16[128,3840]{1,0:T(8,128)(2,1)S(1)}, u32[]{:S(2)}, u32[]{:S(2)}) collective-permute-start(bf16[128,3840]{1,0:T(8,128)(2,1)S(1)} %add_convert_fusion), channel_id=1, source_target_pairs={{0,16},{1,19},{4,20},{5,23},{8,24},{9,27},{12,28},{13,31},{16,0},{... | collective-permute-start | bytes 2949128 | tf_op jit(solution)/shard_map/ppermute | solution.py:52
  27.1 3.8 %collective-permute-start.6 = (bf16[128,3328]{1,0:T(8,128)(2,1)S(1)}, bf16[128,3328]{1,0:T(8,128)(2,1)S(1)}, u32[]{:S(2)}, u32[]{:S(2)}) collective-permute-start(bf16[128,3328]{1,0:T(8,128)(2,1)S(1)} %add_convert_fusion.2), channel_id=1, source_target_pairs={{0,4},{1,13},{4,0},{5,9},{8,12},{9,5},{12,8},{13,1},{16,20},{17,29... | collective-permute-start | bytes 2555912 | tf_op jit(solution)/shard_map/ppermute | solution.py:52
  30.9 10.1 %collective-permute-done.6 = bf16[128,3328]{1,0:T(8,128)(2,1)S(1)} collective-permute-done((bf16[128,3328]{1,0:T(8,128)(2,1)S(1)}, bf16[128,3328]{1,0:T(8,128)(2,1)S(1)}, u32[]{:S(2)}, u32[]{:S(2)}) %collective-permute-start.6) | collective-permute-done | bytes 852000 | tf_op jit(solution)/shard_map/ppermute | solution.py:52
  43.9 2.7 %collective-permute-start.9 = (bf16[64,3840]{1,0:T(8,128)(2,1)S(1)}, bf16[64,3840]{1,0:T(8,128)(2,1)S(1)}, u32[]{:S(2)}, u32[]{:S(2)}) collective-permute-start(bf16[64,3840]{1,0:T(8,128)(2,1)S(1)} %slice.278), channel_id=1, source_target_pairs={{0,4},{1,13},{4,0},{5,9},{8,12},{9,5},{12,8},{13,1},{16,20},{17,29... | collective-permute-start | bytes 1474568 | tf_op jit(solution)/shard_map/ppermute | solution.py:52
  48.1 6.8 %collective-permute-done.11 = bf16[64,3328]{1,0:T(8,128)(2,1)S(1)} collective-permute-done((bf16[64,3328]{1,0:T(8,128)(2,1)S(1)}, bf16[64,3328]{1,0:T(8,128)(2,1)S(1)}, u32[]{:S(2)}, u32[]{:S(2)}) %collective-permute-start.11) | collective-permute-done | bytes 426016 | tf_op jit(solution)/shard_map/ppermute | solution.py:52
  58.0 4.7 %collective-permute-done.14 = bf16[32,3328]{1,0:T(8,128)(2,1)S(1)} collective-permute-done((bf16[32,3328]{1,0:T(8,128)(2,1)S(1)}, bf16[32,3328]{1,0:T(8,128)(2,1)S(1)}, u32[]{:S(2)}, u32[]{:S(2)}) %collective-permute-start.14) | collective-permute-done | bytes 213024 | tf_op jit(solution)/shard_map/ppermute | solution.py:52
  65.2 5.0 %collective-permute-done.17 = bf16[16,3328]{1,0:T(8,128)(2,1)S(1)} collective-permute-done((bf16[16,3328]{1,0:T(8,128)(2,1)S(1)}, bf16[16,3328]{1,0:T(8,128)(2,1)S(1)}, u32[]{:S(2)}, u32[]{:S(2)}) %collective-permute-start.17) | collective-permute-done | bytes 106528 | tf_op jit(solution)/shard_map/ppermute | solution.py:52
  71.5 2.5 %collective-permute-start.20 = (f32[4,11008]{1,0:T(4,128)S(1)}, f32[4,11008]{1,0:T(4,128)S(1)}, u32[]{:S(2)}, u32[]{:S(2)}) collective-permute-start(f32[4,11008]{1,0:T(4,128)S(1)} %get-tuple-element.115), channel_id=1, source_target_pairs={{0,114},{1,49},{4,118},{5,53},{8,122},{9,57},{12,126},{13,61},{16,... | collective-permute-start | bytes 528392 | tf_op jit(solution)/shard_map/ppermute | solution.py:52
  74.0 1.7 %collective-permute-done.18 = f32[4,11008]{1,0:T(4,128)S(1)} collective-permute-done((f32[4,11008]{1,0:T(4,128)S(1)}, f32[4,11008]{1,0:T(4,128)S(1)}, u32[]{:S(2)}, u32[]{:S(2)}) %collective-permute-start.18) | collective-permute-done | bytes 176160 | tf_op jit(solution)/shard_map/ppermute | solution.py:52
  75.8 3.3 %collective-permute-done.20 = f32[4,11008]{1,0:T(4,128)S(1)} collective-permute-done((f32[4,11008]{1,0:T(4,128)S(1)}, f32[4,11008]{1,0:T(4,128)S(1)}, u32[]{:S(2)}, u32[]{:S(2)}) %collective-permute-start.20) | collective-permute-done | bytes 176160 | tf_op jit(solution)/shard_map/ppermute | solution.py:52
  80.5 2.2 %collective-permute-start.23 = (bf16[4,11008]{1,0:T(4,128)(2,1)S(1)}, bf16[4,11008]{1,0:T(4,128)(2,1)S(1)}, u32[]{:S(2)}, u32[]{:S(2)}) collective-permute-start(bf16[4,11008]{1,0:T(4,128)(2,1)S(1)} %get-tuple-element.105), channel_id=1, source_target_pairs={{0,114},{1,49},{4,118},{5,53},{8,122},{9,57},{12,126},{13,61},{16,... | collective-permute-start | bytes 264200 | tf_op jit(solution)/shard_map/ppermute | solution.py:52
  83.7 1.8 %collective-permute-done.23 = bf16[4,11008]{1,0:T(4,128)(2,1)S(1)} collective-permute-done((bf16[4,11008]{1,0:T(4,128)(2,1)S(1)}, bf16[4,11008]{1,0:T(4,128)(2,1)S(1)}, u32[]{:S(2)}, u32[]{:S(2)}) %collective-permute-start.23) | collective-permute-done | bytes 88096 | tf_op jit(solution)/shard_map/ppermute | solution.py:52
  87.3 3.7 %collective-permute-done.26 = bf16[16,3328]{1,0:T(8,128)(2,1)S(1)} collective-permute-done((bf16[16,3328]{1,0:T(8,128)(2,1)S(1)}, bf16[16,3328]{1,0:T(8,128)(2,1)S(1)}, u32[]{:S(2)}, u32[]{:S(2)}) %collective-permute-start.26) | collective-permute-done | bytes 106528 | tf_op jit(solution)/shard_map/ppermute | solution.py:52
  92.3 2.3 %collective-permute-start.29 = (bf16[32,3328]{1,0:T(8,128)(2,1)S(1)}, bf16[32,3328]{1,0:T(8,128)(2,1)S(1)}, u32[]{:S(2)}, u32[]{:S(2)}) collective-permute-start(bf16[32,3328]{1,0:T(8,128)(2,1)S(1)} %pad_maximum_fusion.6), channel_id=1, source_target_pairs={{0,32},{1,97},{4,36},{5,101},{8,40},{9,105},{12,44},{13,109},{16,4... | collective-permute-start | bytes 638984 | tf_op jit(solution)/shard_map/ppermute | solution.py:52
  94.6 3.6 %collective-permute-done.29 = bf16[32,3328]{1,0:T(8,128)(2,1)S(1)} collective-permute-done((bf16[32,3328]{1,0:T(8,128)(2,1)S(1)}, bf16[32,3328]{1,0:T(8,128)(2,1)S(1)}, u32[]{:S(2)}, u32[]{:S(2)}) %collective-permute-start.29) | collective-permute-done | bytes 213024 | tf_op jit(solution)/shard_map/ppermute | solution.py:52
  98.3 1.8 %collective-permute-start.32 = (bf16[64,3328]{1,0:T(8,128)(2,1)S(1)}, bf16[64,3328]{1,0:T(8,128)(2,1)}, u32[]{:S(2)}, u32[]{:S(2)}) collective-permute-start(bf16[64,3328]{1,0:T(8,128)(2,1)S(1)} %pad_maximum_fusion.3.refs_0_), channel_id=1, source_target_pairs={{0,16},{1,19},{4,20},{5,23},{8,24},{9,27},{12,28},{13,31},{16,0},{... | collective-permute-start | bytes 1277960 | tf_op jit(solution)/shard_map/ppermute | solution.py:52
  100.1 1.8 %collective-permute-start.30 = (bf16[64,3840]{1,0:T(8,128)(2,1)S(1)}, bf16[64,3840]{1,0:T(8,128)(2,1)S(1)}, u32[]{:S(2)}, u32[]{:S(2)}) collective-permute-start(bf16[64,3840]{1,0:T(8,128)(2,1)S(1)} %pad_maximum_fusion.1.refs_0_), channel_id=1, source_target_pairs={{0,4},{1,13},{4,0},{5,9},{8,12},{9,5},{12,8},{13,1},{16,20},{17,29... | collective-permute-start | bytes 1474568 | tf_op jit(solution)/shard_map/ppermute | solution.py:52
  102.9 1.7 %collective-permute-start.33 = (bf16[64,3840]{1,0:T(8,128)(2,1)S(1)}, bf16[64,3840]{1,0:T(8,128)(2,1)S(1)}, u32[]{:S(2)}, u32[]{:S(2)}) collective-permute-start(bf16[64,3840]{1,0:T(8,128)(2,1)S(1)} %pad_maximum_fusion.1.refs_0_), channel_id=1, source_target_pairs={{0,32},{1,97},{4,36},{5,101},{8,40},{9,105},{12,44},{13,109},{16,4... | collective-permute-start | bytes 1474568 | tf_op jit(solution)/shard_map/ppermute | solution.py:52
  106.7 2.1 %collective-permute-start.35 = (bf16[64,3328]{1,0:T(8,128)(2,1)S(1)}, bf16[64,3328]{1,0:T(8,128)(2,1)}, u32[]{:S(2)}, u32[]{:S(2)}) collective-permute-start(bf16[64,3328]{1,0:T(8,128)(2,1)S(1)} %pad_maximum_fusion.3.refs_0_), channel_id=1, source_target_pairs={{0,4},{1,13},{4,0},{5,9},{8,12},{9,5},{12,8},{13,1},{16,20},{17,29... | collective-permute-start | bytes 1277960 | tf_op jit(solution)/shard_map/ppermute | solution.py:52
  113.5 2.8 %collective-permute-done.35.refs_2_ = bf16[64,3328]{1,0:T(8,128)(2,1)} collective-permute-done((bf16[64,3328]{1,0:T(8,128)(2,1)S(1)}, bf16[64,3328]{1,0:T(8,128)(2,1)}, u32[]{:S(2)}, u32[]{:S(2)}) %collective-permute-start.35) | collective-permute-done | bytes 426016 | tf_op jit(solution)/shard_map/ppermute | solution.py:52
  117.3 15.3 %collective-permute-start.47 = (bf16[64,3840]{1,0:T(8,128)(2,1)S(1)}, bf16[64,3840]{1,0:T(8,128)(2,1)S(1)}, u32[]{:S(2)}, u32[]{:S(2)}) collective-permute-start(bf16[64,3840]{1,0:T(8,128)(2,1)S(1)} %pad_maximum_fusion.1.refs_0_), channel_id=1, source_target_pairs={{0,1},{1,0},{2,3},{3,2},{4,5},{5,4},{6,7},{7,6},{8,9},{9,8},{10,11... | collective-permute-start | bytes 1474568 | tf_op jit(solution)/shard_map/ppermute | solution.py:52
  132.7 2.4 %collective-permute-start.49 = (bf16[64,3840]{1,0:T(8,128)(2,1)S(1)}, bf16[64,3840]{1,0:T(8,128)(2,1)S(1)}, u32[]{:S(2)}, u32[]{:S(2)}) collective-permute-start(bf16[64,3840]{1,0:T(8,128)(2,1)S(1)} %collective-permute-done.33.refs_2_), channel_id=1, source_target_pairs={{0,1},{1,0},{2,3},{3,2},{4,5},{5,4},{6,7},{7,6},{8,9},{9,8},{10,11... | collective-permute-start | bytes 1474568 | tf_op jit(solution)/shard_map/ppermute | solution.py:52
  135.8 3.7 %collective-permute-start.45 = (bf16[64,3840]{1,0:T(8,128)(2,1)S(1)}, bf16[64,3840]{1,0:T(8,128)(2,1)S(1)}, u32[]{:S(2)}, u32[]{:S(2)}) collective-permute-start(bf16[64,3840]{1,0:T(8,128)(2,1)S(1)} %collective-permute-done.34.refs_2_), channel_id=1, source_target_pairs={{0,1},{1,0},{2,3},{3,2},{4,5},{5,4},{6,7},{7,6},{8,9},{9,8},{10,11... | collective-permute-start | bytes 1474568 | tf_op jit(solution)/shard_map/ppermute | solution.py:52
  152.2 2.6 %expand.3.refs_8_ = f32[128,11008]{1,0:T(8,128)} custom-call(bf16[128,1536]{1,0:T(8,128)(2,1)S(1)} %fusion.6.basis_ref, bf16[64,3840]{1,0:T(8,128)(2,1)S(1)} %pad_maximum_fusion.1.refs_0_, bf16[64,3840]{1,0:T(8,128)(2,1)S(1)} %collective-permute-done.30.refs_1_, bf16[64,3840]{1,0:T(8,128)(2,1)S(1)} %collective-permute-done.33.refs_2_, ...), custom_call_target="tpu_custom_call" | custom-call | flops 503316480 | bytes 5898240 | tf_op jit(solution)/shard_map/expand/pallas_call | solution.py:80
  154.9 3.9 %expand.4.refs_8_ = f32[128,11008]{1,0:T(8,128)} custom-call(bf16[128,1536]{1,0:T(8,128)(2,1)S(1)} %fusion.6.basis_ref, bf16[64,3840]{1,0:T(8,128)(2,1)S(1)} %pad_maximum_fusion.2.refs_0_, bf16[64,3840]{1,0:T(8,128)(2,1)S(1)} %copy-done.7, bf16[64,3840]{1,0:T(8,128)(2,1)S(1)} %copy-done.9, ...), custom_call_target="tpu_custom_call", output_to_operand_aliasing={{}: (9, {})} | custom-call | flops 503316480 | bytes 5898240 | tf_op jit(solution)/shard_map/expand/pallas_call | solution.py:80
  158.8 4.5 %expand.5 = f32[128,11008]{1,0:T(8,128)} custom-call(bf16[128,1536]{1,0:T(8,128)(2,1)S(1)} %fusion.6.basis_ref, bf16[64,3328]{1,0:T(8,128)(2,1)S(1)} %pad_maximum_fusion.3.refs_0_, bf16[64,3328]{1,0:T(8,128)(2,1)} %collective-permute-done.32.refs_1_, bf16[64,3328]{1,0:T(8,128)(2,1)} %collective-permute-done.35.refs_2_, ...), custom_call_target="tpu_custom_call", output_to_operand_aliasing={{}: (9, {})} | custom-call | flops 436207616 | bytes 5111808 | tf_op jit(solution)/shard_map/expand/pallas_call | solution.py:80
  (157 shorter events, 42.5 us)
Async XLA Ops:
  12.1 7.1 %collective-permute-start.2 = (bf16[128,3840]{1,0:T(8,128)(2,1)S(1)}, bf16[128,3840]{1,0:T(8,128)(2,1)S(1)}, u32[]{:S(2)}, u32[]{:S(2)}) collective-permute-start(bf16[128,3840]{1,0:T(8,128)(2,1)S(1)} %get-tuple-element.109), channel_id=1, source_target_pairs={{0,1},{1,0},{2,3},{3,2},{4,5},{5,4},{6,7},{7,6},{8,9},{9,8},{10,11... | collective-permute-start | bytes 2949128 | tf_op jit(solution)/shard_map/ppermute | solution.py:52
  21.7 19.2 %collective-permute-start.4 = (bf16[128,3840]{1,0:T(8,128)(2,1)S(1)}, bf16[128,3840]{1,0:T(8,128)(2,1)S(1)}, u32[]{:S(2)}, u32[]{:S(2)}) collective-permute-start(bf16[128,3840]{1,0:T(8,128)(2,1)S(1)} %add_convert_fusion.1), channel_id=1, source_target_pairs={{0,32},{1,97},{4,36},{5,101},{8,40},{9,105},{12,44},{13,109},{16,4... | collective-permute-start | bytes 2949128 | tf_op jit(solution)/shard_map/ppermute | solution.py:52
  24.4 16.6 %collective-permute-start.5 = (bf16[128,3840]{1,0:T(8,128)(2,1)S(1)}, bf16[128,3840]{1,0:T(8,128)(2,1)S(1)}, u32[]{:S(2)}, u32[]{:S(2)}) collective-permute-start(bf16[128,3840]{1,0:T(8,128)(2,1)S(1)} %add_convert_fusion), channel_id=1, source_target_pairs={{0,16},{1,19},{4,20},{5,23},{8,24},{9,27},{12,28},{13,31},{16,0},{... | collective-permute-start | bytes 2949128 | tf_op jit(solution)/shard_map/ppermute | solution.py:52
  27.1 13.9 %collective-permute-start.7 = (bf16[128,3840]{1,0:T(8,128)(2,1)S(1)}, bf16[128,3840]{1,0:T(8,128)(2,1)S(1)}, u32[]{:S(2)}, u32[]{:S(2)}) collective-permute-start(bf16[128,3840]{1,0:T(8,128)(2,1)S(1)} %get-tuple-element.108), channel_id=1, source_target_pairs={{0,1},{1,0},{2,3},{3,2},{4,5},{5,4},{6,7},{7,6},{8,9},{9,8},{10,11... | collective-permute-start | bytes 2949128 | tf_op jit(solution)/shard_map/ppermute | solution.py:52
  27.1 13.8 %collective-permute-start.6 = (bf16[128,3328]{1,0:T(8,128)(2,1)S(1)}, bf16[128,3328]{1,0:T(8,128)(2,1)S(1)}, u32[]{:S(2)}, u32[]{:S(2)}) collective-permute-start(bf16[128,3328]{1,0:T(8,128)(2,1)S(1)} %add_convert_fusion.2), channel_id=1, source_target_pairs={{0,4},{1,13},{4,0},{5,9},{8,12},{9,5},{12,8},{13,1},{16,20},{17,29... | collective-permute-start | bytes 2555912 | tf_op jit(solution)/shard_map/ppermute | solution.py:52
  30.9 10.6 %collective-permute-start = (bf16[128,3840]{1,0:T(8,128)(2,1)S(1)}, bf16[128,3840]{1,0:T(8,128)(2,1)S(1)}, u32[]{:S(2)}, u32[]{:S(2)}) collective-permute-start(bf16[128,3840]{1,0:T(8,128)(2,1)S(1)} %get-tuple-element.110), channel_id=1, source_target_pairs={{0,1},{1,0},{2,3},{3,2},{4,5},{5,4},{6,7},{7,6},{8,9},{9,8},{10,11... | collective-permute-start | bytes 2949128 | tf_op jit(solution)/shard_map/ppermute | solution.py:52
  43.6 11.2 %collective-permute-start.10 = (bf16[64,3840]{1,0:T(8,128)(2,1)S(1)}, bf16[64,3840]{1,0:T(8,128)(2,1)S(1)}, u32[]{:S(2)}, u32[]{:S(2)}) collective-permute-start(bf16[64,3840]{1,0:T(8,128)(2,1)S(1)} %slice.277), channel_id=1, source_target_pairs={{0,32},{1,97},{4,36},{5,101},{8,40},{9,105},{12,44},{13,109},{16,4... | collective-permute-start | bytes 1474568 | tf_op jit(solution)/shard_map/ppermute | solution.py:52
  43.9 10.9 %collective-permute-start.9 = (bf16[64,3840]{1,0:T(8,128)(2,1)S(1)}, bf16[64,3840]{1,0:T(8,128)(2,1)S(1)}, u32[]{:S(2)}, u32[]{:S(2)}) collective-permute-start(bf16[64,3840]{1,0:T(8,128)(2,1)S(1)} %slice.278), channel_id=1, source_target_pairs={{0,4},{1,13},{4,0},{5,9},{8,12},{9,5},{12,8},{13,1},{16,20},{17,29... | collective-permute-start | bytes 1474568 | tf_op jit(solution)/shard_map/ppermute | solution.py:52
  46.7 8.2 %collective-permute-start.11 = (bf16[64,3328]{1,0:T(8,128)(2,1)S(1)}, bf16[64,3328]{1,0:T(8,128)(2,1)S(1)}, u32[]{:S(2)}, u32[]{:S(2)}) collective-permute-start(bf16[64,3328]{1,0:T(8,128)(2,1)S(1)} %slice.279), channel_id=1, source_target_pairs={{0,16},{1,19},{4,20},{5,23},{8,24},{9,27},{12,28},{13,31},{16,0},{... | collective-permute-start | bytes 1277960 | tf_op jit(solution)/shard_map/ppermute | solution.py:52
  55.3 7.4 %collective-permute-start.12 = (bf16[32,3840]{1,0:T(8,128)(2,1)S(1)}, bf16[32,3840]{1,0:T(8,128)(2,1)S(1)}, u32[]{:S(2)}, u32[]{:S(2)}) collective-permute-start(bf16[32,3840]{1,0:T(8,128)(2,1)S(1)} %slice.281), channel_id=1, source_target_pairs={{0,16},{1,19},{4,20},{5,23},{8,24},{9,27},{12,28},{13,31},{16,0},{... | collective-permute-start | bytes 737288 | tf_op jit(solution)/shard_map/ppermute | solution.py:52
  62.9 7.2 %collective-permute-start.15 = (bf16[16,3840]{1,0:T(8,128)(2,1)S(1)}, bf16[16,3840]{1,0:T(8,128)(2,1)S(1)}, u32[]{:S(2)}, u32[]{:S(2)}) collective-permute-start(bf16[16,3840]{1,0:T(8,128)(2,1)S(1)} %slice.284), channel_id=1, source_target_pairs={{0,12},{1,5},{4,8},{5,1},{8,4},{9,13},{12,0},{13,9},{16,28},{17,21... | collective-permute-start | bytes 368648 | tf_op jit(solution)/shard_map/ppermute | solution.py:52
  71.5 7.6 %collective-permute-start.20 = (f32[4,11008]{1,0:T(4,128)S(1)}, f32[4,11008]{1,0:T(4,128)S(1)}, u32[]{:S(2)}, u32[]{:S(2)}) collective-permute-start(f32[4,11008]{1,0:T(4,128)S(1)} %get-tuple-element.115), channel_id=1, source_target_pairs={{0,114},{1,49},{4,118},{5,53},{8,122},{9,57},{12,126},{13,61},{16,... | collective-permute-start | bytes 528392 | tf_op jit(solution)/shard_map/ppermute | solution.py:52
  91.2 7.0 %collective-permute-start.27 = (bf16[32,3840]{1,0:T(8,128)(2,1)S(1)}, bf16[32,3840]{1,0:T(8,128)(2,1)S(1)}, u32[]{:S(2)}, u32[]{:S(2)}) collective-permute-start(bf16[32,3840]{1,0:T(8,128)(2,1)S(1)} %pad_maximum_fusion.4), channel_id=1, source_target_pairs={{0,16},{1,19},{4,20},{5,23},{8,24},{9,27},{12,28},{13,31},{16,0},{... | collective-permute-start | bytes 737288 | tf_op jit(solution)/shard_map/ppermute | solution.py:52
  98.3 8.4 %collective-permute-start.32 = (bf16[64,3328]{1,0:T(8,128)(2,1)S(1)}, bf16[64,3328]{1,0:T(8,128)(2,1)}, u32[]{:S(2)}, u32[]{:S(2)}) collective-permute-start(bf16[64,3328]{1,0:T(8,128)(2,1)S(1)} %pad_maximum_fusion.3.refs_0_), channel_id=1, source_target_pairs={{0,16},{1,19},{4,20},{5,23},{8,24},{9,27},{12,28},{13,31},{16,0},{... | collective-permute-start | bytes 1277960 | tf_op jit(solution)/shard_map/ppermute | solution.py:52
  100.1 10.0 %collective-permute-start.30 = (bf16[64,3840]{1,0:T(8,128)(2,1)S(1)}, bf16[64,3840]{1,0:T(8,128)(2,1)S(1)}, u32[]{:S(2)}, u32[]{:S(2)}) collective-permute-start(bf16[64,3840]{1,0:T(8,128)(2,1)S(1)} %pad_maximum_fusion.1.refs_0_), channel_id=1, source_target_pairs={{0,4},{1,13},{4,0},{5,9},{8,12},{9,5},{12,8},{13,1},{16,20},{17,29... | collective-permute-start | bytes 1474568 | tf_op jit(solution)/shard_map/ppermute | solution.py:52
  101.9 9.2 %collective-permute-start.31 = (bf16[64,3840]{1,0:T(8,128)(2,1)S(1)}, bf16[64,3840]{1,0:T(8,128)(2,1)S(1)}, u32[]{:S(2)}, u32[]{:S(2)}) collective-permute-start(bf16[64,3840]{1,0:T(8,128)(2,1)S(1)} %pad_maximum_fusion.2.refs_0_), channel_id=1, source_target_pairs={{0,32},{1,97},{4,36},{5,101},{8,40},{9,105},{12,44},{13,109},{16,4... | collective-permute-start | bytes 1474568 | tf_op jit(solution)/shard_map/ppermute | solution.py:52
  102.9 14.4 %collective-permute-start.33 = (bf16[64,3840]{1,0:T(8,128)(2,1)S(1)}, bf16[64,3840]{1,0:T(8,128)(2,1)S(1)}, u32[]{:S(2)}, u32[]{:S(2)}) collective-permute-start(bf16[64,3840]{1,0:T(8,128)(2,1)S(1)} %pad_maximum_fusion.1.refs_0_), channel_id=1, source_target_pairs={{0,32},{1,97},{4,36},{5,101},{8,40},{9,105},{12,44},{13,109},{16,4... | collective-permute-start | bytes 1474568 | tf_op jit(solution)/shard_map/ppermute | solution.py:52
  104.6 28.1 %collective-permute-start.34 = (bf16[64,3840]{1,0:T(8,128)(2,1)S(1)}, bf16[64,3840]{1,0:T(8,128)(2,1)S(1)}, u32[]{:S(2)}, u32[]{:S(2)}) collective-permute-start(bf16[64,3840]{1,0:T(8,128)(2,1)S(1)} %pad_maximum_fusion.2.refs_0_), channel_id=1, source_target_pairs={{0,16},{1,19},{4,20},{5,23},{8,24},{9,27},{12,28},{13,31},{16,0},{... | collective-permute-start | bytes 1474568 | tf_op jit(solution)/shard_map/ppermute | solution.py:52
  106.7 9.6 %collective-permute-start.35 = (bf16[64,3328]{1,0:T(8,128)(2,1)S(1)}, bf16[64,3328]{1,0:T(8,128)(2,1)}, u32[]{:S(2)}, u32[]{:S(2)}) collective-permute-start(bf16[64,3328]{1,0:T(8,128)(2,1)S(1)} %pad_maximum_fusion.3.refs_0_), channel_id=1, source_target_pairs={{0,4},{1,13},{4,0},{5,9},{8,12},{9,5},{12,8},{13,1},{16,20},{17,29... | collective-permute-start | bytes 1277960 | tf_op jit(solution)/shard_map/ppermute | solution.py:52
  111.1 21.6 %collective-permute-start.38 = (bf16[64,3328]{1,0:T(8,128)(2,1)}, bf16[64,3328]{1,0:T(8,128)(2,1)}, u32[]{:S(2)}, u32[]{:S(2)}) collective-permute-start(bf16[64,3328]{1,0:T(8,128)(2,1)} %collective-permute-done.32.refs_1_), channel_id=1, source_target_pairs={{0,4},{1,13},{4,0},{5,9},{8,12},{9,5},{12,8},{13,1},{16,20},{17,29... | collective-permute-start | bytes 1277960 | tf_op jit(solution)/shard_map/ppermute | solution.py:52
  112.2 22.9 %collective-permute-start.36 = (bf16[64,3840]{1,0:T(8,128)(2,1)S(1)}, bf16[64,3840]{1,0:T(8,128)(2,1)S(1)}, u32[]{:S(2)}, u32[]{:S(2)}) collective-permute-start(bf16[64,3840]{1,0:T(8,128)(2,1)S(1)} %collective-permute-done.30.refs_1_), channel_id=1, source_target_pairs={{0,32},{1,97},{4,36},{5,101},{8,40},{9,105},{12,44},{13,109},{16,4... | collective-permute-start | bytes 1474568 | tf_op jit(solution)/shard_map/ppermute | solution.py:52
  116.3 19.5 %collective-permute-start.37 = (bf16[64,3840]{1,0:T(8,128)(2,1)S(1)}, bf16[64,3840]{1,0:T(8,128)(2,1)}, u32[]{:S(2)}, u32[]{:S(2)}) collective-permute-start(bf16[64,3840]{1,0:T(8,128)(2,1)S(1)} %collective-permute-done.31.refs_1_), channel_id=1, source_target_pairs={{0,16},{1,19},{4,20},{5,23},{8,24},{9,27},{12,28},{13,31},{16,0},{... | collective-permute-start | bytes 1474568 | tf_op jit(solution)/shard_map/ppermute | solution.py:52
  117.3 23.0 %collective-permute-start.47 = (bf16[64,3840]{1,0:T(8,128)(2,1)S(1)}, bf16[64,3840]{1,0:T(8,128)(2,1)S(1)}, u32[]{:S(2)}, u32[]{:S(2)}) collective-permute-start(bf16[64,3840]{1,0:T(8,128)(2,1)S(1)} %pad_maximum_fusion.1.refs_0_), channel_id=1, source_target_pairs={{0,1},{1,0},{2,3},{3,2},{4,5},{5,4},{6,7},{7,6},{8,9},{9,8},{10,11... | collective-permute-start | bytes 1474568 | tf_op jit(solution)/shard_map/ppermute | solution.py:52
  132.6 8.5 %collective-permute-start.43 = (bf16[64,3840]{1,0:T(8,128)(2,1)S(1)}, bf16[64,3840]{1,0:T(8,128)(2,1)S(1)}, u32[]{:S(2)}, u32[]{:S(2)}) collective-permute-start(bf16[64,3840]{1,0:T(8,128)(2,1)S(1)} %pad_maximum_fusion.2.refs_0_), channel_id=1, source_target_pairs={{0,1},{1,0},{2,3},{3,2},{4,5},{5,4},{6,7},{7,6},{8,9},{9,8},{10,11... | collective-permute-start | bytes 1474568 | tf_op jit(solution)/shard_map/ppermute | solution.py:52
  132.7 9.7 %collective-permute-start.49 = (bf16[64,3840]{1,0:T(8,128)(2,1)S(1)}, bf16[64,3840]{1,0:T(8,128)(2,1)S(1)}, u32[]{:S(2)}, u32[]{:S(2)}) collective-permute-start(bf16[64,3840]{1,0:T(8,128)(2,1)S(1)} %collective-permute-done.33.refs_2_), channel_id=1, source_target_pairs={{0,1},{1,0},{2,3},{3,2},{4,5},{5,4},{6,7},{7,6},{8,9},{9,8},{10,11... | collective-permute-start | bytes 1474568 | tf_op jit(solution)/shard_map/ppermute | solution.py:52
  135.2 8.1 %collective-permute-start.48 = (bf16[64,3840]{1,0:T(8,128)(2,1)S(1)}, bf16[64,3840]{1,0:T(8,128)(2,1)S(1)}, u32[]{:S(2)}, u32[]{:S(2)}) collective-permute-start(bf16[64,3840]{1,0:T(8,128)(2,1)S(1)} %collective-permute-done.30.refs_1_), channel_id=1, source_target_pairs={{0,1},{1,0},{2,3},{3,2},{4,5},{5,4},{6,7},{7,6},{8,9},{9,8},{10,11... | collective-permute-start | bytes 1474568 | tf_op jit(solution)/shard_map/ppermute | solution.py:52
  135.8 8.7 %collective-permute-start.45 = (bf16[64,3840]{1,0:T(8,128)(2,1)S(1)}, bf16[64,3840]{1,0:T(8,128)(2,1)S(1)}, u32[]{:S(2)}, u32[]{:S(2)}) collective-permute-start(bf16[64,3840]{1,0:T(8,128)(2,1)S(1)} %collective-permute-done.34.refs_2_), channel_id=1, source_target_pairs={{0,1},{1,0},{2,3},{3,2},{4,5},{5,4},{6,7},{7,6},{8,9},{9,8},{10,11... | collective-permute-start | bytes 1474568 | tf_op jit(solution)/shard_map/ppermute | solution.py:52
  143.2 11.6 %collective-permute-start.46 = (bf16[64,3840]{1,0:T(8,128)(2,1)}, bf16[64,3840]{1,0:T(8,128)(2,1)}, u32[]{:S(2)}, u32[]{:S(2)}) collective-permute-start(bf16[64,3840]{1,0:T(8,128)(2,1)} %collective-permute-done.37.refs_3_), channel_id=1, source_target_pairs={{0,1},{1,0},{2,3},{3,2},{4,5},{5,4},{6,7},{7,6},{8,9},{9,8},{10,11... | collective-permute-start | bytes 1474568 | tf_op jit(solution)/shard_map/ppermute | solution.py:52
  144.0 14.7 %collective-permute-start.39 = (bf16[64,3328]{1,0:T(8,128)(2,1)S(1)}, bf16[64,3328]{1,0:T(8,128)(2,1)}, u32[]{:S(2)}, u32[]{:S(2)}) collective-permute-start(bf16[64,3328]{1,0:T(8,128)(2,1)S(1)} %pad_maximum_fusion.3.refs_0_), channel_id=1, source_target_pairs={{0,1},{1,0},{2,3},{3,2},{4,5},{5,4},{6,7},{7,6},{8,9},{9,8},{10,11... | collective-permute-start | bytes 1277960 | tf_op jit(solution)/shard_map/ppermute | solution.py:52
  145.3 13.4 %collective-permute-start.41 = (bf16[64,3328]{1,0:T(8,128)(2,1)}, bf16[64,3328]{1,0:T(8,128)(2,1)}, u32[]{:S(2)}, u32[]{:S(2)}) collective-permute-start(bf16[64,3328]{1,0:T(8,128)(2,1)} %collective-permute-done.35.refs_2_), channel_id=1, source_target_pairs={{0,1},{1,0},{2,3},{3,2},{4,5},{5,4},{6,7},{7,6},{8,9},{9,8},{10,11... | collective-permute-start | bytes 1277960 | tf_op jit(solution)/shard_map/ppermute | solution.py:52
  146.1 12.6 %collective-permute-start.40 = (bf16[64,3328]{1,0:T(8,128)(2,1)}, bf16[64,3328]{1,0:T(8,128)(2,1)}, u32[]{:S(2)}, u32[]{:S(2)}) collective-permute-start(bf16[64,3328]{1,0:T(8,128)(2,1)} %collective-permute-done.32.refs_1_), channel_id=1, source_target_pairs={{0,1},{1,0},{2,3},{3,2},{4,5},{5,4},{6,7},{7,6},{8,9},{9,8},{10,11... | collective-permute-start | bytes 1277960 | tf_op jit(solution)/shard_map/ppermute | solution.py:52
  147.4 11.3 %collective-permute-start.42 = (bf16[64,3328]{1,0:T(8,128)(2,1)}, bf16[64,3328]{1,0:T(8,128)(2,1)}, u32[]{:S(2)}, u32[]{:S(2)}) collective-permute-start(bf16[64,3328]{1,0:T(8,128)(2,1)} %collective-permute-done.38.refs_3_), channel_id=1, source_target_pairs={{0,1},{1,0},{2,3},{3,2},{4,5},{5,4},{6,7},{7,6},{8,9},{9,8},{10,11... | collective-permute-start | bytes 1277960 | tf_op jit(solution)/shard_map/ppermute | solution.py:52
  (38 other events, 150.9 us)

commit v3 on v2

v3 whole, which is shorter than its diff:
```python
import itertools

import jax
import jax.numpy as jnp
from jax import lax
from jax.experimental import pallas as pl
from jax.experimental.pallas import tpu as pltpu
from jax.sharding import PartitionSpec as P

STEP = 100

beta_first = 0.9
beta_second = 0.999
epsilon = 1e-08
galore_scale = 0.25

AXES = ("dp", "outer")
WIDTH = 3840
PIECES = ((0, 3840), (3840, 3840), (7680, 3328))
X, Y, Z = 0, 1, 2
BITS = (
    ((X, 0), (Z, 0), (Y, 0)),
    ((Y, 0), (X, 0), (Z, 0)),
    ((Z, 0), (Y, 0), (X, 0)),
)
LAST = ((X, 1), (Y, 1), (Z, 1))


def linear(x, y, z, core):
    return (((x * 2 + y % 2) * 4 + z) * 2 + y // 2) * 2 + core


def code(second, core):
    return 1 + 2 * ((second + core) % 2)


def exchange(*bits):
    pairs = []
    for x, y, z, core in itertools.product(range(4), range(4), range(4), range(2)):
        there = [x, y, z]
        for axis, second in bits:
            there[axis] ^= code(second, core)
        pairs.append((linear(x, y, z, core), linear(*there, core)))
    return pairs


SWAP = [(2 * i + core, 2 * i + 1 - core) for i in range(64) for core in range(2)]


def groups():
    found = []
    for x, y, z, core in itertools.product(range(4), range(4), range(4), range(2)):
        last = code(1, core)
        if all(at < at ^ last for at in (x, y, z)):
            corners = itertools.product((0, last), repeat=3)
            found.append([linear(x ^ dx, y ^ dy, z ^ dz, core) for dx, dy, dz in corners])
    return found


def swap_groups(value):
    return lax.all_to_all(value, AXES, 0, 0, axis_index_groups=groups(), tiled=True)


def send(value, pairs):
    return lax.ppermute(value, AXES, pairs)


def send_pieces(values, level):
    values = lax.optimization_barrier(tuple(values))
    return lax.optimization_barrier(
        tuple(send(v, exchange(bits[level])) for v, bits in zip(values, BITS))
    )


def rank_order(bits, dp, outer):
    here = (dp // 8, (outer // 2) * 2 + (dp // 4) % 2, dp % 4)
    place = lax.iota(jnp.int32, 512)
    core = (outer + place // 256) % 2
    there = list(here)
    for level, (axis, second) in enumerate(bits):
        there[axis] = there[axis] ^ ((place // (128 >> level)) % 2 * code(second, core))
    for level, (axis, second) in enumerate(LAST):
        last = code(second, core)
        first = jnp.minimum(there[axis], there[axis] ^ last)
        there[axis] = first ^ ((place // (16 >> level)) % 2 * last)
    return linear(*there, core) * 4 + place % 4


def project_kernel(tokens_ref, basis_ref, out_ref, total_ref):
    step = pl.program_id(0)
    product = jnp.dot(tokens_ref[...], basis_ref[...], preferred_element_type=jnp.float32)

    @pl.when(step == 0)
    def _():
        total_ref[...] = product

    @pl.when(step > 0)
    def _():
        total_ref[...] += product

    @pl.when(step == pl.num_programs(0) - 1)
    def _():
        out_ref[...] = total_ref[...].astype(jnp.bfloat16)


def project(tokens, basis, depth=1024):
    rows, width = tokens.shape[0], basis.shape[1]
    return pl.pallas_call(
        project_kernel,
        grid=(basis.shape[0] // depth,),
        in_specs=[
            pl.BlockSpec((rows, depth), lambda k: (0, k)),
            pl.BlockSpec((depth, width), lambda k: (k, 0)),
        ],
        out_specs=pl.BlockSpec((rows, width), lambda k: (0, 0)),
        out_shape=jax.ShapeDtypeStruct((rows, width), jnp.bfloat16),
        scratch_shapes=[pltpu.VMEM((rows, width), jnp.float32)],
        cost_estimate=pl.CostEstimate(
            flops=2 * rows * basis.shape[0] * width,
            bytes_accessed=2 * (rows + width) * basis.shape[0],
            transcendentals=0,
        ),
        compiler_params=pltpu.CompilerParams(vmem_limit_bytes=8 * 1024 * 1024),
        name="project",
    )(tokens, basis)


def expand_kernel(basis_ref, *refs):
    for piece in range(3):

        @pl.when(pl.program_id(0) == piece)
        def _(piece=piece):
            size = PIECES[piece][1]
            low = jnp.concatenate([refs[piece][...], refs[3 + piece][...]], axis=0)
            product = jnp.dot(basis_ref[...], low, preferred_element_type=jnp.float32)
            if len(refs) == 8:
                product = -galore_scale * (refs[6][:, :size] + product)
            refs[-1][:, :size] = product


def expand(basis_rows, own, other, *early):
    rows, depth, width = basis_rows.shape[0], 2 * own[0].shape[0], sum(size for _, size in PIECES)
    total = pl.BlockSpec((rows, WIDTH), lambda j: (0, j))
    return pl.pallas_call(
        expand_kernel,
        grid=(3,),
        in_specs=[pl.BlockSpec((rows, depth), lambda j: (0, j))]
        + [pl.BlockSpec(block.shape, lambda j: (0, 0)) for block in (*own, *other)]
        + [total] * len(early),
        out_specs=total,
        out_shape=jax.ShapeDtypeStruct((rows, width), jnp.float32),
        cost_estimate=pl.CostEstimate(
            flops=2 * rows * depth * width,
            bytes_accessed=(2 * depth + 4 * rows) * width,
            transcendentals=0,
        ),
        compiler_params=pltpu.CompilerParams(vmem_limit_bytes=24 * 1024 * 1024),
        name="expand",
    )(basis_rows, *own, *other, *early)


def shards(tokens, grad_out, projection_basis, first_moment, second_moment):
    dp, outer = lax.axis_index("dp"), lax.axis_index("outer")
    f32, bf16 = jnp.float32, jnp.bfloat16

    places = jnp.concatenate([rank_order(bits, dp, outer) for bits in BITS])
    picks = (lax.broadcasted_iota(jnp.int32, (512, 1536), 0) == places[None, :]).astype(bf16)

    projected = project(tokens, projection_basis)
    projected = jnp.dot(projected, picks, preferred_element_type=f32).astype(bf16)

    local_width = projection_basis.shape[0] // 32
    basis_rows = lax.dynamic_slice_in_dim(projection_basis, dp * local_width, local_width, 0)
    projected, basis_rows = lax.optimization_barrier((projected, basis_rows))

    own, other = [], []
    for piece, (start, size) in enumerate(PIECES):
        terms = lax.dot_general(
            projected[:, 512 * piece : 512 * piece + 512],
            grad_out[:, start : start + size],
            (((0,), (0,)), ((), ())),
            preferred_element_type=f32,
        ).astype(bf16)
        own.append(terms[:256])
        other.append(terms[256:])
    sent = [o[128:].astype(f32) + send(t[128:], SWAP).astype(f32) for o, t in zip(own, other)]
    held = [o[:128].astype(f32) + send(t[:128], SWAP).astype(f32) for o, t in zip(own, other)]
    for level in range(3):
        got = send_pieces([s.astype(bf16) for s in sent], level)
        if level == 0:
            basis_rows = jnp.dot(basis_rows, picks, preferred_element_type=f32).astype(bf16)
            starts = range(0, 1536, 256)
            early_basis = jnp.concatenate([basis_rows[:, at : at + 128] for at in starts], axis=1)
            late_basis = jnp.concatenate([basis_rows[:, at + 128 : at + 256] for at in starts], axis=1)
            got, early_basis, late_basis = lax.optimization_barrier((got, early_basis, late_basis))
        held = [h + g.astype(f32) for h, g in zip(held, got)]
        half = held[0].shape[0] // 2
        if level < 2:
            sent, held = [h[half:] for h in held], [h[:half] for h in held]
    held = jnp.concatenate(held, axis=1)
    terms = swap_groups(held.astype(bf16).reshape(8, 4, -1))
    owned_grad = jnp.sum(terms.astype(f32), axis=0)

    new_first = beta_first * first_moment + (1.0 - beta_first) * owned_grad
    new_second = beta_second * second_moment + (1.0 - beta_second) * owned_grad * owned_grad
    first_bias = 1.0 - beta_first**STEP
    second_bias = 1.0 - beta_second**STEP
    low_update = (new_first / first_bias / (jnp.sqrt(new_second / second_bias) + epsilon)).astype(bf16)

    low = swap_groups(jnp.broadcast_to(low_update[None], (8, *low_update.shape)))
    low = low.reshape(32, -1)
    low = [low[:, start : start + size] for start, size in PIECES]
    for level in (2, 1):
        got = send_pieces(low, level)
        low = [jnp.concatenate([mine, theirs], axis=0) for mine, theirs in zip(low, got)]
    late = send_pieces(low, 0)
    early = expand(early_basis, low, [send(part, SWAP) for part in low])
    weight_update = expand(late_basis, late, [send(part, SWAP) for part in late], early)
    return (weight_update, new_first, new_second)


def solution(mesh):
    in_specs = (
        P(("dp", "outer"), None),
        P(("dp", "outer"), None),
        P(),
        P(("dp", "outer"), None),
        P(("dp", "outer"), None),
    )
    out_specs = (P("dp", None), P(("dp", "outer"), None), P(("dp", "outer"), None))
    return jax.shard_map(shards, mesh=mesh, in_specs=in_specs, out_specs=out_specs, check_vma=False)
```

time: 164 us -> 146 us (0.89)
  blocking collectives: 0 us -> 20.7 us
  starting transfers between devices: 68 us -> 52.9 us
  waiting for transfers between devices: 52.1 us -> 43 us
  matrix products: 17 us -> 8.32 us
  local copies, waits for them, and re-layouts: 10.2 us -> 6.59 us
  Pallas kernels: 10.9 us -> 9.01 us
    all_to_all x0 -> x2, blocking collectives: none -> 20.7 us  [swap_groups(): lax.all_to_all(value, AXES, 0, 0, axis_index_groups=groups(), tiled=True)]
    ppermute x51 -> x30, starting transfers between devices: 68 us -> 52.9 us  [send(): return lax.ppermute(value, AXES, pairs)]
    ppermute x51 -> x30, waiting for transfers between devices: 52.1 us -> 43 us  [send(): return lax.ppermute(value, AXES, pairs)]
    dot_general x1, matrix products: 6.63 us -> 1.05 us  [shards(): jnp.dot(projected, picks, preferred_element_type=f32).astype(bf16)]
    unnamed x38 -> x15, local copies, waits for them, and re-layouts: 9.46 us -> 4.48 us
    dot_general x3, matrix products: 8.76 us -> 6.52 us  [shards(): lax.dot_general(projected[:, 512 * piece:512 * piece + 512], grad_out[:,...]
    pallas_call x3, Pallas kernels: 10.9 us -> 9.01 us  [the longest x2 5.44 us: expand(): pl.pallas_call(expand_kernel, grid=(3,), in_specs=[pl.BlockSpec((rows, de...]
  transfers between devices with their start and end apart: 51 -> 30, of which waited for: 19 -> 12; matrix products, arithmetic and copies ran while one was open for 5% -> 5% of each run, Pallas kernels for 4% -> 1%
where the time goes in v3:
time: 146 us
  starting transfers between devices  52.9 us (36%)
  waiting for transfers between devices  43 us (29%)
  blocking collectives  20.7 us (14%)
  Pallas kernels  9.01 us (6%)
  matrix products  8.32 us (6%)
  local copies, waits for them, and re-layouts  6.59 us (5%)
  other arithmetic  4.2 us (3%)
    ppermute x30, starting transfers between devices, send(): return lax.ppermute(value, AXES, pairs)  52.9 us
    ppermute x30, waiting for transfers between devices, send(): return lax.ppermute(value, AXES, pairs)  43 us
    all_to_all x2, blocking collectives, swap_groups(): lax.all_to_all(value, AXES, 0, 0, axis_index_groups=groups(), tiled=True)  20.7 us
    dot_general x3, matrix products, shards(): lax.dot_general(projected[:, 512 * piece:512 * piece + 512], grad_out[:,...  6.52 us
    pallas_call x2, Pallas kernels, expand(): pl.pallas_call(expand_kernel, grid=(3,), in_specs=[pl.BlockSpec((rows, de...  5.44 us
    unnamed x15, local copies, waits for them, and re-layouts  4.48 us
    pallas_call x1, Pallas kernels, project(): pl.pallas_call(project_kernel, grid=(basis.shape[0] // depth,), in_specs=...  3.57 us
  transfers between devices with their start and end apart: 30, of which 12 were waited for; matrix products, arithmetic and copies ran while one was open for 5% of the time, Pallas kernels for 1%

profile of v3, /device:TPU:1, one launch (start us, length us, event | category | flops | bytes accessed | tf_op | source)
XLA Modules:
  0.0 145.9 jit_solution(17259939669585546756)
XLA Ops:
  1.7 2.2 %copy-done = bf16[4096,512]{1,0:T(8,128)(2,1)S(1)} copy-done((bf16[4096,512]{1,0:T(8,128)(2,1)S(1)}, bf16[4096,512]{1,0:T(8,128)(2,1)}, u32[]{:S(2)}) %copy-start) | copy-done | bytes 4194328
  3.9 2.2 %copy-done.1 = bf16[512,4096]{1,0:T(8,128)(2,1)S(1)} copy-done((bf16[512,4096]{1,0:T(8,128)(2,1)S(1)}, bf16[512,4096]{1,0:T(8,128)(2,1)}, u32[]{:S(2)}) %copy-start.1) | copy-done | bytes 4194328
  6.1 3.6 %project.1 = bf16[512,512]{1,0:T(8,128)(2,1)S(1)} custom-call(bf16[512,4096]{1,0:T(8,128)(2,1)S(1)} %copy-done.1, bf16[4096,512]{1,0:T(8,128)(2,1)S(1)} %copy-done), custom_call_target="tpu_custom_call" | custom-call | flops 2147483648 | bytes 8388608 | tf_op jit(solution)/shard_map/project/pallas_call | solution.py:108
  10.7 2.0 %convolution_convert_fusion = bf16[512,3328]{1,0:T(8,128)(2,1)S(1)} fusion(bf16[512,11008]{1,0:T(8,128)(2,1)S(1)} %copy-done.2, bf16[512,1536]{1,0:T(8,128)(2,1)S(1)} %fusion.5), kind=kOutput, calls=%fused_computation | convolution fusion | flops 1746534400 | bytes 7340032 | tf_op jit(solution)/shard_map/dot_general | solution.py:178
  12.9 1.5 %collective-permute-start.8 = (bf16[128,3328]{1,0:T(8,128)(2,1)S(1)}, bf16[128,3328]{1,0:T(8,128)(2,1)S(1)}, u32[]{:S(2)}, u32[]{:S(2)}) collective-permute-start(bf16[128,3328]{1,0:T(8,128)(2,1)S(1)} %get-tuple-element.96), channel_id=1, source_target_pairs={{0,1},{1,0},{2,3},{3,2},{4,5},{5,4},{6,7},{7,6},{8,9},{9,8},{10,11... | collective-permute-start | bytes 2555912 | tf_op jit(solution)/shard_map/ppermute | solution.py:65
  14.4 2.3 %convolution_convert_fusion.1 = bf16[512,3840]{1,0:T(8,128)(2,1)S(1)} fusion(bf16[512,11008]{1,0:T(8,128)(2,1)S(1)} %copy-done.2, bf16[512,1536]{1,0:T(8,128)(2,1)S(1)} %fusion.5), kind=kOutput, calls=%fused_computation.1 | convolution fusion | flops 2015232000 | bytes 8388608 | tf_op jit(solution)/shard_map/dot_general | solution.py:178
  17.4 2.3 %convolution_convert_fusion.2 = bf16[512,3840]{1,0:T(8,128)(2,1)S(1)} fusion(bf16[512,11008]{1,0:T(8,128)(2,1)S(1)} %copy-done.2, bf16[512,1536]{1,0:T(8,128)(2,1)S(1)} %fusion.5), kind=kOutput, calls=%fused_computation.2 | convolution fusion | flops 2015232000 | bytes 8388608 | tf_op jit(solution)/shard_map/dot_general | solution.py:178
  22.9 2.6 %collective-permute-start.3 = (bf16[128,3840]{1,0:T(8,128)(2,1)S(1)}, bf16[128,3840]{1,0:T(8,128)(2,1)S(1)}, u32[]{:S(2)}, u32[]{:S(2)}) collective-permute-start(bf16[128,3840]{1,0:T(8,128)(2,1)S(1)} %add_convert_fusion.1), channel_id=1, source_target_pairs={{0,32},{1,97},{4,36},{5,101},{8,40},{9,105},{12,44},{13,109},{16,4... | collective-permute-start | bytes 2949128 | tf_op jit(solution)/shard_map/ppermute | solution.py:65
  25.5 2.7 %collective-permute-start.4 = (bf16[128,3840]{1,0:T(8,128)(2,1)S(1)}, bf16[128,3840]{1,0:T(8,128)(2,1)S(1)}, u32[]{:S(2)}, u32[]{:S(2)}) collective-permute-start(bf16[128,3840]{1,0:T(8,128)(2,1)S(1)} %add_convert_fusion), channel_id=1, source_target_pairs={{0,16},{1,19},{4,20},{5,23},{8,24},{9,27},{12,28},{13,31},{16,0},{... | collective-permute-start | bytes 2949128 | tf_op jit(solution)/shard_map/ppermute | solution.py:65
  28.2 3.8 %collective-permute-start.5 = (bf16[128,3328]{1,0:T(8,128)(2,1)S(1)}, bf16[128,3328]{1,0:T(8,128)(2,1)S(1)}, u32[]{:S(2)}, u32[]{:S(2)}) collective-permute-start(bf16[128,3328]{1,0:T(8,128)(2,1)S(1)} %add_convert_fusion.2), channel_id=1, source_target_pairs={{0,4},{1,13},{4,0},{5,9},{8,12},{9,5},{12,8},{13,1},{16,20},{17,29... | collective-permute-start | bytes 2555912 | tf_op jit(solution)/shard_map/ppermute | solution.py:65
  32.2 10.0 %collective-permute-done.5 = bf16[128,3328]{1,0:T(8,128)(2,1)S(1)} collective-permute-done((bf16[128,3328]{1,0:T(8,128)(2,1)S(1)}, bf16[128,3328]{1,0:T(8,128)(2,1)S(1)}, u32[]{:S(2)}, u32[]{:S(2)}) %collective-permute-start.5) | collective-permute-done | bytes 852000 | tf_op jit(solution)/shard_map/ppermute | solution.py:65
  42.5 2.2 %collective-permute-done.6 = bf16[128,3840]{1,0:T(8,128)(2,1)S(1)} collective-permute-done((bf16[128,3840]{1,0:T(8,128)(2,1)S(1)}, bf16[128,3840]{1,0:T(8,128)(2,1)S(1)}, u32[]{:S(2)}, u32[]{:S(2)}) %collective-permute-start.6) | collective-permute-done | bytes 983072 | tf_op jit(solution)/shard_map/ppermute | solution.py:65
  45.7 2.8 %collective-permute-start.9 = (bf16[64,3840]{1,0:T(8,128)(2,1)S(1)}, bf16[64,3840]{1,0:T(8,128)(2,1)S(1)}, u32[]{:S(2)}, u32[]{:S(2)}) collective-permute-start(bf16[64,3840]{1,0:T(8,128)(2,1)S(1)} %slice.292), channel_id=1, source_target_pairs={{0,4},{1,13},{4,0},{5,9},{8,12},{9,5},{12,8},{13,1},{16,20},{17,29... | collective-permute-start | bytes 1474568 | tf_op jit(solution)/shard_map/ppermute | solution.py:65
  50.0 6.9 %collective-permute-done.11 = bf16[64,3328]{1,0:T(8,128)(2,1)S(1)} collective-permute-done((bf16[64,3328]{1,0:T(8,128)(2,1)S(1)}, bf16[64,3328]{1,0:T(8,128)(2,1)S(1)}, u32[]{:S(2)}, u32[]{:S(2)}) %collective-permute-start.11) | collective-permute-done | bytes 426016 | tf_op jit(solution)/shard_map/ppermute | solution.py:65
  60.0 4.6 %collective-permute-done.14 = bf16[32,3328]{1,0:T(8,128)(2,1)S(1)} collective-permute-done((bf16[32,3328]{1,0:T(8,128)(2,1)S(1)}, bf16[32,3328]{1,0:T(8,128)(2,1)S(1)}, u32[]{:S(2)}, u32[]{:S(2)}) %collective-permute-start.14) | collective-permute-done | bytes 213024 | tf_op jit(solution)/shard_map/ppermute | solution.py:65
  65.6 10.4 %all_to_all.10 = bf16[8,4,11008]{2,1,0:T(4,128)(2,1)S(1)} all-to-all(bf16[8,4,11008]{2,1,0:T(4,128)(2,1)S(1)} %pad_maximum_fusion.3), channel_id=1, replica_groups={{0,12,18,30,96,108,114,126},{1,5,17,21,33,37,49,53},{4,8,22,26,100,104,..., dimensions={0} | all-to-all | bytes 1409024 | tf_op jit(solution)/shard_map/all_to_all | solution.py:61
  77.4 10.4 %all_to_all.11 = bf16[8,4,11008]{2,1,0:T(4,128)(2,1)S(1)} all-to-all(bf16[8,4,11008]{2,1,0:T(4,128)(2,1)S(1)} %broadcast_in_dim.2), channel_id=1, replica_groups={{0,12,18,30,96,108,114,126},{1,5,17,21,33,37,49,53},{4,8,22,26,100,104,..., dimensions={0} | all-to-all | bytes 1409024 | tf_op jit(solution)/shard_map/all_to_all | solution.py:61
  89.2 2.6 %collective-permute-start.16 = (bf16[32,3840]{1,0:T(8,128)(2,1)S(1)}, bf16[32,3840]{1,0:T(8,128)(2,1)S(1)}, u32[]{:S(2)}, u32[]{:S(2)}) collective-permute-start(bf16[32,3840]{1,0:T(8,128)(2,1)S(1)} %get-tuple-element.71), channel_id=1, source_target_pairs={{0,4},{1,13},{4,0},{5,9},{8,12},{9,5},{12,8},{13,1},{16,20},{17,29... | collective-permute-start | bytes 737288 | tf_op jit(solution)/shard_map/ppermute | solution.py:65
  91.8 1.7 %collective-permute-start.17 = (bf16[32,3328]{1,0:T(8,128)(2,1)S(1)}, bf16[32,3328]{1,0:T(8,128)(2,1)S(1)}, u32[]{:S(2)}, u32[]{:S(2)}) collective-permute-start(bf16[32,3328]{1,0:T(8,128)(2,1)S(1)} %slice.242), channel_id=1, source_target_pairs={{0,32},{1,97},{4,36},{5,101},{8,40},{9,105},{12,44},{13,109},{16,4... | collective-permute-start | bytes 638984 | tf_op jit(solution)/shard_map/ppermute | solution.py:65
  93.4 4.6 %collective-permute-done.17 = bf16[32,3328]{1,0:T(8,128)(2,1)S(1)} collective-permute-done((bf16[32,3328]{1,0:T(8,128)(2,1)S(1)}, bf16[32,3328]{1,0:T(8,128)(2,1)S(1)}, u32[]{:S(2)}, u32[]{:S(2)}) %collective-permute-start.17) | collective-permute-done | bytes 213024 | tf_op jit(solution)/shard_map/ppermute | solution.py:65
  98.1 2.4 %collective-permute-start.18 = (bf16[64,3840]{1,0:T(8,128)(2,1)S(1)}, bf16[64,3840]{1,0:T(8,128)(2,1)S(1)}, u32[]{:S(2)}, u32[]{:S(2)}) collective-permute-start(bf16[64,3840]{1,0:T(8,128)(2,1)S(1)} %pad_maximum_fusion.4), channel_id=1, source_target_pairs={{0,4},{1,13},{4,0},{5,9},{8,12},{9,5},{12,8},{13,1},{16,20},{17,29... | collective-permute-start | bytes 1474568 | tf_op jit(solution)/shard_map/ppermute | solution.py:65
  101.9 1.4 collective-permute-start.20
  103.4 6.8 %collective-permute-done.20 = bf16[64,3328]{1,0:T(8,128)(2,1)S(1)} collective-permute-done((bf16[64,3328]{1,0:T(8,128)(2,1)S(1)}, bf16[64,3328]{1,0:T(8,128)(2,1)S(1)}, u32[]{:S(2)}, u32[]{:S(2)}) %collective-permute-start.20) | collective-permute-done | bytes 426016 | tf_op jit(solution)/shard_map/ppermute | solution.py:65
  110.3 1.4 collective-permute-start.21
  111.8 1.5 %collective-permute-start.22 = (bf16[128,3840]{1,0:T(8,128)(2,1)S(1)}, bf16[128,3840]{1,0:T(8,128)(2,1)S(1)}, u32[]{:S(2)}, u32[]{:S(2)}) collective-permute-start(bf16[128,3840]{1,0:T(8,128)(2,1)S(1)} %pad_maximum_fusion.1.refs_1_), channel_id=1, source_target_pairs={{0,16},{1,19},{4,20},{5,23},{8,24},{9,27},{12,28},{13,31},{16,0},{... | collective-permute-start | bytes 2949128 | tf_op jit(solution)/shard_map/ppermute | solution.py:65
  114.5 9.1 %collective-permute-start.29 = (bf16[128,3328]{1,0:T(8,128)(2,1)S(1)}, bf16[128,3328]{1,0:T(8,128)(2,1)S(1)}, u32[]{:S(2)}, u32[]{:S(2)}) collective-permute-start(bf16[128,3328]{1,0:T(8,128)(2,1)S(1)} %pad_maximum_fusion.2.refs_2_), channel_id=1, source_target_pairs={{0,1},{1,0},{2,3},{3,2},{4,5},{5,4},{6,7},{7,6},{8,9},{9,8},{10,11... | collective-permute-start | bytes 2555912 | tf_op jit(solution)/shard_map/ppermute | solution.py:65
  123.6 2.4 %collective-permute-done.23.refs_2_ = bf16[128,3328]{1,0:T(8,128)(2,1)S(1)} collective-permute-done((bf16[128,3328]{1,0:T(8,128)(2,1)S(1)}, bf16[128,3328]{1,0:T(8,128)(2,1)S(1)}, u32[]{:S(2)}, u32[]{:S(2)}) %collective-permute-start.23) | collective-permute-done | bytes 852000 | tf_op jit(solution)/shard_map/ppermute | solution.py:65
  126.0 10.0 %collective-permute-start.27 = (bf16[128,3840]{1,0:T(8,128)(2,1)S(1)}, bf16[128,3840]{1,0:T(8,128)(2,1)S(1)}, u32[]{:S(2)}, u32[]{:S(2)}) collective-permute-start(bf16[128,3840]{1,0:T(8,128)(2,1)S(1)} %pad_maximum_fusion.refs_0_), channel_id=1, source_target_pairs={{0,1},{1,0},{2,3},{3,2},{4,5},{5,4},{6,7},{7,6},{8,9},{9,8},{10,11... | collective-permute-start | bytes 2949128 | tf_op jit(solution)/shard_map/ppermute | solution.py:65
  136.6 1.6 %collective-permute-done.27.refs_3_ = bf16[128,3840]{1,0:T(8,128)(2,1)S(1)} collective-permute-done((bf16[128,3840]{1,0:T(8,128)(2,1)S(1)}, bf16[128,3840]{1,0:T(8,128)(2,1)S(1)}, u32[]{:S(2)}, u32[]{:S(2)}) %collective-permute-start.27) | collective-permute-done | bytes 983072 | tf_op jit(solution)/shard_map/ppermute | solution.py:65
  138.2 1.8 %expand.2.refs_6_ = f32[128,11008]{1,0:T(8,128)S(1)} custom-call(bf16[128,768]{1,0:T(8,128)(2,1)S(1)} %get-tuple-element.88.basis_ref, bf16[128,3840]{1,0:T(8,128)(2,1)S(1)} %pad_maximum_fusion.refs_0_, bf16[128,3840]{1,0:T(8,128)(2,1)S(1)} %pad_maximum_fusion.1.refs_1_, bf16[128,3328]{1,0:T(8,128)(2,1)S(1)} %pad_maximum_fusion.2.refs_2_, ...), custom_call_target="tpu_custom_call" | custom-call | flops 721420288 | bytes 11272192 | tf_op jit(solution)/shard_map/expand/pallas_call | solution.py:144
  139.9 2.2 %collective-permute-done.26.refs_5_ = bf16[128,3328]{1,0:T(8,128)(2,1)S(1)} collective-permute-done((bf16[128,3328]{1,0:T(8,128)(2,1)S(1)}, bf16[128,3328]{1,0:T(8,128)(2,1)S(1)}, u32[]{:S(2)}, u32[]{:S(2)}) %collective-permute-start.26) | collective-permute-done | bytes 852000 | tf_op jit(solution)/shard_map/ppermute | solution.py:65
  142.2 3.7 %expand.3 = f32[128,11008]{1,0:T(8,128)} custom-call(bf16[128,768]{1,0:T(8,128)(2,1)S(1)} %get-tuple-element.54.basis_ref, bf16[128,3840]{1,0:T(8,128)(2,1)S(1)} %collective-permute-done.21.refs_0_, bf16[128,3840]{1,0:T(8,128)(2,1)S(1)} %collective-permute-done.22.refs_1_, bf16[128,3328]{1,0:T(8,128)(2,1)S(1)} %collective-permute-done.23.refs_2_, ...), custom_call_target="tpu_custom_call" | custom-call | flops 721420288 | bytes 11272192 | tf_op jit(solution)/shard_map/expand/pallas_call | solution.py:144
  (95 shorter events, 19.3 us)
Async XLA Ops:
  12.9 29.3 %collective-permute-start.8 = (bf16[128,3328]{1,0:T(8,128)(2,1)S(1)}, bf16[128,3328]{1,0:T(8,128)(2,1)S(1)}, u32[]{:S(2)}, u32[]{:S(2)}) collective-permute-start(bf16[128,3328]{1,0:T(8,128)(2,1)S(1)} %get-tuple-element.96), channel_id=1, source_target_pairs={{0,1},{1,0},{2,3},{3,2},{4,5},{5,4},{6,7},{7,6},{8,9},{9,8},{10,11... | collective-permute-start | bytes 2555912 | tf_op jit(solution)/shard_map/ppermute | solution.py:65
  14.4 6.8 %collective-permute-start.2 = (bf16[128,3328]{1,0:T(8,128)(2,1)S(1)}, bf16[128,3328]{1,0:T(8,128)(2,1)S(1)}, u32[]{:S(2)}, u32[]{:S(2)}) collective-permute-start(bf16[128,3328]{1,0:T(8,128)(2,1)S(1)} %get-tuple-element.97), channel_id=1, source_target_pairs={{0,1},{1,0},{2,3},{3,2},{4,5},{5,4},{6,7},{7,6},{8,9},{9,8},{10,11... | collective-permute-start | bytes 2555912 | tf_op jit(solution)/shard_map/ppermute | solution.py:65
  16.9 28.3 %collective-permute-start.7 = (bf16[128,3840]{1,0:T(8,128)(2,1)S(1)}, bf16[128,3840]{1,0:T(8,128)(2,1)S(1)}, u32[]{:S(2)}, u32[]{:S(2)}) collective-permute-start(bf16[128,3840]{1,0:T(8,128)(2,1)S(1)} %get-tuple-element.92), channel_id=1, source_target_pairs={{0,1},{1,0},{2,3},{3,2},{4,5},{5,4},{6,7},{7,6},{8,9},{9,8},{10,11... | collective-permute-start | bytes 2949128 | tf_op jit(solution)/shard_map/ppermute | solution.py:65
  17.4 4.0 %collective-permute-start.1 = (bf16[128,3840]{1,0:T(8,128)(2,1)S(1)}, bf16[128,3840]{1,0:T(8,128)(2,1)S(1)}, u32[]{:S(2)}, u32[]{:S(2)}) collective-permute-start(bf16[128,3840]{1,0:T(8,128)(2,1)S(1)} %get-tuple-element.93), channel_id=1, source_target_pairs={{0,1},{1,0},{2,3},{3,2},{4,5},{5,4},{6,7},{7,6},{8,9},{9,8},{10,11... | collective-permute-start | bytes 2949128 | tf_op jit(solution)/shard_map/ppermute | solution.py:65
  19.9 2.7 %collective-permute-start = (bf16[128,3840]{1,0:T(8,128)(2,1)S(1)}, bf16[128,3840]{1,0:T(8,128)(2,1)S(1)}, u32[]{:S(2)}, u32[]{:S(2)}) collective-permute-start(bf16[128,3840]{1,0:T(8,128)(2,1)S(1)} %get-tuple-element.95), channel_id=1, source_target_pairs={{0,1},{1,0},{2,3},{3,2},{4,5},{5,4},{6,7},{7,6},{8,9},{9,8},{10,11... | collective-permute-start | bytes 2949128 | tf_op jit(solution)/shard_map/ppermute | solution.py:65
  22.9 19.3 %collective-permute-start.3 = (bf16[128,3840]{1,0:T(8,128)(2,1)S(1)}, bf16[128,3840]{1,0:T(8,128)(2,1)S(1)}, u32[]{:S(2)}, u32[]{:S(2)}) collective-permute-start(bf16[128,3840]{1,0:T(8,128)(2,1)S(1)} %add_convert_fusion.1), channel_id=1, source_target_pairs={{0,32},{1,97},{4,36},{5,101},{8,40},{9,105},{12,44},{13,109},{16,4... | collective-permute-start | bytes 2949128 | tf_op jit(solution)/shard_map/ppermute | solution.py:65
  25.5 16.7 %collective-permute-start.4 = (bf16[128,3840]{1,0:T(8,128)(2,1)S(1)}, bf16[128,3840]{1,0:T(8,128)(2,1)S(1)}, u32[]{:S(2)}, u32[]{:S(2)}) collective-permute-start(bf16[128,3840]{1,0:T(8,128)(2,1)S(1)} %add_convert_fusion), channel_id=1, source_target_pairs={{0,16},{1,19},{4,20},{5,23},{8,24},{9,27},{12,28},{13,31},{16,0},{... | collective-permute-start | bytes 2949128 | tf_op jit(solution)/shard_map/ppermute | solution.py:65
  28.2 13.9 %collective-permute-start.5 = (bf16[128,3328]{1,0:T(8,128)(2,1)S(1)}, bf16[128,3328]{1,0:T(8,128)(2,1)S(1)}, u32[]{:S(2)}, u32[]{:S(2)}) collective-permute-start(bf16[128,3328]{1,0:T(8,128)(2,1)S(1)} %add_convert_fusion.2), channel_id=1, source_target_pairs={{0,4},{1,13},{4,0},{5,9},{8,12},{9,5},{12,8},{13,1},{16,20},{17,29... | collective-permute-start | bytes 2555912 | tf_op jit(solution)/shard_map/ppermute | solution.py:65
  42.2 2.6 %collective-permute-start.6 = (bf16[128,3840]{1,0:T(8,128)(2,1)S(1)}, bf16[128,3840]{1,0:T(8,128)(2,1)S(1)}, u32[]{:S(2)}, u32[]{:S(2)}) collective-permute-start(bf16[128,3840]{1,0:T(8,128)(2,1)S(1)} %get-tuple-element.94), channel_id=1, source_target_pairs={{0,1},{1,0},{2,3},{3,2},{4,5},{5,4},{6,7},{7,6},{8,9},{9,8},{10,11... | collective-permute-start | bytes 2949128 | tf_op jit(solution)/shard_map/ppermute | solution.py:65
  45.7 11.1 %collective-permute-start.9 = (bf16[64,3840]{1,0:T(8,128)(2,1)S(1)}, bf16[64,3840]{1,0:T(8,128)(2,1)S(1)}, u32[]{:S(2)}, u32[]{:S(2)}) collective-permute-start(bf16[64,3840]{1,0:T(8,128)(2,1)S(1)} %slice.292), channel_id=1, source_target_pairs={{0,4},{1,13},{4,0},{5,9},{8,12},{9,5},{12,8},{13,1},{16,20},{17,29... | collective-permute-start | bytes 1474568 | tf_op jit(solution)/shard_map/ppermute | solution.py:65
  48.4 8.9 %collective-permute-start.10 = (bf16[64,3840]{1,0:T(8,128)(2,1)S(1)}, bf16[64,3840]{1,0:T(8,128)(2,1)S(1)}, u32[]{:S(2)}, u32[]{:S(2)}) collective-permute-start(bf16[64,3840]{1,0:T(8,128)(2,1)S(1)} %slice.291), channel_id=1, source_target_pairs={{0,32},{1,97},{4,36},{5,101},{8,40},{9,105},{12,44},{13,109},{16,4... | collective-permute-start | bytes 1474568 | tf_op jit(solution)/shard_map/ppermute | solution.py:65
  48.6 8.2 %collective-permute-start.11 = (bf16[64,3328]{1,0:T(8,128)(2,1)S(1)}, bf16[64,3328]{1,0:T(8,128)(2,1)S(1)}, u32[]{:S(2)}, u32[]{:S(2)}) collective-permute-start(bf16[64,3328]{1,0:T(8,128)(2,1)S(1)} %slice.293), channel_id=1, source_target_pairs={{0,16},{1,19},{4,20},{5,23},{8,24},{9,27},{12,28},{13,31},{16,0},{... | collective-permute-start | bytes 1277960 | tf_op jit(solution)/shard_map/ppermute | solution.py:65
  57.7 6.9 %collective-permute-start.12 = (bf16[32,3840]{1,0:T(8,128)(2,1)S(1)}, bf16[32,3840]{1,0:T(8,128)(2,1)S(1)}, u32[]{:S(2)}, u32[]{:S(2)}) collective-permute-start(bf16[32,3840]{1,0:T(8,128)(2,1)S(1)} %slice.295), channel_id=1, source_target_pairs={{0,16},{1,19},{4,20},{5,23},{8,24},{9,27},{12,28},{13,31},{16,0},{... | collective-permute-start | bytes 737288 | tf_op jit(solution)/shard_map/ppermute | solution.py:65
  58.6 6.3 %collective-permute-start.13 = (bf16[32,3840]{1,0:T(8,128)(2,1)S(1)}, bf16[32,3840]{1,0:T(8,128)(2,1)S(1)}, u32[]{:S(2)}, u32[]{:S(2)}) collective-permute-start(bf16[32,3840]{1,0:T(8,128)(2,1)S(1)} %slice.294), channel_id=1, source_target_pairs={{0,4},{1,13},{4,0},{5,9},{8,12},{9,5},{12,8},{13,1},{16,20},{17,29... | collective-permute-start | bytes 737288 | tf_op jit(solution)/shard_map/ppermute | solution.py:65
  58.7 5.9 %collective-permute-start.14 = (bf16[32,3328]{1,0:T(8,128)(2,1)S(1)}, bf16[32,3328]{1,0:T(8,128)(2,1)S(1)}, u32[]{:S(2)}, u32[]{:S(2)}) collective-permute-start(bf16[32,3328]{1,0:T(8,128)(2,1)S(1)} %slice.296), channel_id=1, source_target_pairs={{0,32},{1,97},{4,36},{5,101},{8,40},{9,105},{12,44},{13,109},{16,4... | collective-permute-start | bytes 638984 | tf_op jit(solution)/shard_map/ppermute | solution.py:65
  65.2 11.0 %copy-start.3 = (f32[4,11008]{1,0:T(4,128)S(1)}, f32[4,11008]{1,0:T(4,128)}, u32[]{:S(2)}) copy-start(f32[4,11008]{1,0:T(4,128)} %param.8) | copy-start | bytes 528388
  65.2 11.0 %copy-start.4 = (f32[4,11008]{1,0:T(4,128)S(1)}, f32[4,11008]{1,0:T(4,128)}, u32[]{:S(2)}) copy-start(f32[4,11008]{1,0:T(4,128)} %param.9) | copy-start | bytes 528388
  88.0 10.0 %collective-permute-start.15 = (bf16[32,3840]{1,0:T(8,128)(2,1)S(1)}, bf16[32,3840]{1,0:T(8,128)(2,1)S(1)}, u32[]{:S(2)}, u32[]{:S(2)}) collective-permute-start(bf16[32,3840]{1,0:T(8,128)(2,1)S(1)} %get-tuple-element.70), channel_id=1, source_target_pairs={{0,16},{1,19},{4,20},{5,23},{8,24},{9,27},{12,28},{13,31},{16,0},{... | collective-permute-start | bytes 737288 | tf_op jit(solution)/shard_map/ppermute | solution.py:65
  89.2 8.9 %collective-permute-start.16 = (bf16[32,3840]{1,0:T(8,128)(2,1)S(1)}, bf16[32,3840]{1,0:T(8,128)(2,1)S(1)}, u32[]{:S(2)}, u32[]{:S(2)}) collective-permute-start(bf16[32,3840]{1,0:T(8,128)(2,1)S(1)} %get-tuple-element.71), channel_id=1, source_target_pairs={{0,4},{1,13},{4,0},{5,9},{8,12},{9,5},{12,8},{13,1},{16,20},{17,29... | collective-permute-start | bytes 737288 | tf_op jit(solution)/shard_map/ppermute | solution.py:65
  91.8 6.3 %collective-permute-start.17 = (bf16[32,3328]{1,0:T(8,128)(2,1)S(1)}, bf16[32,3328]{1,0:T(8,128)(2,1)S(1)}, u32[]{:S(2)}, u32[]{:S(2)}) collective-permute-start(bf16[32,3328]{1,0:T(8,128)(2,1)S(1)} %slice.242), channel_id=1, source_target_pairs={{0,32},{1,97},{4,36},{5,101},{8,40},{9,105},{12,44},{13,109},{16,4... | collective-permute-start | bytes 638984 | tf_op jit(solution)/shard_map/ppermute | solution.py:65
  98.1 12.0 %collective-permute-start.18 = (bf16[64,3840]{1,0:T(8,128)(2,1)S(1)}, bf16[64,3840]{1,0:T(8,128)(2,1)S(1)}, u32[]{:S(2)}, u32[]{:S(2)}) collective-permute-start(bf16[64,3840]{1,0:T(8,128)(2,1)S(1)} %pad_maximum_fusion.4), channel_id=1, source_target_pairs={{0,4},{1,13},{4,0},{5,9},{8,12},{9,5},{12,8},{13,1},{16,20},{17,29... | collective-permute-start | bytes 1474568 | tf_op jit(solution)/shard_map/ppermute | solution.py:65
  100.6 9.5 %collective-permute-start.19 = (bf16[64,3840]{1,0:T(8,128)(2,1)S(1)}, bf16[64,3840]{1,0:T(8,128)(2,1)S(1)}, u32[]{:S(2)}, u32[]{:S(2)}) collective-permute-start(bf16[64,3840]{1,0:T(8,128)(2,1)S(1)} %pad_maximum_fusion.5), channel_id=1, source_target_pairs={{0,32},{1,97},{4,36},{5,101},{8,40},{9,105},{12,44},{13,109},{16,4... | collective-permute-start | bytes 1474568 | tf_op jit(solution)/shard_map/ppermute | solution.py:65
  101.9 8.2 %collective-permute-start.20 = (bf16[64,3328]{1,0:T(8,128)(2,1)S(1)}, bf16[64,3328]{1,0:T(8,128)(2,1)S(1)}, u32[]{:S(2)}, u32[]{:S(2)}) collective-permute-start(bf16[64,3328]{1,0:T(8,128)(2,1)S(1)} %pad_maximum_fusion.6), channel_id=1, source_target_pairs={{0,16},{1,19},{4,20},{5,23},{8,24},{9,27},{12,28},{13,31},{16,0},{... | collective-permute-start | bytes 1277960 | tf_op jit(solution)/shard_map/ppermute | solution.py:65
  110.3 25.6 %collective-permute-start.21 = (bf16[128,3840]{1,0:T(8,128)(2,1)S(1)}, bf16[128,3840]{1,0:T(8,128)(2,1)S(1)}, u32[]{:S(2)}, u32[]{:S(2)}) collective-permute-start(bf16[128,3840]{1,0:T(8,128)(2,1)S(1)} %pad_maximum_fusion.refs_0_), channel_id=1, source_target_pairs={{0,32},{1,97},{4,36},{5,101},{8,40},{9,105},{12,44},{13,109},{16,4... | collective-permute-start | bytes 2949128 | tf_op jit(solution)/shard_map/ppermute | solution.py:65
  111.8 24.2 %collective-permute-start.22 = (bf16[128,3840]{1,0:T(8,128)(2,1)S(1)}, bf16[128,3840]{1,0:T(8,128)(2,1)S(1)}, u32[]{:S(2)}, u32[]{:S(2)}) collective-permute-start(bf16[128,3840]{1,0:T(8,128)(2,1)S(1)} %pad_maximum_fusion.1.refs_1_), channel_id=1, source_target_pairs={{0,16},{1,19},{4,20},{5,23},{8,24},{9,27},{12,28},{13,31},{16,0},{... | collective-permute-start | bytes 2949128 | tf_op jit(solution)/shard_map/ppermute | solution.py:65
  113.2 12.8 %collective-permute-start.23 = (bf16[128,3328]{1,0:T(8,128)(2,1)S(1)}, bf16[128,3328]{1,0:T(8,128)(2,1)S(1)}, u32[]{:S(2)}, u32[]{:S(2)}) collective-permute-start(bf16[128,3328]{1,0:T(8,128)(2,1)S(1)} %pad_maximum_fusion.2.refs_2_), channel_id=1, source_target_pairs={{0,4},{1,13},{4,0},{5,9},{8,12},{9,5},{12,8},{13,1},{16,20},{17,29... | collective-permute-start | bytes 2555912 | tf_op jit(solution)/shard_map/ppermute | solution.py:65
  114.5 22.0 %collective-permute-start.29 = (bf16[128,3328]{1,0:T(8,128)(2,1)S(1)}, bf16[128,3328]{1,0:T(8,128)(2,1)S(1)}, u32[]{:S(2)}, u32[]{:S(2)}) collective-permute-start(bf16[128,3328]{1,0:T(8,128)(2,1)S(1)} %pad_maximum_fusion.2.refs_2_), channel_id=1, source_target_pairs={{0,1},{1,0},{2,3},{3,2},{4,5},{5,4},{6,7},{7,6},{8,9},{9,8},{10,11... | collective-permute-start | bytes 2555912 | tf_op jit(solution)/shard_map/ppermute | solution.py:65
  123.6 13.0 %collective-permute-start.28 = (bf16[128,3840]{1,0:T(8,128)(2,1)S(1)}, bf16[128,3840]{1,0:T(8,128)(2,1)S(1)}, u32[]{:S(2)}, u32[]{:S(2)}) collective-permute-start(bf16[128,3840]{1,0:T(8,128)(2,1)S(1)} %pad_maximum_fusion.1.refs_1_), channel_id=1, source_target_pairs={{0,1},{1,0},{2,3},{3,2},{4,5},{5,4},{6,7},{7,6},{8,9},{9,8},{10,11... | collective-permute-start | bytes 2949128 | tf_op jit(solution)/shard_map/ppermute | solution.py:65
  126.0 12.2 %collective-permute-start.27 = (bf16[128,3840]{1,0:T(8,128)(2,1)S(1)}, bf16[128,3840]{1,0:T(8,128)(2,1)S(1)}, u32[]{:S(2)}, u32[]{:S(2)}) collective-permute-start(bf16[128,3840]{1,0:T(8,128)(2,1)S(1)} %pad_maximum_fusion.refs_0_), channel_id=1, source_target_pairs={{0,1},{1,0},{2,3},{3,2},{4,5},{5,4},{6,7},{7,6},{8,9},{9,8},{10,11... | collective-permute-start | bytes 2949128 | tf_op jit(solution)/shard_map/ppermute | solution.py:65
  136.0 6.2 %collective-permute-start.24 = (bf16[128,3840]{1,0:T(8,128)(2,1)S(1)}, bf16[128,3840]{1,0:T(8,128)(2,1)S(1)}, u32[]{:S(2)}, u32[]{:S(2)}) collective-permute-start(bf16[128,3840]{1,0:T(8,128)(2,1)S(1)} %collective-permute-done.21.refs_0_), channel_id=1, source_target_pairs={{0,1},{1,0},{2,3},{3,2},{4,5},{5,4},{6,7},{7,6},{8,9},{9,8},{10,11... | collective-permute-start | bytes 2949128 | tf_op jit(solution)/shard_map/ppermute | solution.py:65
  136.1 6.1 %collective-permute-start.25 = (bf16[128,3840]{1,0:T(8,128)(2,1)S(1)}, bf16[128,3840]{1,0:T(8,128)(2,1)S(1)}, u32[]{:S(2)}, u32[]{:S(2)}) collective-permute-start(bf16[128,3840]{1,0:T(8,128)(2,1)S(1)} %collective-permute-done.22.refs_1_), channel_id=1, source_target_pairs={{0,1},{1,0},{2,3},{3,2},{4,5},{5,4},{6,7},{7,6},{8,9},{9,8},{10,11... | collective-permute-start | bytes 2949128 | tf_op jit(solution)/shard_map/ppermute | solution.py:65
  136.5 5.7 %collective-permute-start.26 = (bf16[128,3328]{1,0:T(8,128)(2,1)S(1)}, bf16[128,3328]{1,0:T(8,128)(2,1)S(1)}, u32[]{:S(2)}, u32[]{:S(2)}) collective-permute-start(bf16[128,3328]{1,0:T(8,128)(2,1)S(1)} %collective-permute-done.23.refs_2_), channel_id=1, source_target_pairs={{0,1},{1,0},{2,3},{3,2},{4,5},{5,4},{6,7},{7,6},{8,9},{9,8},{10,11... | collective-permute-start | bytes 2555912 | tf_op jit(solution)/shard_map/ppermute | solution.py:65
  (3 other events, 9.0 us)

commit v4 on v3

--- a/solution.py
+++ b/solution.py
@@ -86,13 +86,14 @@
     return linear(*there, core) * 4 + place % 4
 
 
-def project_kernel(tokens_ref, basis_ref, out_ref, total_ref):
+def project_kernel(at_ref, places_ref, tokens_ref, basis_ref, rows_ref, out_ref, own_rows_ref, total_ref):
     step = pl.program_id(0)
     product = jnp.dot(tokens_ref[...], basis_ref[...], preferred_element_type=jnp.float32)
 
     @pl.when(step == 0)
     def _():
         total_ref[...] = product
+        own_rows_ref[...] = rows_ref[...]
 
     @pl.when(step > 0)
     def _():
@@ -100,29 +101,46 @@
 
     @pl.when(step == pl.num_programs(0) - 1)
     def _():
-        out_ref[...] = total_ref[...].astype(jnp.bfloat16)
-
-
-def project(tokens, basis, depth=1024):
-    rows, width = tokens.shape[0], basis.shape[1]
+        projected = total_ref[...].astype(jnp.bfloat16)
+        for piece in range(3):
+            columns = slice(512 * piece, 512 * piece + 512)
+            picks = lax.broadcasted_iota(jnp.int32, (512, 512), 0) == places_ref[:, columns]
+            picks = jnp.where(picks, 1.0, 0.0).astype(jnp.bfloat16)
+            picked = jnp.dot(projected, picks, preferred_element_type=jnp.float32)
+            out_ref[:, columns] = picked.astype(jnp.bfloat16)
+
+
+def project(at, places, tokens, basis, depth=1024):
+    rows, rank, width = tokens.shape[0], basis.shape[1], places.shape[1]
     return pl.pallas_call(
         project_kernel,
-        grid=(basis.shape[0] // depth,),
-        in_specs=[
-            pl.BlockSpec((rows, depth), lambda k: (0, k)),
-            pl.BlockSpec((depth, width), lambda k: (k, 0)),
+        grid_spec=pltpu.PrefetchScalarGridSpec(
+            num_scalar_prefetch=1,
+            grid=(basis.shape[0] // depth,),
+            in_specs=[
+                pl.BlockSpec((1, width), lambda k, at: (0, 0)),
+                pl.BlockSpec((rows, depth), lambda k, at: (0, k)),
+                pl.BlockSpec((depth, rank), lambda k, at: (k, 0)),
+                pl.BlockSpec((128, rank), lambda k, at: (at[0], 0)),
+            ],
+            out_specs=[
+                pl.BlockSpec((rows, width), lambda k, at: (0, 0)),
+                pl.BlockSpec((128, rank), lambda k, at: (0, 0)),
+            ],
+            scratch_shapes=[pltpu.VMEM((rows, rank), jnp.float32)],
+        ),
+        out_shape=[
+            jax.ShapeDtypeStruct((rows, width), jnp.bfloat16),
+            jax.ShapeDtypeStruct((128, rank), jnp.bfloat16),
         ],
-        out_specs=pl.BlockSpec((rows, width), lambda k: (0, 0)),
-        out_shape=jax.ShapeDtypeStruct((rows, width), jnp.bfloat16),
-        scratch_shapes=[pltpu.VMEM((rows, width), jnp.float32)],
         cost_estimate=pl.CostEstimate(
-            flops=2 * rows * basis.shape[0] * width,
-            bytes_accessed=2 * (rows + width) * basis.shape[0],
+            flops=2 * rows * (basis.shape[0] + width) * rank,
+            bytes_accessed=2 * (rows + rank) * basis.shape[0],
             transcendentals=0,
         ),
-        compiler_params=pltpu.CompilerParams(vmem_limit_bytes=8 * 1024 * 1024),
+        compiler_params=pltpu.CompilerParams(vmem_limit_bytes=12 * 1024 * 1024),
         name="project",
-    )(tokens, basis)
+    )(at, places, tokens, basis, basis)
 
 
 def expand_kernel(basis_ref, *refs):
@@ -159,6 +177,36 @@
     )(basis_rows, *own, *other, *early)
 
 
+def late_kernel(basis_ref, own_ref, other_ref, early_ref, *refs):
+    low = jnp.concatenate([own_ref[...], other_ref[...]], axis=0)
+    product = jnp.dot(basis_ref[...], low, preferred_element_type=jnp.float32)
+    refs[-1][...] = -galore_scale * (early_ref[...] + product)
+
+
+def expand_late(piece, basis_rows, own, other, early, *done):
+    rows, half, (start, size) = basis_rows.shape[0], own.shape[0], PIECES[piece]
+    step = WIDTH // 2
+    total = pl.BlockSpec((rows, step), lambda j: (0, start // step + j))
+    return pl.pallas_call(
+        late_kernel,
+        grid=(2,),
+        in_specs=[pl.BlockSpec((rows, 2 * half), lambda j: (0, piece))]
+        + [pl.BlockSpec((half, step), lambda j: (0, j))] * 2
+        + [total]
+        + [pl.BlockSpec(memory_space=pl.ANY)] * len(done),
+        out_specs=total,
+        out_shape=jax.ShapeDtypeStruct(early.shape, jnp.float32),
+        input_output_aliases={4: 0} if done else {},
+        cost_estimate=pl.CostEstimate(
+            flops=4 * rows * half * size,
+            bytes_accessed=(4 * half + 8 * rows) * size,
+            transcendentals=0,
+        ),
+        compiler_params=pltpu.CompilerParams(vmem_limit_bytes=16 * 1024 * 1024),
+        name="expand_late",
+    )(basis_rows, own, other, early, *done)
+
+
 def shards(tokens, grad_out, projection_basis, first_moment, second_moment):
     dp, outer = lax.axis_index("dp"), lax.axis_index("outer")
     f32, bf16 = jnp.float32, jnp.bfloat16
@@ -166,12 +214,7 @@
     places = jnp.concatenate([rank_order(bits, dp, outer) for bits in BITS])
     picks = (lax.broadcasted_iota(jnp.int32, (512, 1536), 0) == places[None, :]).astype(bf16)
 
-    projected = project(tokens, projection_basis)
-    projected = jnp.dot(projected, picks, preferred_element_type=f32).astype(bf16)
-
-    local_width = projection_basis.shape[0] // 32
-    basis_rows = lax.dynamic_slice_in_dim(projection_basis, dp * local_width, local_width, 0)
-    projected, basis_rows = lax.optimization_barrier((projected, basis_rows))
+    projected, basis_rows = project(dp.reshape(1), places[None, :], tokens, projection_basis)
 
     own, other = [], []
     for piece, (start, size) in enumerate(PIECES):
@@ -183,8 +226,11 @@
         ).astype(bf16)
         own.append(terms[:256])
         other.append(terms[256:])
-    sent = [o[128:].astype(f32) + send(t[128:], SWAP).astype(f32) for o, t in zip(own, other)]
-    held = [o[:128].astype(f32) + send(t[:128], SWAP).astype(f32) for o, t in zip(own, other)]
+    halves = [[send(t[128:], SWAP), send(t[:128], SWAP)] for t in other[:2]]
+    whole = send(other[2], SWAP)
+    halves.append([whole[128:], whole[:128]])
+    sent = [o[128:].astype(f32) + t[0].astype(f32) for o, t in zip(own, halves)]
+    held = [o[:128].astype(f32) + t[1].astype(f32) for o, t in zip(own, halves)]
     for level in range(3):
         got = send_pieces([s.astype(bf16) for s in sent], level)
         if level == 0:
@@ -215,7 +261,10 @@
         low = [jnp.concatenate([mine, theirs], axis=0) for mine, theirs in zip(low, got)]
     late = send_pieces(low, 0)
     early = expand(early_basis, low, [send(part, SWAP) for part in low])
-    weight_update = expand(late_basis, late, [send(part, SWAP) for part in late], early)
+    others, done = [send(part, SWAP) for part in late], ()
+    for piece in range(3):
+        done = (expand_late(piece, late_basis, late[piece], others[piece], early, *done),)
+    weight_update = done[0]
     return (weight_update, new_first, new_second)
 
 

time: 146 us -> 143 us (0.979)
  waiting for transfers between devices: 43 us -> 37.7 us
  Pallas kernels: 9.01 us -> 12.3 us
    pallas_call x1 -> x4, Pallas kernels: 3.57 us -> 10.5 us  [the longest x3 5.93 us: expand_late(): pl.pallas_call(late_kernel, grid=(2,), in_specs=[pl.BlockSpec((rows, 2 *...]
    ppermute x30 -> x29, waiting for transfers between devices: 43 us -> 37.7 us  [send(): return lax.ppermute(value, AXES, pairs)]
    pallas_call x2 -> x1, Pallas kernels: 5.44 us -> 1.79 us  [expand(): pl.pallas_call(expand_kernel, grid=(3,), in_specs=[pl.BlockSpec((rows, de...]
    ppermute x30 -> x29, starting transfers between devices: 52.9 us -> 53.7 us  [send(): return lax.ppermute(value, AXES, pairs)]
  transfers between devices with their start and end apart: 30 -> 29, of which waited for: 12 -> 10; matrix products, arithmetic and copies ran while one was open for 5% -> 4% of each run, Pallas kernels for 1% -> 4%
where the time goes in v4:
time: 143 us; the launch traced here: 142 us
  starting transfers between devices  53.7 us (38%)
  waiting for transfers between devices  37.7 us (26%)
  blocking collectives  20.7 us (14%)
  Pallas kernels  12.3 us (9%)
  matrix products  7.27 us (5%)
  local copies, waits for them, and re-layouts  5.68 us (4%)
  other arithmetic  3.95 us (3%)
    ppermute x29, starting transfers between devices, send(): return lax.ppermute(value, AXES, pairs)  53.7 us
    ppermute x29, waiting for transfers between devices, send(): return lax.ppermute(value, AXES, pairs)  37.7 us
    all_to_all x2, blocking collectives, swap_groups(): lax.all_to_all(value, AXES, 0, 0, axis_index_groups=groups(), tiled=True)  20.7 us
    dot_general x3, matrix products, shards(): lax.dot_general(projected[:, 512 * piece:512 * piece + 512], grad_out[:,...  6.52 us
    pallas_call x3, Pallas kernels, expand_late(): pl.pallas_call(late_kernel, grid=(2,), in_specs=[pl.BlockSpec((rows, 2 *...  5.93 us
    pallas_call x1, Pallas kernels, project(): pl.pallas_call(project_kernel, grid_spec=pltpu.PrefetchScalarGridSpec(num...  4.56 us
    unnamed x15, local copies, waits for them, and re-layouts  4.48 us
  transfers between devices with their start and end apart: 29, of which 10 were waited for; matrix products, arithmetic and copies ran while one was open for 4% of the time, Pallas kernels for 4%

profile of v4, /device:TPU:1, one launch (start us, length us, event | category | flops | bytes accessed | tf_op | source)
XLA Modules:
  0.0 142.4 jit_solution(169537774588573795)
XLA Ops:
  0.8 2.2 %copy-done = bf16[4096,512]{1,0:T(8,128)(2,1)S(1)} copy-done((bf16[4096,512]{1,0:T(8,128)(2,1)S(1)}, bf16[4096,512]{1,0:T(8,128)(2,1)}, u32[]{:S(2)}) %copy-start) | copy-done | bytes 4194328
  3.0 2.2 %copy-done.1 = bf16[512,4096]{1,0:T(8,128)(2,1)S(1)} copy-done((bf16[512,4096]{1,0:T(8,128)(2,1)S(1)}, bf16[512,4096]{1,0:T(8,128)(2,1)}, u32[]{:S(2)}) %copy-start.1) | copy-done | bytes 4194328
  5.2 4.6 %project.1 = (bf16[512,1536]{1,0:T(8,128)(2,1)S(1)}, bf16[128,512]{1,0:T(8,128)(2,1)S(1)}) custom-call(s32[1]{0:T(128)} %bitcast.at_ref, s32[1,1536]{1,0:T(1,128)S(1)} %broadcast_in_dim.4.places_ref, bf16[512,4096]{1,0:T(8,128)(2,1)S(1)} %copy-done.1, bf16[4096,512]{1,0:T(8,128)(2,1)S(1)} %copy-done, bf16[4096,512]{1,0:T(8,128)(2,1)S(1)} %copy-done), custom_call_target="tpu_custom_call" | custom-call | flops 2952790016 | bytes 8388608 | tf_op jit(solution)/shard_map/project/pallas_call | solution.py:115
  9.8 2.3 %convolution_convert_fusion.1 = bf16[512,3840]{1,0:T(8,128)(2,1)S(1)} fusion(bf16[512,11008]{1,0:T(8,128)(2,1)S(1)} %copy-done.2, bf16[512,1536]{1,0:T(8,128)(2,1)S(1)} %get-tuple-element.46), kind=kOutput, calls=%fused_computation.1 | convolution fusion | flops 2015232000 | bytes 8388608 | tf_op jit(solution)/shard_map/dot_general | solution.py:221
  13.7 2.0 %convolution_convert_fusion = bf16[512,3328]{1,0:T(8,128)(2,1)S(1)} fusion(bf16[512,11008]{1,0:T(8,128)(2,1)S(1)} %copy-done.2, bf16[512,1536]{1,0:T(8,128)(2,1)S(1)} %get-tuple-element.46), kind=kOutput, calls=%fused_computation | convolution fusion | flops 1746534400 | bytes 7340032 | tf_op jit(solution)/shard_map/dot_general | solution.py:221
  15.9 2.3 %convolution_convert_fusion.2 = bf16[512,3840]{1,0:T(8,128)(2,1)S(1)} fusion(bf16[512,11008]{1,0:T(8,128)(2,1)S(1)} %copy-done.2, bf16[512,1536]{1,0:T(8,128)(2,1)S(1)} %get-tuple-element.46), kind=kOutput, calls=%fused_computation.2 | convolution fusion | flops 2015232000 | bytes 8388608 | tf_op jit(solution)/shard_map/dot_general | solution.py:221
  21.5 2.6 %collective-permute-start.3 = (bf16[128,3840]{1,0:T(8,128)(2,1)S(1)}, bf16[128,3840]{1,0:T(8,128)(2,1)S(1)}, u32[]{:S(2)}, u32[]{:S(2)}) collective-permute-start(bf16[128,3840]{1,0:T(8,128)(2,1)S(1)} %add_convert_fusion.1), channel_id=1, source_target_pairs={{0,32},{1,97},{4,36},{5,101},{8,40},{9,105},{12,44},{13,109},{16,4... | collective-permute-start | bytes 2949128 | tf_op jit(solution)/shard_map/ppermute | solution.py:65
  24.2 2.7 %collective-permute-start.4 = (bf16[128,3840]{1,0:T(8,128)(2,1)S(1)}, bf16[128,3840]{1,0:T(8,128)(2,1)S(1)}, u32[]{:S(2)}, u32[]{:S(2)}) collective-permute-start(bf16[128,3840]{1,0:T(8,128)(2,1)S(1)} %add_convert_fusion), channel_id=1, source_target_pairs={{0,16},{1,19},{4,20},{5,23},{8,24},{9,27},{12,28},{13,31},{16,0},{... | collective-permute-start | bytes 2949128 | tf_op jit(solution)/shard_map/ppermute | solution.py:65
  26.9 4.0 %collective-permute-start.5 = (bf16[128,3328]{1,0:T(8,128)(2,1)S(1)}, bf16[128,3328]{1,0:T(8,128)(2,1)S(1)}, u32[]{:S(2)}, u32[]{:S(2)}) collective-permute-start(bf16[128,3328]{1,0:T(8,128)(2,1)S(1)} %add_convert_fusion.2), channel_id=1, source_target_pairs={{0,4},{1,13},{4,0},{5,9},{8,12},{9,5},{12,8},{13,1},{16,20},{17,29... | collective-permute-start | bytes 2555912 | tf_op jit(solution)/shard_map/ppermute | solution.py:65
  31.0 10.0 %collective-permute-done.5 = bf16[128,3328]{1,0:T(8,128)(2,1)S(1)} collective-permute-done((bf16[128,3328]{1,0:T(8,128)(2,1)S(1)}, bf16[128,3328]{1,0:T(8,128)(2,1)S(1)}, u32[]{:S(2)}, u32[]{:S(2)}) %collective-permute-start.5) | collective-permute-done | bytes 852000 | tf_op jit(solution)/shard_map/ppermute | solution.py:65
  42.2 2.8 %collective-permute-start.8 = (bf16[64,3840]{1,0:T(8,128)(2,1)S(1)}, bf16[64,3840]{1,0:T(8,128)(2,1)S(1)}, u32[]{:S(2)}, u32[]{:S(2)}) collective-permute-start(bf16[64,3840]{1,0:T(8,128)(2,1)S(1)} %slice.296), channel_id=1, source_target_pairs={{0,4},{1,13},{4,0},{5,9},{8,12},{9,5},{12,8},{13,1},{16,20},{17,29... | collective-permute-start | bytes 1474568 | tf_op jit(solution)/shard_map/ppermute | solution.py:65
  46.2 7.1 %collective-permute-done.10 = bf16[64,3328]{1,0:T(8,128)(2,1)S(1)} collective-permute-done((bf16[64,3328]{1,0:T(8,128)(2,1)S(1)}, bf16[64,3328]{1,0:T(8,128)(2,1)S(1)}, u32[]{:S(2)}, u32[]{:S(2)}) %collective-permute-start.10) | collective-permute-done | bytes 426016 | tf_op jit(solution)/shard_map/ppermute | solution.py:65
  55.5 2.0 %collective-permute-start.13 = (bf16[32,3328]{1,0:T(8,128)(2,1)S(1)}, bf16[32,3328]{1,0:T(8,128)(2,1)S(1)}, u32[]{:S(2)}, u32[]{:S(2)}) collective-permute-start(bf16[32,3328]{1,0:T(8,128)(2,1)S(1)} %slice.300), channel_id=1, source_target_pairs={{0,32},{1,97},{4,36},{5,101},{8,40},{9,105},{12,44},{13,109},{16,4... | collective-permute-start | bytes 638984 | tf_op jit(solution)/shard_map/ppermute | solution.py:65
  57.5 3.9 %collective-permute-done.13 = bf16[32,3328]{1,0:T(8,128)(2,1)S(1)} collective-permute-done((bf16[32,3328]{1,0:T(8,128)(2,1)S(1)}, bf16[32,3328]{1,0:T(8,128)(2,1)S(1)}, u32[]{:S(2)}, u32[]{:S(2)}) %collective-permute-start.13) | collective-permute-done | bytes 213024 | tf_op jit(solution)/shard_map/ppermute | solution.py:65
  62.3 10.4 %all_to_all.10 = bf16[8,4,11008]{2,1,0:T(4,128)(2,1)S(1)} all-to-all(bf16[8,4,11008]{2,1,0:T(4,128)(2,1)S(1)} %pad_maximum_fusion.3), channel_id=1, replica_groups={{0,12,18,30,96,108,114,126},{1,5,17,21,33,37,49,53},{4,8,22,26,100,104,..., dimensions={0} | all-to-all | bytes 1409024 | tf_op jit(solution)/shard_map/all_to_all | solution.py:61
  74.2 10.4 %all_to_all.11 = bf16[8,4,11008]{2,1,0:T(4,128)(2,1)S(1)} all-to-all(bf16[8,4,11008]{2,1,0:T(4,128)(2,1)S(1)} %broadcast_in_dim.5), channel_id=1, replica_groups={{0,12,18,30,96,108,114,126},{1,5,17,21,33,37,49,53},{4,8,22,26,100,104,..., dimensions={0} | all-to-all | bytes 1409024 | tf_op jit(solution)/shard_map/all_to_all | solution.py:61
  85.5 2.7 %collective-permute-start.15 = (bf16[32,3840]{1,0:T(8,128)(2,1)S(1)}, bf16[32,3840]{1,0:T(8,128)(2,1)S(1)}, u32[]{:S(2)}, u32[]{:S(2)}) collective-permute-start(bf16[32,3840]{1,0:T(8,128)(2,1)S(1)} %get-tuple-element.71), channel_id=1, source_target_pairs={{0,4},{1,13},{4,0},{5,9},{8,12},{9,5},{12,8},{13,1},{16,20},{17,29... | collective-permute-start | bytes 737288 | tf_op jit(solution)/shard_map/ppermute | solution.py:65
  88.2 1.7 %collective-permute-start.16 = (bf16[32,3328]{1,0:T(8,128)(2,1)S(1)}, bf16[32,3328]{1,0:T(8,128)(2,1)S(1)}, u32[]{:S(2)}, u32[]{:S(2)}) collective-permute-start(bf16[32,3328]{1,0:T(8,128)(2,1)S(1)} %slice.244), channel_id=1, source_target_pairs={{0,32},{1,97},{4,36},{5,101},{8,40},{9,105},{12,44},{13,109},{16,4... | collective-permute-start | bytes 638984 | tf_op jit(solution)/shard_map/ppermute | solution.py:65
  89.9 4.6 %collective-permute-done.16 = bf16[32,3328]{1,0:T(8,128)(2,1)S(1)} collective-permute-done((bf16[32,3328]{1,0:T(8,128)(2,1)S(1)}, bf16[32,3328]{1,0:T(8,128)(2,1)S(1)}, u32[]{:S(2)}, u32[]{:S(2)}) %collective-permute-start.16) | collective-permute-done | bytes 213024 | tf_op jit(solution)/shard_map/ppermute | solution.py:65
  94.7 2.3 %collective-permute-start.17 = (bf16[64,3840]{1,0:T(8,128)(2,1)S(1)}, bf16[64,3840]{1,0:T(8,128)(2,1)S(1)}, u32[]{:S(2)}, u32[]{:S(2)}) collective-permute-start(bf16[64,3840]{1,0:T(8,128)(2,1)S(1)} %pad_maximum_fusion.4), channel_id=1, source_target_pairs={{0,4},{1,13},{4,0},{5,9},{8,12},{9,5},{12,8},{13,1},{16,20},{17,29... | collective-permute-start | bytes 1474568 | tf_op jit(solution)/shard_map/ppermute | solution.py:65
  98.2 1.6 %collective-permute-start.19 = (bf16[64,3328]{1,0:T(8,128)(2,1)S(1)}, bf16[64,3328]{1,0:T(8,128)(2,1)S(1)}, u32[]{:S(2)}, u32[]{:S(2)}) collective-permute-start(bf16[64,3328]{1,0:T(8,128)(2,1)S(1)} %pad_maximum_fusion.6), channel_id=1, source_target_pairs={{0,16},{1,19},{4,20},{5,23},{8,24},{9,27},{12,28},{13,31},{16,0},{... | collective-permute-start | bytes 1277960 | tf_op jit(solution)/shard_map/ppermute | solution.py:65
  99.8 6.6 %collective-permute-done.19 = bf16[64,3328]{1,0:T(8,128)(2,1)S(1)} collective-permute-done((bf16[64,3328]{1,0:T(8,128)(2,1)S(1)}, bf16[64,3328]{1,0:T(8,128)(2,1)S(1)}, u32[]{:S(2)}, u32[]{:S(2)}) %collective-permute-start.19) | collective-permute-done | bytes 426016 | tf_op jit(solution)/shard_map/ppermute | solution.py:65
  106.6 1.5 %collective-permute-start.20 = (bf16[128,3840]{1,0:T(8,128)(2,1)S(1)}, bf16[128,3840]{1,0:T(8,128)(2,1)S(1)}, u32[]{:S(2)}, u32[]{:S(2)}) collective-permute-start(bf16[128,3840]{1,0:T(8,128)(2,1)S(1)} %pad_maximum_fusion.refs_0_), channel_id=1, source_target_pairs={{0,32},{1,97},{4,36},{5,101},{8,40},{9,105},{12,44},{13,109},{16,4... | collective-permute-start | bytes 2949128 | tf_op jit(solution)/shard_map/ppermute | solution.py:65
  108.1 1.7 %collective-permute-start.21 = (bf16[128,3840]{1,0:T(8,128)(2,1)S(1)}, bf16[128,3840]{1,0:T(8,128)(2,1)S(1)}, u32[]{:S(2)}, u32[]{:S(2)}) collective-permute-start(bf16[128,3840]{1,0:T(8,128)(2,1)S(1)} %pad_maximum_fusion.1.refs_1_), channel_id=1, source_target_pairs={{0,16},{1,19},{4,20},{5,23},{8,24},{9,27},{12,28},{13,31},{16,0},{... | collective-permute-start | bytes 2949128 | tf_op jit(solution)/shard_map/ppermute | solution.py:65
  111.1 9.0 %collective-permute-start.26 = (bf16[128,3328]{1,0:T(8,128)(2,1)S(1)}, bf16[128,3328]{1,0:T(8,128)(2,1)S(1)}, u32[]{:S(2)}, u32[]{:S(2)}) collective-permute-start(bf16[128,3328]{1,0:T(8,128)(2,1)S(1)} %pad_maximum_fusion.2.refs_2_), channel_id=1, source_target_pairs={{0,1},{1,0},{2,3},{3,2},{4,5},{5,4},{6,7},{7,6},{8,9},{9,8},{10,11... | collective-permute-start | bytes 2555912 | tf_op jit(solution)/shard_map/ppermute | solution.py:65
  120.1 2.5 %collective-permute-done.22.own_ref = bf16[128,3328]{1,0:T(8,128)(2,1)S(1)} collective-permute-done((bf16[128,3328]{1,0:T(8,128)(2,1)S(1)}, bf16[128,3328]{1,0:T(8,128)(2,1)S(1)}, u32[]{:S(2)}, u32[]{:S(2)}) %collective-permute-start.22) | collective-permute-done | bytes 852000 | tf_op jit(solution)/shard_map/ppermute | solution.py:65
  122.6 9.9 %collective-permute-start.24 = (bf16[128,3840]{1,0:T(8,128)(2,1)S(1)}, bf16[128,3840]{1,0:T(8,128)(2,1)S(1)}, u32[]{:S(2)}, u32[]{:S(2)}) collective-permute-start(bf16[128,3840]{1,0:T(8,128)(2,1)S(1)} %pad_maximum_fusion.refs_0_), channel_id=1, source_target_pairs={{0,1},{1,0},{2,3},{3,2},{4,5},{5,4},{6,7},{7,6},{8,9},{9,8},{10,11... | collective-permute-start | bytes 2949128 | tf_op jit(solution)/shard_map/ppermute | solution.py:65
  133.0 1.6 %collective-permute-done.24.refs_3_ = bf16[128,3840]{1,0:T(8,128)(2,1)S(1)} collective-permute-done((bf16[128,3840]{1,0:T(8,128)(2,1)S(1)}, bf16[128,3840]{1,0:T(8,128)(2,1)S(1)}, u32[]{:S(2)}, u32[]{:S(2)}) %collective-permute-start.24) | collective-permute-done | bytes 983072 | tf_op jit(solution)/shard_map/ppermute | solution.py:65
  134.6 1.8 %expand.1.early_ref = f32[128,11008]{1,0:T(8,128)S(1)} custom-call(bf16[128,768]{1,0:T(8,128)(2,1)S(1)} %get-tuple-element.86.basis_ref, bf16[128,3840]{1,0:T(8,128)(2,1)S(1)} %pad_maximum_fusion.refs_0_, bf16[128,3840]{1,0:T(8,128)(2,1)S(1)} %pad_maximum_fusion.1.refs_1_, bf16[128,3328]{1,0:T(8,128)(2,1)S(1)} %pad_maximum_fusion.2.refs_2_, ...), custom_call_target="tpu_custom_call" | custom-call | flops 721420288 | bytes 11272192 | tf_op jit(solution)/shard_map/expand/pallas_call | solution.py:162
  136.4 2.0 %expand_late.3.refs_0_ = f32[128,11008]{1,0:T(8,128)} custom-call(bf16[128,768]{1,0:T(8,128)(2,1)S(1)} %get-tuple-element.54.basis_ref, bf16[128,3840]{1,0:T(8,128)(2,1)S(1)} %collective-permute-done.20.own_ref, bf16[128,3840]{1,0:T(8,128)(2,1)S(1)} %collective-permute-done.28.other_ref, f32[128,11008]{1,0:T(8,128)S(1)} %expand.1.early_ref), custom_call_target="tpu_custom_call" | custom-call | flops 251658240 | bytes 5898240 | tf_op jit(solution)/shard_map/expand_late/pallas_call | solution.py:190
  138.4 2.0 %expand_late.4.refs_0_ = f32[128,11008]{1,0:T(8,128)} custom-call(bf16[128,768]{1,0:T(8,128)(2,1)S(1)} %get-tuple-element.54.basis_ref, bf16[128,3840]{1,0:T(8,128)(2,1)S(1)} %collective-permute-done.21.own_ref, bf16[128,3840]{1,0:T(8,128)(2,1)S(1)} %collective-permute-done.27.other_ref, ...), custom_call_target="tpu_custom_call", output_to_operand_aliasing={{}: (4, {})} | custom-call | flops 251658240 | bytes 5898240 | tf_op jit(solution)/shard_map/expand_late/pallas_call | solution.py:190
  140.4 2.0 %expand_late.5 = f32[128,11008]{1,0:T(8,128)} custom-call(bf16[128,768]{1,0:T(8,128)(2,1)S(1)} %get-tuple-element.54.basis_ref, bf16[128,3328]{1,0:T(8,128)(2,1)S(1)} %collective-permute-done.22.own_ref, bf16[128,3328]{1,0:T(8,128)(2,1)S(1)} %collective-permute-done.23.other_ref, f32[128,11008]{1,0:T(8,128)S(1)} %expand.1.early_ref, ...), custom_call_target="tpu_custom_call", output_to_operand_aliasing={{}: (4, {})} | custom-call | flops 218103808 | bytes 5111808 | tf_op jit(solution)/shard_map/expand_late/pallas_call | solution.py:190
  (94 shorter events, 16.6 us)
Async XLA Ops:
  5.2 4.6 %copy-start.2 = (bf16[512,11008]{1,0:T(8,128)(2,1)S(1)}, bf16[512,11008]{1,0:T(8,128)(2,1)}, u32[]{:S(2)}) copy-start(bf16[512,11008]{1,0:T(8,128)(2,1)} %param.6) | copy-start | bytes 33816580
  12.2 8.0 %collective-permute-start.1 = (bf16[128,3840]{1,0:T(8,128)(2,1)S(1)}, bf16[128,3840]{1,0:T(8,128)(2,1)S(1)}, u32[]{:S(2)}, u32[]{:S(2)}) collective-permute-start(bf16[128,3840]{1,0:T(8,128)(2,1)S(1)} %get-tuple-element.93), channel_id=1, source_target_pairs={{0,1},{1,0},{2,3},{3,2},{4,5},{5,4},{6,7},{7,6},{8,9},{9,8},{10,11... | collective-permute-start | bytes 2949128 | tf_op jit(solution)/shard_map/ppermute | solution.py:65
  15.8 5.5 %collective-permute-start.2 = (bf16[256,3328]{1,0:T(8,128)(2,1)S(1)}, bf16[256,3328]{1,0:T(8,128)(2,1)S(1)}, u32[]{:S(2)}, u32[]{:S(2)}) collective-permute-start(bf16[256,3328]{1,0:T(8,128)(2,1)S(1)} %slice.210), channel_id=1, source_target_pairs={{0,1},{1,0},{2,3},{3,2},{4,5},{5,4},{6,7},{7,6},{8,9},{9,8},{10,11... | collective-permute-start | bytes 5111816 | tf_op jit(solution)/shard_map/ppermute | solution.py:65
  18.3 2.8 %collective-permute-start = (bf16[128,3840]{1,0:T(8,128)(2,1)S(1)}, bf16[128,3840]{1,0:T(8,128)(2,1)S(1)}, u32[]{:S(2)}, u32[]{:S(2)}) collective-permute-start(bf16[128,3840]{1,0:T(8,128)(2,1)S(1)} %get-tuple-element.95), channel_id=1, source_target_pairs={{0,1},{1,0},{2,3},{3,2},{4,5},{5,4},{6,7},{7,6},{8,9},{9,8},{10,11... | collective-permute-start | bytes 2949128 | tf_op jit(solution)/shard_map/ppermute | solution.py:65
  18.9 22.1 %collective-permute-start.7 = (bf16[128,3840]{1,0:T(8,128)(2,1)S(1)}, bf16[128,3840]{1,0:T(8,128)(2,1)S(1)}, u32[]{:S(2)}, u32[]{:S(2)}) collective-permute-start(bf16[128,3840]{1,0:T(8,128)(2,1)S(1)} %get-tuple-element.92), channel_id=1, source_target_pairs={{0,1},{1,0},{2,3},{3,2},{4,5},{5,4},{6,7},{7,6},{8,9},{9,8},{10,11... | collective-permute-start | bytes 2949128 | tf_op jit(solution)/shard_map/ppermute | solution.py:65
  19.0 22.4 %collective-permute-start.6 = (bf16[128,3840]{1,0:T(8,128)(2,1)S(1)}, bf16[128,3840]{1,0:T(8,128)(2,1)S(1)}, u32[]{:S(2)}, u32[]{:S(2)}) collective-permute-start(bf16[128,3840]{1,0:T(8,128)(2,1)S(1)} %get-tuple-element.94), channel_id=1, source_target_pairs={{0,1},{1,0},{2,3},{3,2},{4,5},{5,4},{6,7},{7,6},{8,9},{9,8},{10,11... | collective-permute-start | bytes 2949128 | tf_op jit(solution)/shard_map/ppermute | solution.py:65
  21.5 19.5 %collective-permute-start.3 = (bf16[128,3840]{1,0:T(8,128)(2,1)S(1)}, bf16[128,3840]{1,0:T(8,128)(2,1)S(1)}, u32[]{:S(2)}, u32[]{:S(2)}) collective-permute-start(bf16[128,3840]{1,0:T(8,128)(2,1)S(1)} %add_convert_fusion.1), channel_id=1, source_target_pairs={{0,32},{1,97},{4,36},{5,101},{8,40},{9,105},{12,44},{13,109},{16,4... | collective-permute-start | bytes 2949128 | tf_op jit(solution)/shard_map/ppermute | solution.py:65
  24.2 16.9 %collective-permute-start.4 = (bf16[128,3840]{1,0:T(8,128)(2,1)S(1)}, bf16[128,3840]{1,0:T(8,128)(2,1)S(1)}, u32[]{:S(2)}, u32[]{:S(2)}) collective-permute-start(bf16[128,3840]{1,0:T(8,128)(2,1)S(1)} %add_convert_fusion), channel_id=1, source_target_pairs={{0,16},{1,19},{4,20},{5,23},{8,24},{9,27},{12,28},{13,31},{16,0},{... | collective-permute-start | bytes 2949128 | tf_op jit(solution)/shard_map/ppermute | solution.py:65
  26.9 14.1 %collective-permute-start.5 = (bf16[128,3328]{1,0:T(8,128)(2,1)S(1)}, bf16[128,3328]{1,0:T(8,128)(2,1)S(1)}, u32[]{:S(2)}, u32[]{:S(2)}) collective-permute-start(bf16[128,3328]{1,0:T(8,128)(2,1)S(1)} %add_convert_fusion.2), channel_id=1, source_target_pairs={{0,4},{1,13},{4,0},{5,9},{8,12},{9,5},{12,8},{13,1},{16,20},{17,29... | collective-permute-start | bytes 2555912 | tf_op jit(solution)/shard_map/ppermute | solution.py:65
  42.2 11.1 %collective-permute-start.8 = (bf16[64,3840]{1,0:T(8,128)(2,1)S(1)}, bf16[64,3840]{1,0:T(8,128)(2,1)S(1)}, u32[]{:S(2)}, u32[]{:S(2)}) collective-permute-start(bf16[64,3840]{1,0:T(8,128)(2,1)S(1)} %slice.296), channel_id=1, source_target_pairs={{0,4},{1,13},{4,0},{5,9},{8,12},{9,5},{12,8},{13,1},{16,20},{17,29... | collective-permute-start | bytes 1474568 | tf_op jit(solution)/shard_map/ppermute | solution.py:65
  44.9 8.9 %collective-permute-start.9 = (bf16[64,3840]{1,0:T(8,128)(2,1)S(1)}, bf16[64,3840]{1,0:T(8,128)(2,1)S(1)}, u32[]{:S(2)}, u32[]{:S(2)}) collective-permute-start(bf16[64,3840]{1,0:T(8,128)(2,1)S(1)} %slice.295), channel_id=1, source_target_pairs={{0,32},{1,97},{4,36},{5,101},{8,40},{9,105},{12,44},{13,109},{16,4... | collective-permute-start | bytes 1474568 | tf_op jit(solution)/shard_map/ppermute | solution.py:65
  45.1 8.2 %collective-permute-start.10 = (bf16[64,3328]{1,0:T(8,128)(2,1)S(1)}, bf16[64,3328]{1,0:T(8,128)(2,1)S(1)}, u32[]{:S(2)}, u32[]{:S(2)}) collective-permute-start(bf16[64,3328]{1,0:T(8,128)(2,1)S(1)} %slice.297), channel_id=1, source_target_pairs={{0,16},{1,19},{4,20},{5,23},{8,24},{9,27},{12,28},{13,31},{16,0},{... | collective-permute-start | bytes 1277960 | tf_op jit(solution)/shard_map/ppermute | solution.py:65
  54.2 7.2 %collective-permute-start.11 = (bf16[32,3840]{1,0:T(8,128)(2,1)S(1)}, bf16[32,3840]{1,0:T(8,128)(2,1)S(1)}, u32[]{:S(2)}, u32[]{:S(2)}) collective-permute-start(bf16[32,3840]{1,0:T(8,128)(2,1)S(1)} %slice.299), channel_id=1, source_target_pairs={{0,16},{1,19},{4,20},{5,23},{8,24},{9,27},{12,28},{13,31},{16,0},{... | collective-permute-start | bytes 737288 | tf_op jit(solution)/shard_map/ppermute | solution.py:65
  55.4 6.3 %collective-permute-start.12 = (bf16[32,3840]{1,0:T(8,128)(2,1)S(1)}, bf16[32,3840]{1,0:T(8,128)(2,1)S(1)}, u32[]{:S(2)}, u32[]{:S(2)}) collective-permute-start(bf16[32,3840]{1,0:T(8,128)(2,1)S(1)} %slice.298), channel_id=1, source_target_pairs={{0,4},{1,13},{4,0},{5,9},{8,12},{9,5},{12,8},{13,1},{16,20},{17,29... | collective-permute-start | bytes 737288 | tf_op jit(solution)/shard_map/ppermute | solution.py:65
  55.5 5.9 %collective-permute-start.13 = (bf16[32,3328]{1,0:T(8,128)(2,1)S(1)}, bf16[32,3328]{1,0:T(8,128)(2,1)S(1)}, u32[]{:S(2)}, u32[]{:S(2)}) collective-permute-start(bf16[32,3328]{1,0:T(8,128)(2,1)S(1)} %slice.300), channel_id=1, source_target_pairs={{0,32},{1,97},{4,36},{5,101},{8,40},{9,105},{12,44},{13,109},{16,4... | collective-permute-start | bytes 638984 | tf_op jit(solution)/shard_map/ppermute | solution.py:65
  61.9 11.1 %copy-start.3 = (f32[4,11008]{1,0:T(4,128)S(1)}, f32[4,11008]{1,0:T(4,128)}, u32[]{:S(2)}) copy-start(f32[4,11008]{1,0:T(4,128)} %param.8) | copy-start | bytes 528388
  61.9 11.1 %copy-start.4 = (f32[4,11008]{1,0:T(4,128)S(1)}, f32[4,11008]{1,0:T(4,128)}, u32[]{:S(2)}) copy-start(f32[4,11008]{1,0:T(4,128)} %param.9) | copy-start | bytes 528388
  84.8 9.8 %collective-permute-start.14 = (bf16[32,3840]{1,0:T(8,128)(2,1)S(1)}, bf16[32,3840]{1,0:T(8,128)(2,1)S(1)}, u32[]{:S(2)}, u32[]{:S(2)}) collective-permute-start(bf16[32,3840]{1,0:T(8,128)(2,1)S(1)} %get-tuple-element.70), channel_id=1, source_target_pairs={{0,16},{1,19},{4,20},{5,23},{8,24},{9,27},{12,28},{13,31},{16,0},{... | collective-permute-start | bytes 737288 | tf_op jit(solution)/shard_map/ppermute | solution.py:65
  85.5 9.0 %collective-permute-start.15 = (bf16[32,3840]{1,0:T(8,128)(2,1)S(1)}, bf16[32,3840]{1,0:T(8,128)(2,1)S(1)}, u32[]{:S(2)}, u32[]{:S(2)}) collective-permute-start(bf16[32,3840]{1,0:T(8,128)(2,1)S(1)} %get-tuple-element.71), channel_id=1, source_target_pairs={{0,4},{1,13},{4,0},{5,9},{8,12},{9,5},{12,8},{13,1},{16,20},{17,29... | collective-permute-start | bytes 737288 | tf_op jit(solution)/shard_map/ppermute | solution.py:65
  88.2 6.3 %collective-permute-start.16 = (bf16[32,3328]{1,0:T(8,128)(2,1)S(1)}, bf16[32,3328]{1,0:T(8,128)(2,1)S(1)}, u32[]{:S(2)}, u32[]{:S(2)}) collective-permute-start(bf16[32,3328]{1,0:T(8,128)(2,1)S(1)} %slice.244), channel_id=1, source_target_pairs={{0,32},{1,97},{4,36},{5,101},{8,40},{9,105},{12,44},{13,109},{16,4... | collective-permute-start | bytes 638984 | tf_op jit(solution)/shard_map/ppermute | solution.py:65
  94.7 11.7 %collective-permute-start.17 = (bf16[64,3840]{1,0:T(8,128)(2,1)S(1)}, bf16[64,3840]{1,0:T(8,128)(2,1)S(1)}, u32[]{:S(2)}, u32[]{:S(2)}) collective-permute-start(bf16[64,3840]{1,0:T(8,128)(2,1)S(1)} %pad_maximum_fusion.4), channel_id=1, source_target_pairs={{0,4},{1,13},{4,0},{5,9},{8,12},{9,5},{12,8},{13,1},{16,20},{17,29... | collective-permute-start | bytes 1474568 | tf_op jit(solution)/shard_map/ppermute | solution.py:65
  97.0 9.4 %collective-permute-start.18 = (bf16[64,3840]{1,0:T(8,128)(2,1)S(1)}, bf16[64,3840]{1,0:T(8,128)(2,1)S(1)}, u32[]{:S(2)}, u32[]{:S(2)}) collective-permute-start(bf16[64,3840]{1,0:T(8,128)(2,1)S(1)} %pad_maximum_fusion.5), channel_id=1, source_target_pairs={{0,32},{1,97},{4,36},{5,101},{8,40},{9,105},{12,44},{13,109},{16,4... | collective-permute-start | bytes 1474568 | tf_op jit(solution)/shard_map/ppermute | solution.py:65
  98.2 8.2 %collective-permute-start.19 = (bf16[64,3328]{1,0:T(8,128)(2,1)S(1)}, bf16[64,3328]{1,0:T(8,128)(2,1)S(1)}, u32[]{:S(2)}, u32[]{:S(2)}) collective-permute-start(bf16[64,3328]{1,0:T(8,128)(2,1)S(1)} %pad_maximum_fusion.6), channel_id=1, source_target_pairs={{0,16},{1,19},{4,20},{5,23},{8,24},{9,27},{12,28},{13,31},{16,0},{... | collective-permute-start | bytes 1277960 | tf_op jit(solution)/shard_map/ppermute | solution.py:65
  106.6 25.8 %collective-permute-start.20 = (bf16[128,3840]{1,0:T(8,128)(2,1)S(1)}, bf16[128,3840]{1,0:T(8,128)(2,1)S(1)}, u32[]{:S(2)}, u32[]{:S(2)}) collective-permute-start(bf16[128,3840]{1,0:T(8,128)(2,1)S(1)} %pad_maximum_fusion.refs_0_), channel_id=1, source_target_pairs={{0,32},{1,97},{4,36},{5,101},{8,40},{9,105},{12,44},{13,109},{16,4... | collective-permute-start | bytes 2949128 | tf_op jit(solution)/shard_map/ppermute | solution.py:65
  108.1 24.3 %collective-permute-start.21 = (bf16[128,3840]{1,0:T(8,128)(2,1)S(1)}, bf16[128,3840]{1,0:T(8,128)(2,1)S(1)}, u32[]{:S(2)}, u32[]{:S(2)}) collective-permute-start(bf16[128,3840]{1,0:T(8,128)(2,1)S(1)} %pad_maximum_fusion.1.refs_1_), channel_id=1, source_target_pairs={{0,16},{1,19},{4,20},{5,23},{8,24},{9,27},{12,28},{13,31},{16,0},{... | collective-permute-start | bytes 2949128 | tf_op jit(solution)/shard_map/ppermute | solution.py:65
  109.8 12.8 %collective-permute-start.22 = (bf16[128,3328]{1,0:T(8,128)(2,1)S(1)}, bf16[128,3328]{1,0:T(8,128)(2,1)S(1)}, u32[]{:S(2)}, u32[]{:S(2)}) collective-permute-start(bf16[128,3328]{1,0:T(8,128)(2,1)S(1)} %pad_maximum_fusion.2.refs_2_), channel_id=1, source_target_pairs={{0,4},{1,13},{4,0},{5,9},{8,12},{9,5},{12,8},{13,1},{16,20},{17,29... | collective-permute-start | bytes 2555912 | tf_op jit(solution)/shard_map/ppermute | solution.py:65
  111.1 21.9 %collective-permute-start.26 = (bf16[128,3328]{1,0:T(8,128)(2,1)S(1)}, bf16[128,3328]{1,0:T(8,128)(2,1)S(1)}, u32[]{:S(2)}, u32[]{:S(2)}) collective-permute-start(bf16[128,3328]{1,0:T(8,128)(2,1)S(1)} %pad_maximum_fusion.2.refs_2_), channel_id=1, source_target_pairs={{0,1},{1,0},{2,3},{3,2},{4,5},{5,4},{6,7},{7,6},{8,9},{9,8},{10,11... | collective-permute-start | bytes 2555912 | tf_op jit(solution)/shard_map/ppermute | solution.py:65
  120.1 13.0 %collective-permute-start.25 = (bf16[128,3840]{1,0:T(8,128)(2,1)S(1)}, bf16[128,3840]{1,0:T(8,128)(2,1)S(1)}, u32[]{:S(2)}, u32[]{:S(2)}) collective-permute-start(bf16[128,3840]{1,0:T(8,128)(2,1)S(1)} %pad_maximum_fusion.1.refs_1_), channel_id=1, source_target_pairs={{0,1},{1,0},{2,3},{3,2},{4,5},{5,4},{6,7},{7,6},{8,9},{9,8},{10,11... | collective-permute-start | bytes 2949128 | tf_op jit(solution)/shard_map/ppermute | solution.py:65
  122.6 12.1 %collective-permute-start.24 = (bf16[128,3840]{1,0:T(8,128)(2,1)S(1)}, bf16[128,3840]{1,0:T(8,128)(2,1)S(1)}, u32[]{:S(2)}, u32[]{:S(2)}) collective-permute-start(bf16[128,3840]{1,0:T(8,128)(2,1)S(1)} %pad_maximum_fusion.refs_0_), channel_id=1, source_target_pairs={{0,1},{1,0},{2,3},{3,2},{4,5},{5,4},{6,7},{7,6},{8,9},{9,8},{10,11... | collective-permute-start | bytes 2949128 | tf_op jit(solution)/shard_map/ppermute | solution.py:65
  132.4 4.0 %collective-permute-start.28 = (bf16[128,3840]{1,0:T(8,128)(2,1)S(1)}, bf16[128,3840]{1,0:T(8,128)(2,1)S(1)}, u32[]{:S(2)}, u32[]{:S(2)}) collective-permute-start(bf16[128,3840]{1,0:T(8,128)(2,1)S(1)} %collective-permute-done.20.own_ref), channel_id=1, source_target_pairs={{0,1},{1,0},{2,3},{3,2},{4,5},{5,4},{6,7},{7,6},{8,9},{9,8},{10,11... | collective-permute-start | bytes 2949128 | tf_op jit(solution)/shard_map/ppermute | solution.py:65
  132.5 5.9 %collective-permute-start.27 = (bf16[128,3840]{1,0:T(8,128)(2,1)S(1)}, bf16[128,3840]{1,0:T(8,128)(2,1)S(1)}, u32[]{:S(2)}, u32[]{:S(2)}) collective-permute-start(bf16[128,3840]{1,0:T(8,128)(2,1)S(1)} %collective-permute-done.21.own_ref), channel_id=1, source_target_pairs={{0,1},{1,0},{2,3},{3,2},{4,5},{5,4},{6,7},{7,6},{8,9},{9,8},{10,11... | collective-permute-start | bytes 2949128 | tf_op jit(solution)/shard_map/ppermute | solution.py:65
  133.0 7.4 %collective-permute-start.23 = (bf16[128,3328]{1,0:T(8,128)(2,1)S(1)}, bf16[128,3328]{1,0:T(8,128)(2,1)S(1)}, u32[]{:S(2)}, u32[]{:S(2)}) collective-permute-start(bf16[128,3328]{1,0:T(8,128)(2,1)S(1)} %collective-permute-done.22.own_ref), channel_id=1, source_target_pairs={{0,1},{1,0},{2,3},{3,2},{4,5},{5,4},{6,7},{7,6},{8,9},{9,8},{10,11... | collective-permute-start | bytes 2555912 | tf_op jit(solution)/shard_map/ppermute | solution.py:65
  (2 other events, 4.4 us)

commit v5 on v4

--- a/solution.py
+++ b/solution.py
@@ -15,7 +15,7 @@
 galore_scale = 0.25
 
 AXES = ("dp", "outer")
-WIDTH = 3840
+WIDTH = 1920
 PIECES = ((0, 3840), (3840, 3840), (7680, 3328))
 X, Y, Z = 0, 1, 2
 BITS = (
@@ -144,67 +144,30 @@
 
 
 def expand_kernel(basis_ref, *refs):
-    for piece in range(3):
-
-        @pl.when(pl.program_id(0) == piece)
-        def _(piece=piece):
-            size = PIECES[piece][1]
-            low = jnp.concatenate([refs[piece][...], refs[3 + piece][...]], axis=0)
-            product = jnp.dot(basis_ref[...], low, preferred_element_type=jnp.float32)
-            if len(refs) == 8:
-                product = -galore_scale * (refs[6][:, :size] + product)
-            refs[-1][:, :size] = product
-
-
-def expand(basis_rows, own, other, *early):
-    rows, depth, width = basis_rows.shape[0], 2 * own[0].shape[0], sum(size for _, size in PIECES)
-    total = pl.BlockSpec((rows, WIDTH), lambda j: (0, j))
+    low = jnp.concatenate([ref[...] for ref in refs[:4]], axis=0)
+    product = jnp.dot(basis_ref[...], low, preferred_element_type=jnp.float32)
+    refs[-1][...] = -galore_scale * product
+
+
+def expand(piece, basis_rows, blocks, places, width, *done):
+    rows, (start, size) = basis_rows.shape[0], PIECES[piece]
     return pl.pallas_call(
         expand_kernel,
-        grid=(3,),
-        in_specs=[pl.BlockSpec((rows, depth), lambda j: (0, j))]
-        + [pl.BlockSpec(block.shape, lambda j: (0, 0)) for block in (*own, *other)]
-        + [total] * len(early),
-        out_specs=total,
+        grid=(pl.cdiv(size, WIDTH),),
+        in_specs=[pl.BlockSpec((rows, 512), lambda j: (0, piece))]
+        + [pl.BlockSpec((128, WIDTH), lambda j, place=place: (place, j)) for place in places]
+        + [pl.BlockSpec(memory_space=pl.ANY)] * len(done),
+        out_specs=pl.BlockSpec((rows, WIDTH), lambda j: (0, start // WIDTH + j)),
         out_shape=jax.ShapeDtypeStruct((rows, width), jnp.float32),
+        input_output_aliases={5: 0} if done else {},
         cost_estimate=pl.CostEstimate(
-            flops=2 * rows * depth * width,
-            bytes_accessed=(2 * depth + 4 * rows) * width,
-            transcendentals=0,
-        ),
-        compiler_params=pltpu.CompilerParams(vmem_limit_bytes=24 * 1024 * 1024),
-        name="expand",
-    )(basis_rows, *own, *other, *early)
-
-
-def late_kernel(basis_ref, own_ref, other_ref, early_ref, *refs):
-    low = jnp.concatenate([own_ref[...], other_ref[...]], axis=0)
-    product = jnp.dot(basis_ref[...], low, preferred_element_type=jnp.float32)
-    refs[-1][...] = -galore_scale * (early_ref[...] + product)
-
-
-def expand_late(piece, basis_rows, own, other, early, *done):
-    rows, half, (start, size) = basis_rows.shape[0], own.shape[0], PIECES[piece]
-    step = WIDTH // 2
-    total = pl.BlockSpec((rows, step), lambda j: (0, start // step + j))
-    return pl.pallas_call(
-        late_kernel,
-        grid=(2,),
-        in_specs=[pl.BlockSpec((rows, 2 * half), lambda j: (0, piece))]
-        + [pl.BlockSpec((half, step), lambda j: (0, j))] * 2
-        + [total]
-        + [pl.BlockSpec(memory_space=pl.ANY)] * len(done),
-        out_specs=total,
-        out_shape=jax.ShapeDtypeStruct(early.shape, jnp.float32),
-        input_output_aliases={4: 0} if done else {},
-        cost_estimate=pl.CostEstimate(
-            flops=4 * rows * half * size,
-            bytes_accessed=(4 * half + 8 * rows) * size,
+            flops=2 * rows * 512 * size,
+            bytes_accessed=(2 * 512 + 4 * rows) * size,
             transcendentals=0,
         ),
         compiler_params=pltpu.CompilerParams(vmem_limit_bytes=16 * 1024 * 1024),
-        name="expand_late",
-    )(basis_rows, own, other, early, *done)
+        name="expand",
+    )(basis_rows, *blocks, *done)
 
 
 def shards(tokens, grad_out, projection_basis, first_moment, second_moment):
@@ -235,10 +198,9 @@
         got = send_pieces([s.astype(bf16) for s in sent], level)
         if level == 0:
             basis_rows = jnp.dot(basis_rows, picks, preferred_element_type=f32).astype(bf16)
-            starts = range(0, 1536, 256)
-            early_basis = jnp.concatenate([basis_rows[:, at : at + 128] for at in starts], axis=1)
-            late_basis = jnp.concatenate([basis_rows[:, at + 128 : at + 256] for at in starts], axis=1)
-            got, early_basis, late_basis = lax.optimization_barrier((got, early_basis, late_basis))
+            starts = [512 * p + 128 * at for p in range(3) for at in (0, 2, 1, 3)]
+            basis_rows = jnp.concatenate([basis_rows[:, at : at + 128] for at in starts], axis=1)
+            got, basis_rows = lax.optimization_barrier((got, basis_rows))
         held = [h + g.astype(f32) for h, g in zip(held, got)]
         half = held[0].shape[0] // 2
         if level < 2:
@@ -260,10 +222,14 @@
         got = send_pieces(low, level)
         low = [jnp.concatenate([mine, theirs], axis=0) for mine, theirs in zip(low, got)]
     late = send_pieces(low, 0)
-    early = expand(early_basis, low, [send(part, SWAP) for part in low])
-    others, done = [send(part, SWAP) for part in late], ()
+    pair, third = send(jnp.concatenate(low[:2], axis=0), SWAP), send(low[2], SWAP)
+    late, pair, third = lax.optimization_barrier((late, pair, third))
+    blocks = [low, [pair, pair, third], late, [send(part, SWAP) for part in late]]
+    done = ()
     for piece in range(3):
-        done = (expand_late(piece, late_basis, late[piece], others[piece], early, *done),)
+        parts = [block[piece] for block in blocks]
+        places = (0, piece % 2, 0, 0)
+        done = (expand(piece, basis_rows, parts, places, grad_out.shape[1], *done),)
     weight_update = done[0]
     return (weight_update, new_first, new_second)
 

time: 143 us -> 142 us (level)
  waiting for transfers between devices: 37.7 us -> 46 us
  starting transfers between devices: 53.7 us -> 45.5 us
    ppermute x29 -> x28, waiting for transfers between devices: 37.7 us -> 46 us  [send(): return lax.ppermute(value, AXES, pairs)]
    ppermute x29 -> x28, starting transfers between devices: 53.7 us -> 45.5 us  [send(): return lax.ppermute(value, AXES, pairs)]
    pallas_call x4 -> x3, Pallas kernels: 7.72 us -> 6.7 us  [expand(): pl.pallas_call(expand_kernel, grid=(pl.cdiv(size, WIDTH),), in_specs=[pl....]
    unnamed x15 -> x24, local copies, waits for them, and re-layouts: 4.48 us -> 4.63 us
  transfers between devices with their start and end apart: 29 -> 28, of which waited for: 10 -> 13; matrix products, arithmetic and copies ran while one was open for 4% -> 5% of each run, Pallas kernels for 4% -> 3%
where the time goes in v5:
time: 142 us
  waiting for transfers between devices  46 us (32%)
  starting transfers between devices  45.5 us (32%)
  blocking collectives  20.7 us (15%)
  Pallas kernels  11.3 us (8%)
  matrix products  7.27 us (5%)
  local copies, waits for them, and re-layouts  5.83 us (4%)
  other arithmetic  3.98 us (3%)
    ppermute x28, waiting for transfers between devices, send(): return lax.ppermute(value, AXES, pairs)  46 us
    ppermute x28, starting transfers between devices, send(): return lax.ppermute(value, AXES, pairs)  45.5 us
    all_to_all x2, blocking collectives, swap_groups(): lax.all_to_all(value, AXES, 0, 0, axis_index_groups=groups(), tiled=True)  20.7 us
    pallas_call x3, Pallas kernels, expand(): pl.pallas_call(expand_kernel, grid=(pl.cdiv(size, WIDTH),), in_specs=[pl....  6.7 us
    dot_general x3, matrix products, shards(): lax.dot_general(projected[:, 512 * piece:512 * piece + 512], grad_out[:,...  6.52 us
    unnamed x24, local copies, waits for them, and re-layouts  4.63 us
    pallas_call x1, Pallas kernels, project(): pl.pallas_call(project_kernel, grid_spec=pltpu.PrefetchScalarGridSpec(num...  4.56 us
  transfers between devices with their start and end apart: 28, of which 13 were waited for; matrix products, arithmetic and copies ran while one was open for 5% of the time, Pallas kernels for 3%

profile of v5, /device:TPU:1, one launch (start us, length us, event | category | flops | bytes accessed | tf_op | source)
XLA Modules:
  0.0 141.7 jit_solution(193045844121759376)
XLA Ops:
  0.8 2.2 %copy-done = bf16[4096,512]{1,0:T(8,128)(2,1)S(1)} copy-done((bf16[4096,512]{1,0:T(8,128)(2,1)S(1)}, bf16[4096,512]{1,0:T(8,128)(2,1)}, u32[]{:S(2)}) %copy-start) | copy-done | bytes 4194328
  3.0 2.2 %copy-done.1 = bf16[512,4096]{1,0:T(8,128)(2,1)S(1)} copy-done((bf16[512,4096]{1,0:T(8,128)(2,1)S(1)}, bf16[512,4096]{1,0:T(8,128)(2,1)}, u32[]{:S(2)}) %copy-start.1) | copy-done | bytes 4194328
  5.2 4.6 %project.1 = (bf16[512,1536]{1,0:T(8,128)(2,1)S(1)}, bf16[128,512]{1,0:T(8,128)(2,1)S(1)}) custom-call(s32[1]{0:T(128)} %bitcast.at_ref, s32[1,1536]{1,0:T(1,128)S(1)} %broadcast_in_dim.4.places_ref, bf16[512,4096]{1,0:T(8,128)(2,1)S(1)} %copy-done.1, bf16[4096,512]{1,0:T(8,128)(2,1)S(1)} %copy-done, bf16[4096,512]{1,0:T(8,128)(2,1)S(1)} %copy-done), custom_call_target="tpu_custom_call" | custom-call | flops 2952790016 | bytes 8388608 | tf_op jit(solution)/shard_map/project/pallas_call | solution.py:115
  9.8 2.3 %convolution_convert_fusion.1 = bf16[512,3840]{1,0:T(8,128)(2,1)S(1)} fusion(bf16[512,11008]{1,0:T(8,128)(2,1)S(1)} %copy-done.2, bf16[512,1536]{1,0:T(8,128)(2,1)S(1)} %get-tuple-element.50), kind=kOutput, calls=%fused_computation.1 | convolution fusion | flops 2015232000 | bytes 8388608 | tf_op jit(solution)/shard_map/dot_general | solution.py:184
  12.2 1.5 %collective-permute-start.1 = (bf16[128,3840]{1,0:T(8,128)(2,1)S(1)}, bf16[128,3840]{1,0:T(8,128)(2,1)S(1)}, u32[]{:S(2)}, u32[]{:S(2)}) collective-permute-start(bf16[128,3840]{1,0:T(8,128)(2,1)S(1)} %get-tuple-element.101), channel_id=1, source_target_pairs={{0,1},{1,0},{2,3},{3,2},{4,5},{5,4},{6,7},{7,6},{8,9},{9,8},{10,11... | collective-permute-start | bytes 2949128 | tf_op jit(solution)/shard_map/ppermute | solution.py:65
  13.7 2.0 %convolution_convert_fusion = bf16[512,3328]{1,0:T(8,128)(2,1)S(1)} fusion(bf16[512,11008]{1,0:T(8,128)(2,1)S(1)} %copy-done.2, bf16[512,1536]{1,0:T(8,128)(2,1)S(1)} %get-tuple-element.50), kind=kOutput, calls=%fused_computation | convolution fusion | flops 1746534400 | bytes 7340032 | tf_op jit(solution)/shard_map/dot_general | solution.py:184
  15.9 2.3 %convolution_convert_fusion.2 = bf16[512,3840]{1,0:T(8,128)(2,1)S(1)} fusion(bf16[512,11008]{1,0:T(8,128)(2,1)S(1)} %copy-done.2, bf16[512,1536]{1,0:T(8,128)(2,1)S(1)} %get-tuple-element.50), kind=kOutput, calls=%fused_computation.2 | convolution fusion | flops 2015232000 | bytes 8388608 | tf_op jit(solution)/shard_map/dot_general | solution.py:184
  21.5 2.6 %collective-permute-start.3 = (bf16[128,3840]{1,0:T(8,128)(2,1)S(1)}, bf16[128,3840]{1,0:T(8,128)(2,1)S(1)}, u32[]{:S(2)}, u32[]{:S(2)}) collective-permute-start(bf16[128,3840]{1,0:T(8,128)(2,1)S(1)} %add_convert_fusion.1), channel_id=1, source_target_pairs={{0,32},{1,97},{4,36},{5,101},{8,40},{9,105},{12,44},{13,109},{16,4... | collective-permute-start | bytes 2949128 | tf_op jit(solution)/shard_map/ppermute | solution.py:65
  24.2 2.7 %collective-permute-start.4 = (bf16[128,3840]{1,0:T(8,128)(2,1)S(1)}, bf16[128,3840]{1,0:T(8,128)(2,1)S(1)}, u32[]{:S(2)}, u32[]{:S(2)}) collective-permute-start(bf16[128,3840]{1,0:T(8,128)(2,1)S(1)} %add_convert_fusion), channel_id=1, source_target_pairs={{0,16},{1,19},{4,20},{5,23},{8,24},{9,27},{12,28},{13,31},{16,0},{... | collective-permute-start | bytes 2949128 | tf_op jit(solution)/shard_map/ppermute | solution.py:65
  26.9 4.0 %collective-permute-start.5 = (bf16[128,3328]{1,0:T(8,128)(2,1)S(1)}, bf16[128,3328]{1,0:T(8,128)(2,1)S(1)}, u32[]{:S(2)}, u32[]{:S(2)}) collective-permute-start(bf16[128,3328]{1,0:T(8,128)(2,1)S(1)} %add_convert_fusion.2), channel_id=1, source_target_pairs={{0,4},{1,13},{4,0},{5,9},{8,12},{9,5},{12,8},{13,1},{16,20},{17,29... | collective-permute-start | bytes 2555912 | tf_op jit(solution)/shard_map/ppermute | solution.py:65
  31.0 10.0 %collective-permute-done.5 = bf16[128,3328]{1,0:T(8,128)(2,1)S(1)} collective-permute-done((bf16[128,3328]{1,0:T(8,128)(2,1)S(1)}, bf16[128,3328]{1,0:T(8,128)(2,1)S(1)}, u32[]{:S(2)}, u32[]{:S(2)}) %collective-permute-start.5) | collective-permute-done | bytes 852000 | tf_op jit(solution)/shard_map/ppermute | solution.py:65
  42.2 2.8 %collective-permute-start.8 = (bf16[64,3840]{1,0:T(8,128)(2,1)S(1)}, bf16[64,3840]{1,0:T(8,128)(2,1)S(1)}, u32[]{:S(2)}, u32[]{:S(2)}) collective-permute-start(bf16[64,3840]{1,0:T(8,128)(2,1)S(1)} %slice.290), channel_id=1, source_target_pairs={{0,4},{1,13},{4,0},{5,9},{8,12},{9,5},{12,8},{13,1},{16,20},{17,29... | collective-permute-start | bytes 1474568 | tf_op jit(solution)/shard_map/ppermute | solution.py:65
  46.2 7.1 %collective-permute-done.10 = bf16[64,3328]{1,0:T(8,128)(2,1)S(1)} collective-permute-done((bf16[64,3328]{1,0:T(8,128)(2,1)S(1)}, bf16[64,3328]{1,0:T(8,128)(2,1)S(1)}, u32[]{:S(2)}, u32[]{:S(2)}) %collective-permute-start.10) | collective-permute-done | bytes 426016 | tf_op jit(solution)/shard_map/ppermute | solution.py:65
  55.5 2.0 %collective-permute-start.13 = (bf16[32,3328]{1,0:T(8,128)(2,1)S(1)}, bf16[32,3328]{1,0:T(8,128)(2,1)S(1)}, u32[]{:S(2)}, u32[]{:S(2)}) collective-permute-start(bf16[32,3328]{1,0:T(8,128)(2,1)S(1)} %slice.294), channel_id=1, source_target_pairs={{0,32},{1,97},{4,36},{5,101},{8,40},{9,105},{12,44},{13,109},{16,4... | collective-permute-start | bytes 638984 | tf_op jit(solution)/shard_map/ppermute | solution.py:65
  57.5 3.9 %collective-permute-done.13 = bf16[32,3328]{1,0:T(8,128)(2,1)S(1)} collective-permute-done((bf16[32,3328]{1,0:T(8,128)(2,1)S(1)}, bf16[32,3328]{1,0:T(8,128)(2,1)S(1)}, u32[]{:S(2)}, u32[]{:S(2)}) %collective-permute-start.13) | collective-permute-done | bytes 213024 | tf_op jit(solution)/shard_map/ppermute | solution.py:65
  62.3 10.4 %all_to_all.10 = bf16[8,4,11008]{2,1,0:T(4,128)(2,1)S(1)} all-to-all(bf16[8,4,11008]{2,1,0:T(4,128)(2,1)S(1)} %pad_maximum_fusion.3), channel_id=1, replica_groups={{0,12,18,30,96,108,114,126},{1,5,17,21,33,37,49,53},{4,8,22,26,100,104,..., dimensions={0} | all-to-all | bytes 1409024 | tf_op jit(solution)/shard_map/all_to_all | solution.py:61
  74.2 10.4 %all_to_all.11 = bf16[8,4,11008]{2,1,0:T(4,128)(2,1)S(1)} all-to-all(bf16[8,4,11008]{2,1,0:T(4,128)(2,1)S(1)} %broadcast_in_dim.5), channel_id=1, replica_groups={{0,12,18,30,96,108,114,126},{1,5,17,21,33,37,49,53},{4,8,22,26,100,104,..., dimensions={0} | all-to-all | bytes 1409024 | tf_op jit(solution)/shard_map/all_to_all | solution.py:61
  85.5 2.7 %collective-permute-start.15 = (bf16[32,3840]{1,0:T(8,128)(2,1)S(1)}, bf16[32,3840]{1,0:T(8,128)(2,1)S(1)}, u32[]{:S(2)}, u32[]{:S(2)}) collective-permute-start(bf16[32,3840]{1,0:T(8,128)(2,1)S(1)} %get-tuple-element.75), channel_id=1, source_target_pairs={{0,4},{1,13},{4,0},{5,9},{8,12},{9,5},{12,8},{13,1},{16,20},{17,29... | collective-permute-start | bytes 737288 | tf_op jit(solution)/shard_map/ppermute | solution.py:65
  88.2 1.7 %collective-permute-start.16 = (bf16[32,3328]{1,0:T(8,128)(2,1)S(1)}, bf16[32,3328]{1,0:T(8,128)(2,1)S(1)}, u32[]{:S(2)}, u32[]{:S(2)}) collective-permute-start(bf16[32,3328]{1,0:T(8,128)(2,1)S(1)} %slice.236), channel_id=1, source_target_pairs={{0,32},{1,97},{4,36},{5,101},{8,40},{9,105},{12,44},{13,109},{16,4... | collective-permute-start | bytes 638984 | tf_op jit(solution)/shard_map/ppermute | solution.py:65
  89.9 4.6 %collective-permute-done.16 = bf16[32,3328]{1,0:T(8,128)(2,1)S(1)} collective-permute-done((bf16[32,3328]{1,0:T(8,128)(2,1)S(1)}, bf16[32,3328]{1,0:T(8,128)(2,1)S(1)}, u32[]{:S(2)}, u32[]{:S(2)}) %collective-permute-start.16) | collective-permute-done | bytes 213024 | tf_op jit(solution)/shard_map/ppermute | solution.py:65
  94.7 2.3 %collective-permute-start.17 = (bf16[64,3840]{1,0:T(8,128)(2,1)S(1)}, bf16[64,3840]{1,0:T(8,128)(2,1)S(1)}, u32[]{:S(2)}, u32[]{:S(2)}) collective-permute-start(bf16[64,3840]{1,0:T(8,128)(2,1)S(1)} %pad_maximum_fusion.4), channel_id=1, source_target_pairs={{0,4},{1,13},{4,0},{5,9},{8,12},{9,5},{12,8},{13,1},{16,20},{17,29... | collective-permute-start | bytes 1474568 | tf_op jit(solution)/shard_map/ppermute | solution.py:65
  97.0 1.3 collective-permute-start.18
  98.3 1.5 %collective-permute-start.19 = (bf16[64,3328]{1,0:T(8,128)(2,1)S(1)}, bf16[64,3328]{1,0:T(8,128)(2,1)S(1)}, u32[]{:S(2)}, u32[]{:S(2)}) collective-permute-start(bf16[64,3328]{1,0:T(8,128)(2,1)S(1)} %pad_maximum_fusion.6), channel_id=1, source_target_pairs={{0,16},{1,19},{4,20},{5,23},{8,24},{9,27},{12,28},{13,31},{16,0},{... | collective-permute-start | bytes 1277960 | tf_op jit(solution)/shard_map/ppermute | solution.py:65
  99.8 6.6 %collective-permute-done.19 = bf16[64,3328]{1,0:T(8,128)(2,1)S(1)} collective-permute-done((bf16[64,3328]{1,0:T(8,128)(2,1)S(1)}, bf16[64,3328]{1,0:T(8,128)(2,1)S(1)}, u32[]{:S(2)}, u32[]{:S(2)}) %collective-permute-start.19) | collective-permute-done | bytes 426016 | tf_op jit(solution)/shard_map/ppermute | solution.py:65
  106.6 9.8 %collective-permute-start.23 = (bf16[256,3840]{1,0:T(8,128)(2,1)S(1)}, bf16[256,3840]{1,0:T(8,128)(2,1)S(1)}, u32[]{:S(2)}, u32[]{:S(2)}) collective-permute-start(bf16[256,3840]{1,0:T(8,128)(2,1)S(1)} %constant_dynamic-update-slice_fusion.8), channel_id=1, source_target_pairs={{0,1},{1,0},{2,3},{3,2},{4,5},{5,4},{6,7},{7,6},{8,9},{9,8},{10,11... | collective-permute-start | bytes 5898248 | tf_op jit(solution)/shard_map/ppermute | solution.py:65
  117.6 2.7 %collective-permute-start.24 = (bf16[128,3328]{1,0:T(8,128)(2,1)S(1)}, bf16[128,3328]{1,0:T(8,128)(2,1)S(1)}, u32[]{:S(2)}, u32[]{:S(2)}) collective-permute-start(bf16[128,3328]{1,0:T(8,128)(2,1)S(1)} %pad_maximum_fusion.2.refs_0_), channel_id=1, source_target_pairs={{0,1},{1,0},{2,3},{3,2},{4,5},{5,4},{6,7},{7,6},{8,9},{9,8},{10,11... | collective-permute-start | bytes 2555912 | tf_op jit(solution)/shard_map/ppermute | solution.py:65
  120.3 9.4 %collective-permute-done.22.refs_2_ = bf16[128,3328]{1,0:T(8,128)(2,1)S(1)} collective-permute-done((bf16[128,3328]{1,0:T(8,128)(2,1)S(1)}, bf16[128,3328]{1,0:T(8,128)(2,1)S(1)}, u32[]{:S(2)}, u32[]{:S(2)}) %collective-permute-start.22) | collective-permute-done | bytes 852000 | tf_op jit(solution)/shard_map/ppermute | solution.py:65
  131.0 1.8 %collective-permute-start.27 = (bf16[128,3840]{1,0:T(8,128)(2,1)S(1)}, bf16[128,3840]{1,0:T(8,128)(2,1)S(1)}, u32[]{:S(2)}, u32[]{:S(2)}) collective-permute-start(bf16[128,3840]{1,0:T(8,128)(2,1)S(1)} %collective-permute-done.20.refs_2_), channel_id=1, source_target_pairs={{0,1},{1,0},{2,3},{3,2},{4,5},{5,4},{6,7},{7,6},{8,9},{9,8},{10,11... | collective-permute-start | bytes 2949128 | tf_op jit(solution)/shard_map/ppermute | solution.py:65
  133.3 1.7 %collective-permute-done.27.refs_3_ = bf16[128,3840]{1,0:T(8,128)(2,1)S(1)} collective-permute-done((bf16[128,3840]{1,0:T(8,128)(2,1)S(1)}, bf16[128,3840]{1,0:T(8,128)(2,1)S(1)}, u32[]{:S(2)}, u32[]{:S(2)}) %collective-permute-start.27) | collective-permute-done | bytes 983072 | tf_op jit(solution)/shard_map/ppermute | solution.py:65
  135.0 2.2 %expand.3.refs_4_ = f32[128,11008]{1,0:T(8,128)} custom-call(bf16[128,1536]{1,0:T(8,128)(2,1)S(1)} %constant_dynamic-update-slice_fusion.basis_ref, bf16[128,3840]{1,0:T(8,128)(2,1)S(1)} %pad_maximum_fusion.refs_0_, bf16[256,3840]{1,0:T(8,128)(2,1)S(1)} %collective-permute-done.23.refs_1_, bf16[128,3840]{1,0:T(8,128)(2,1)S(1)} %collective-permute-done.20.refs_2_, ...), custom_call_target="tpu_custom_call" | custom-call | flops 503316480 | bytes 5898240 | tf_op jit(solution)/shard_map/expand/pallas_call | solution.py:154
  137.2 2.2 %expand.4.refs_4_ = f32[128,11008]{1,0:T(8,128)} custom-call(bf16[128,1536]{1,0:T(8,128)(2,1)S(1)} %constant_dynamic-update-slice_fusion.basis_ref, bf16[128,3840]{1,0:T(8,128)(2,1)S(1)} %pad_maximum_fusion.1.refs_0_, bf16[256,3840]{1,0:T(8,128)(2,1)S(1)} %collective-permute-done.23.refs_1_, ...), custom_call_target="tpu_custom_call", output_to_operand_aliasing={{}: (5, {})} | custom-call | flops 503316480 | bytes 5898240 | tf_op jit(solution)/shard_map/expand/pallas_call | solution.py:154
  139.4 2.3 %expand.5 = f32[128,11008]{1,0:T(8,128)} custom-call(bf16[128,1536]{1,0:T(8,128)(2,1)S(1)} %constant_dynamic-update-slice_fusion.basis_ref, bf16[128,3328]{1,0:T(8,128)(2,1)S(1)} %pad_maximum_fusion.2.refs_0_, bf16[128,3328]{1,0:T(8,128)(2,1)S(1)} %collective-permute-done.24.refs_1_, ...), custom_call_target="tpu_custom_call", output_to_operand_aliasing={{}: (5, {})} | custom-call | flops 436207616 | bytes 5111808 | tf_op jit(solution)/shard_map/expand/pallas_call | solution.py:154
  (100 shorter events, 14.9 us)
Async XLA Ops:
  0.8 2.2 %copy-start = (bf16[4096,512]{1,0:T(8,128)(2,1)S(1)}, bf16[4096,512]{1,0:T(8,128)(2,1)}, u32[]{:S(2)}) copy-start(bf16[4096,512]{1,0:T(8,128)(2,1)} %rows_ref.1) | copy-start | bytes 12582916
  5.2 4.6 %copy-start.2 = (bf16[512,11008]{1,0:T(8,128)(2,1)S(1)}, bf16[512,11008]{1,0:T(8,128)(2,1)}, u32[]{:S(2)}) copy-start(bf16[512,11008]{1,0:T(8,128)(2,1)} %param.6) | copy-start | bytes 33816580
  12.2 8.1 %collective-permute-start.1 = (bf16[128,3840]{1,0:T(8,128)(2,1)S(1)}, bf16[128,3840]{1,0:T(8,128)(2,1)S(1)}, u32[]{:S(2)}, u32[]{:S(2)}) collective-permute-start(bf16[128,3840]{1,0:T(8,128)(2,1)S(1)} %get-tuple-element.101), channel_id=1, source_target_pairs={{0,1},{1,0},{2,3},{3,2},{4,5},{5,4},{6,7},{7,6},{8,9},{9,8},{10,11... | collective-permute-start | bytes 2949128 | tf_op jit(solution)/shard_map/ppermute | solution.py:65
  15.8 5.5 %collective-permute-start.2 = (bf16[256,3328]{1,0:T(8,128)(2,1)S(1)}, bf16[256,3328]{1,0:T(8,128)(2,1)S(1)}, u32[]{:S(2)}, u32[]{:S(2)}) collective-permute-start(bf16[256,3328]{1,0:T(8,128)(2,1)S(1)} %slice.206), channel_id=1, source_target_pairs={{0,1},{1,0},{2,3},{3,2},{4,5},{5,4},{6,7},{7,6},{8,9},{9,8},{10,11... | collective-permute-start | bytes 5111816 | tf_op jit(solution)/shard_map/ppermute | solution.py:65
  18.3 2.8 %collective-permute-start = (bf16[128,3840]{1,0:T(8,128)(2,1)S(1)}, bf16[128,3840]{1,0:T(8,128)(2,1)S(1)}, u32[]{:S(2)}, u32[]{:S(2)}) collective-permute-start(bf16[128,3840]{1,0:T(8,128)(2,1)S(1)} %get-tuple-element.103), channel_id=1, source_target_pairs={{0,1},{1,0},{2,3},{3,2},{4,5},{5,4},{6,7},{7,6},{8,9},{9,8},{10,11... | collective-permute-start | bytes 2949128 | tf_op jit(solution)/shard_map/ppermute | solution.py:65
  18.9 22.1 %collective-permute-start.7 = (bf16[128,3840]{1,0:T(8,128)(2,1)S(1)}, bf16[128,3840]{1,0:T(8,128)(2,1)S(1)}, u32[]{:S(2)}, u32[]{:S(2)}) collective-permute-start(bf16[128,3840]{1,0:T(8,128)(2,1)S(1)} %get-tuple-element.100), channel_id=1, source_target_pairs={{0,1},{1,0},{2,3},{3,2},{4,5},{5,4},{6,7},{7,6},{8,9},{9,8},{10,11... | collective-permute-start | bytes 2949128 | tf_op jit(solution)/shard_map/ppermute | solution.py:65
  19.0 22.4 %collective-permute-start.6 = (bf16[128,3840]{1,0:T(8,128)(2,1)S(1)}, bf16[128,3840]{1,0:T(8,128)(2,1)S(1)}, u32[]{:S(2)}, u32[]{:S(2)}) collective-permute-start(bf16[128,3840]{1,0:T(8,128)(2,1)S(1)} %get-tuple-element.102), channel_id=1, source_target_pairs={{0,1},{1,0},{2,3},{3,2},{4,5},{5,4},{6,7},{7,6},{8,9},{9,8},{10,11... | collective-permute-start | bytes 2949128 | tf_op jit(solution)/shard_map/ppermute | solution.py:65
  21.5 19.5 %collective-permute-start.3 = (bf16[128,3840]{1,0:T(8,128)(2,1)S(1)}, bf16[128,3840]{1,0:T(8,128)(2,1)S(1)}, u32[]{:S(2)}, u32[]{:S(2)}) collective-permute-start(bf16[128,3840]{1,0:T(8,128)(2,1)S(1)} %add_convert_fusion.1), channel_id=1, source_target_pairs={{0,32},{1,97},{4,36},{5,101},{8,40},{9,105},{12,44},{13,109},{16,4... | collective-permute-start | bytes 2949128 | tf_op jit(solution)/shard_map/ppermute | solution.py:65
  24.2 16.9 %collective-permute-start.4 = (bf16[128,3840]{1,0:T(8,128)(2,1)S(1)}, bf16[128,3840]{1,0:T(8,128)(2,1)S(1)}, u32[]{:S(2)}, u32[]{:S(2)}) collective-permute-start(bf16[128,3840]{1,0:T(8,128)(2,1)S(1)} %add_convert_fusion), channel_id=1, source_target_pairs={{0,16},{1,19},{4,20},{5,23},{8,24},{9,27},{12,28},{13,31},{16,0},{... | collective-permute-start | bytes 2949128 | tf_op jit(solution)/shard_map/ppermute | solution.py:65
  26.9 14.1 %collective-permute-start.5 = (bf16[128,3328]{1,0:T(8,128)(2,1)S(1)}, bf16[128,3328]{1,0:T(8,128)(2,1)S(1)}, u32[]{:S(2)}, u32[]{:S(2)}) collective-permute-start(bf16[128,3328]{1,0:T(8,128)(2,1)S(1)} %add_convert_fusion.2), channel_id=1, source_target_pairs={{0,4},{1,13},{4,0},{5,9},{8,12},{9,5},{12,8},{13,1},{16,20},{17,29... | collective-permute-start | bytes 2555912 | tf_op jit(solution)/shard_map/ppermute | solution.py:65
  42.2 11.1 %collective-permute-start.8 = (bf16[64,3840]{1,0:T(8,128)(2,1)S(1)}, bf16[64,3840]{1,0:T(8,128)(2,1)S(1)}, u32[]{:S(2)}, u32[]{:S(2)}) collective-permute-start(bf16[64,3840]{1,0:T(8,128)(2,1)S(1)} %slice.290), channel_id=1, source_target_pairs={{0,4},{1,13},{4,0},{5,9},{8,12},{9,5},{12,8},{13,1},{16,20},{17,29... | collective-permute-start | bytes 1474568 | tf_op jit(solution)/shard_map/ppermute | solution.py:65
  44.9 8.9 %collective-permute-start.9 = (bf16[64,3840]{1,0:T(8,128)(2,1)S(1)}, bf16[64,3840]{1,0:T(8,128)(2,1)S(1)}, u32[]{:S(2)}, u32[]{:S(2)}) collective-permute-start(bf16[64,3840]{1,0:T(8,128)(2,1)S(1)} %slice.289), channel_id=1, source_target_pairs={{0,32},{1,97},{4,36},{5,101},{8,40},{9,105},{12,44},{13,109},{16,4... | collective-permute-start | bytes 1474568 | tf_op jit(solution)/shard_map/ppermute | solution.py:65
  45.1 8.2 %collective-permute-start.10 = (bf16[64,3328]{1,0:T(8,128)(2,1)S(1)}, bf16[64,3328]{1,0:T(8,128)(2,1)S(1)}, u32[]{:S(2)}, u32[]{:S(2)}) collective-permute-start(bf16[64,3328]{1,0:T(8,128)(2,1)S(1)} %slice.291), channel_id=1, source_target_pairs={{0,16},{1,19},{4,20},{5,23},{8,24},{9,27},{12,28},{13,31},{16,0},{... | collective-permute-start | bytes 1277960 | tf_op jit(solution)/shard_map/ppermute | solution.py:65
  54.2 7.2 %collective-permute-start.11 = (bf16[32,3840]{1,0:T(8,128)(2,1)S(1)}, bf16[32,3840]{1,0:T(8,128)(2,1)S(1)}, u32[]{:S(2)}, u32[]{:S(2)}) collective-permute-start(bf16[32,3840]{1,0:T(8,128)(2,1)S(1)} %slice.293), channel_id=1, source_target_pairs={{0,16},{1,19},{4,20},{5,23},{8,24},{9,27},{12,28},{13,31},{16,0},{... | collective-permute-start | bytes 737288 | tf_op jit(solution)/shard_map/ppermute | solution.py:65
  55.4 6.3 %collective-permute-start.12 = (bf16[32,3840]{1,0:T(8,128)(2,1)S(1)}, bf16[32,3840]{1,0:T(8,128)(2,1)S(1)}, u32[]{:S(2)}, u32[]{:S(2)}) collective-permute-start(bf16[32,3840]{1,0:T(8,128)(2,1)S(1)} %slice.292), channel_id=1, source_target_pairs={{0,4},{1,13},{4,0},{5,9},{8,12},{9,5},{12,8},{13,1},{16,20},{17,29... | collective-permute-start | bytes 737288 | tf_op jit(solution)/shard_map/ppermute | solution.py:65
  55.5 5.9 %collective-permute-start.13 = (bf16[32,3328]{1,0:T(8,128)(2,1)S(1)}, bf16[32,3328]{1,0:T(8,128)(2,1)S(1)}, u32[]{:S(2)}, u32[]{:S(2)}) collective-permute-start(bf16[32,3328]{1,0:T(8,128)(2,1)S(1)} %slice.294), channel_id=1, source_target_pairs={{0,32},{1,97},{4,36},{5,101},{8,40},{9,105},{12,44},{13,109},{16,4... | collective-permute-start | bytes 638984 | tf_op jit(solution)/shard_map/ppermute | solution.py:65
  61.9 11.1 %copy-start.3 = (f32[4,11008]{1,0:T(4,128)S(1)}, f32[4,11008]{1,0:T(4,128)}, u32[]{:S(2)}) copy-start(f32[4,11008]{1,0:T(4,128)} %param.8) | copy-start | bytes 528388
  61.9 11.1 %copy-start.4 = (f32[4,11008]{1,0:T(4,128)S(1)}, f32[4,11008]{1,0:T(4,128)}, u32[]{:S(2)}) copy-start(f32[4,11008]{1,0:T(4,128)} %param.9) | copy-start | bytes 528388
  84.8 9.8 %collective-permute-start.14 = (bf16[32,3840]{1,0:T(8,128)(2,1)S(1)}, bf16[32,3840]{1,0:T(8,128)(2,1)S(1)}, u32[]{:S(2)}, u32[]{:S(2)}) collective-permute-start(bf16[32,3840]{1,0:T(8,128)(2,1)S(1)} %get-tuple-element.74), channel_id=1, source_target_pairs={{0,16},{1,19},{4,20},{5,23},{8,24},{9,27},{12,28},{13,31},{16,0},{... | collective-permute-start | bytes 737288 | tf_op jit(solution)/shard_map/ppermute | solution.py:65
  85.5 9.0 %collective-permute-start.15 = (bf16[32,3840]{1,0:T(8,128)(2,1)S(1)}, bf16[32,3840]{1,0:T(8,128)(2,1)S(1)}, u32[]{:S(2)}, u32[]{:S(2)}) collective-permute-start(bf16[32,3840]{1,0:T(8,128)(2,1)S(1)} %get-tuple-element.75), channel_id=1, source_target_pairs={{0,4},{1,13},{4,0},{5,9},{8,12},{9,5},{12,8},{13,1},{16,20},{17,29... | collective-permute-start | bytes 737288 | tf_op jit(solution)/shard_map/ppermute | solution.py:65
  88.2 6.2 %collective-permute-start.16 = (bf16[32,3328]{1,0:T(8,128)(2,1)S(1)}, bf16[32,3328]{1,0:T(8,128)(2,1)S(1)}, u32[]{:S(2)}, u32[]{:S(2)}) collective-permute-start(bf16[32,3328]{1,0:T(8,128)(2,1)S(1)} %slice.236), channel_id=1, source_target_pairs={{0,32},{1,97},{4,36},{5,101},{8,40},{9,105},{12,44},{13,109},{16,4... | collective-permute-start | bytes 638984 | tf_op jit(solution)/shard_map/ppermute | solution.py:65
  94.7 11.8 %collective-permute-start.17 = (bf16[64,3840]{1,0:T(8,128)(2,1)S(1)}, bf16[64,3840]{1,0:T(8,128)(2,1)S(1)}, u32[]{:S(2)}, u32[]{:S(2)}) collective-permute-start(bf16[64,3840]{1,0:T(8,128)(2,1)S(1)} %pad_maximum_fusion.4), channel_id=1, source_target_pairs={{0,4},{1,13},{4,0},{5,9},{8,12},{9,5},{12,8},{13,1},{16,20},{17,29... | collective-permute-start | bytes 1474568 | tf_op jit(solution)/shard_map/ppermute | solution.py:65
  97.0 9.5 %collective-permute-start.18 = (bf16[64,3840]{1,0:T(8,128)(2,1)S(1)}, bf16[64,3840]{1,0:T(8,128)(2,1)S(1)}, u32[]{:S(2)}, u32[]{:S(2)}) collective-permute-start(bf16[64,3840]{1,0:T(8,128)(2,1)S(1)} %pad_maximum_fusion.5), channel_id=1, source_target_pairs={{0,32},{1,97},{4,36},{5,101},{8,40},{9,105},{12,44},{13,109},{16,4... | collective-permute-start | bytes 1474568 | tf_op jit(solution)/shard_map/ppermute | solution.py:65
  98.3 8.2 %collective-permute-start.19 = (bf16[64,3328]{1,0:T(8,128)(2,1)S(1)}, bf16[64,3328]{1,0:T(8,128)(2,1)S(1)}, u32[]{:S(2)}, u32[]{:S(2)}) collective-permute-start(bf16[64,3328]{1,0:T(8,128)(2,1)S(1)} %pad_maximum_fusion.6), channel_id=1, source_target_pairs={{0,16},{1,19},{4,20},{5,23},{8,24},{9,27},{12,28},{13,31},{16,0},{... | collective-permute-start | bytes 1277960 | tf_op jit(solution)/shard_map/ppermute | solution.py:65
  106.6 24.4 %collective-permute-start.23 = (bf16[256,3840]{1,0:T(8,128)(2,1)S(1)}, bf16[256,3840]{1,0:T(8,128)(2,1)S(1)}, u32[]{:S(2)}, u32[]{:S(2)}) collective-permute-start(bf16[256,3840]{1,0:T(8,128)(2,1)S(1)} %constant_dynamic-update-slice_fusion.8), channel_id=1, source_target_pairs={{0,1},{1,0},{2,3},{3,2},{4,5},{5,4},{6,7},{7,6},{8,9},{9,8},{10,11... | collective-permute-start | bytes 5898248 | tf_op jit(solution)/shard_map/ppermute | solution.py:65
  116.6 14.2 %collective-permute-start.20 = (bf16[128,3840]{1,0:T(8,128)(2,1)S(1)}, bf16[128,3840]{1,0:T(8,128)(2,1)S(1)}, u32[]{:S(2)}, u32[]{:S(2)}) collective-permute-start(bf16[128,3840]{1,0:T(8,128)(2,1)S(1)} %pad_maximum_fusion.refs_0_), channel_id=1, source_target_pairs={{0,32},{1,97},{4,36},{5,101},{8,40},{9,105},{12,44},{13,109},{16,4... | collective-permute-start | bytes 2949128 | tf_op jit(solution)/shard_map/ppermute | solution.py:65
  116.7 14.2 %collective-permute-start.21 = (bf16[128,3840]{1,0:T(8,128)(2,1)S(1)}, bf16[128,3840]{1,0:T(8,128)(2,1)S(1)}, u32[]{:S(2)}, u32[]{:S(2)}) collective-permute-start(bf16[128,3840]{1,0:T(8,128)(2,1)S(1)} %pad_maximum_fusion.1.refs_0_), channel_id=1, source_target_pairs={{0,16},{1,19},{4,20},{5,23},{8,24},{9,27},{12,28},{13,31},{16,0},{... | collective-permute-start | bytes 2949128 | tf_op jit(solution)/shard_map/ppermute | solution.py:65
  117.0 12.8 %collective-permute-start.22 = (bf16[128,3328]{1,0:T(8,128)(2,1)S(1)}, bf16[128,3328]{1,0:T(8,128)(2,1)S(1)}, u32[]{:S(2)}, u32[]{:S(2)}) collective-permute-start(bf16[128,3328]{1,0:T(8,128)(2,1)S(1)} %pad_maximum_fusion.2.refs_0_), channel_id=1, source_target_pairs={{0,4},{1,13},{4,0},{5,9},{8,12},{9,5},{12,8},{13,1},{16,20},{17,29... | collective-permute-start | bytes 2555912 | tf_op jit(solution)/shard_map/ppermute | solution.py:65
  117.6 13.4 %collective-permute-start.24 = (bf16[128,3328]{1,0:T(8,128)(2,1)S(1)}, bf16[128,3328]{1,0:T(8,128)(2,1)S(1)}, u32[]{:S(2)}, u32[]{:S(2)}) collective-permute-start(bf16[128,3328]{1,0:T(8,128)(2,1)S(1)} %pad_maximum_fusion.2.refs_0_), channel_id=1, source_target_pairs={{0,1},{1,0},{2,3},{3,2},{4,5},{5,4},{6,7},{7,6},{8,9},{9,8},{10,11... | collective-permute-start | bytes 2555912 | tf_op jit(solution)/shard_map/ppermute | solution.py:65
  131.0 4.0 %collective-permute-start.27 = (bf16[128,3840]{1,0:T(8,128)(2,1)S(1)}, bf16[128,3840]{1,0:T(8,128)(2,1)S(1)}, u32[]{:S(2)}, u32[]{:S(2)}) collective-permute-start(bf16[128,3840]{1,0:T(8,128)(2,1)S(1)} %collective-permute-done.20.refs_2_), channel_id=1, source_target_pairs={{0,1},{1,0},{2,3},{3,2},{4,5},{5,4},{6,7},{7,6},{8,9},{9,8},{10,11... | collective-permute-start | bytes 2949128 | tf_op jit(solution)/shard_map/ppermute | solution.py:65
  132.8 4.4 %collective-permute-start.26 = (bf16[128,3840]{1,0:T(8,128)(2,1)S(1)}, bf16[128,3840]{1,0:T(8,128)(2,1)S(1)}, u32[]{:S(2)}, u32[]{:S(2)}) collective-permute-start(bf16[128,3840]{1,0:T(8,128)(2,1)S(1)} %collective-permute-done.21.refs_2_), channel_id=1, source_target_pairs={{0,1},{1,0},{2,3},{3,2},{4,5},{5,4},{6,7},{7,6},{8,9},{9,8},{10,11... | collective-permute-start | bytes 2949128 | tf_op jit(solution)/shard_map/ppermute | solution.py:65
  132.9 6.5 %collective-permute-start.25 = (bf16[128,3328]{1,0:T(8,128)(2,1)S(1)}, bf16[128,3328]{1,0:T(8,128)(2,1)S(1)}, u32[]{:S(2)}, u32[]{:S(2)}) collective-permute-start(bf16[128,3328]{1,0:T(8,128)(2,1)S(1)} %collective-permute-done.22.refs_2_), channel_id=1, source_target_pairs={{0,1},{1,0},{2,3},{3,2},{4,5},{5,4},{6,7},{7,6},{8,9},{9,8},{10,11... | collective-permute-start | bytes 2555912 | tf_op jit(solution)/shard_map/ppermute | solution.py:65
  (1 other events, 2.2 us)

commit v6 on v5

--- a/solution.py
+++ b/solution.py
@@ -67,9 +67,7 @@
 
 def send_pieces(values, level):
     values = lax.optimization_barrier(tuple(values))
-    return lax.optimization_barrier(
-        tuple(send(v, exchange(bits[level])) for v, bits in zip(values, BITS))
-    )
+    return tuple(send(v, exchange(bits[level])) for v, bits in zip(values, BITS))
 
 
 def rank_order(bits, dp, outer):
@@ -200,8 +198,9 @@
             basis_rows = jnp.dot(basis_rows, picks, preferred_element_type=f32).astype(bf16)
             starts = [512 * p + 128 * at for p in range(3) for at in (0, 2, 1, 3)]
             basis_rows = jnp.concatenate([basis_rows[:, at : at + 128] for at in starts], axis=1)
-            got, basis_rows = lax.optimization_barrier((got, basis_rows))
         held = [h + g.astype(f32) for h, g in zip(held, got)]
+        if level == 0:
+            held, basis_rows = lax.optimization_barrier((held, basis_rows))
         half = held[0].shape[0] // 2
         if level < 2:
             sent, held = [h[half:] for h in held], [h[:half] for h in held]

time: 142 us -> 140 us (0.986)
  starting transfers between devices: 45.5 us -> 36 us
  waiting for transfers between devices: 46 us -> 52.3 us
    ppermute x28, starting transfers between devices: 45.5 us -> 36 us  [send(): return lax.ppermute(value, AXES, pairs)]
    ppermute x28, waiting for transfers between devices: 46 us -> 52.3 us  [send(): return lax.ppermute(value, AXES, pairs)]
  transfers between devices with their start and end apart: 28 -> 28, of which waited for: 13 -> 17; matrix products, arithmetic and copies ran while one was open for 5% -> 6% of each run, Pallas kernels for 3% -> 3%
where the time goes in v6:
time: 140 us
  waiting for transfers between devices  52.3 us (37%)
  starting transfers between devices  36 us (26%)
  blocking collectives  21 us (15%)
  Pallas kernels  11.3 us (8%)
  matrix products  7.27 us (5%)
  local copies, waits for them, and re-layouts  5.83 us (4%)
  other arithmetic  5.01 us (4%)
    ppermute x28, waiting for transfers between devices, send(): return lax.ppermute(value, AXES, pairs)  52.3 us
    ppermute x28, starting transfers between devices, send(): return lax.ppermute(value, AXES, pairs)  36 us
    all_to_all x2, blocking collectives, swap_groups(): lax.all_to_all(value, AXES, 0, 0, axis_index_groups=groups(), tiled=True)  21 us
    pallas_call x3, Pallas kernels, expand(): pl.pallas_call(expand_kernel, grid=(pl.cdiv(size, WIDTH),), in_specs=[pl....  6.72 us
    dot_general x3, matrix products, shards(): lax.dot_general(projected[:, 512 * piece:512 * piece + 512], grad_out[:,...  6.52 us
    unnamed x24, local copies, waits for them, and re-layouts  4.63 us
    pallas_call x1, Pallas kernels, project(): pl.pallas_call(project_kernel, grid_spec=pltpu.PrefetchScalarGridSpec(num...  4.56 us
  transfers between devices with their start and end apart: 28, of which 17 were waited for; matrix products, arithmetic and copies ran while one was open for 6% of the time, Pallas kernels for 3%

profile of v6, /device:TPU:1, one launch (start us, length us, event | category | flops | bytes accessed | tf_op | source)
XLA Modules:
  0.0 139.8 jit_solution(152184957060553377)
XLA Ops:
  0.8 2.2 %copy-done = bf16[4096,512]{1,0:T(8,128)(2,1)S(1)} copy-done((bf16[4096,512]{1,0:T(8,128)(2,1)S(1)}, bf16[4096,512]{1,0:T(8,128)(2,1)}, u32[]{:S(2)}) %copy-start) | copy-done | bytes 4194328
  3.0 2.2 %copy-done.1 = bf16[512,4096]{1,0:T(8,128)(2,1)S(1)} copy-done((bf16[512,4096]{1,0:T(8,128)(2,1)S(1)}, bf16[512,4096]{1,0:T(8,128)(2,1)}, u32[]{:S(2)}) %copy-start.1) | copy-done | bytes 4194328
  5.2 4.6 %project.1 = (bf16[512,1536]{1,0:T(8,128)(2,1)S(1)}, bf16[128,512]{1,0:T(8,128)(2,1)S(1)}) custom-call(s32[1]{0:T(128)} %bitcast.at_ref, s32[1,1536]{1,0:T(1,128)S(1)} %broadcast_in_dim.4.places_ref, bf16[512,4096]{1,0:T(8,128)(2,1)S(1)} %copy-done.1, bf16[4096,512]{1,0:T(8,128)(2,1)S(1)} %copy-done, bf16[4096,512]{1,0:T(8,128)(2,1)S(1)} %copy-done), custom_call_target="tpu_custom_call" | custom-call | flops 2952790016 | bytes 8388608 | tf_op jit(solution)/shard_map/project/pallas_call | solution.py:113
  9.8 2.3 %convolution_convert_fusion.1 = bf16[512,3840]{1,0:T(8,128)(2,1)S(1)} fusion(bf16[512,11008]{1,0:T(8,128)(2,1)S(1)} %copy-done.2, bf16[512,1536]{1,0:T(8,128)(2,1)S(1)} %get-tuple-element.32), kind=kOutput, calls=%fused_computation.1 | convolution fusion | flops 2015232000 | bytes 8388608 | tf_op jit(solution)/shard_map/dot_general | solution.py:182
  12.2 1.5 %collective-permute-start.2 = (bf16[128,3840]{1,0:T(8,128)(2,1)S(1)}, bf16[128,3840]{1,0:T(8,128)(2,1)S(1)}, u32[]{:S(2)}, u32[]{:S(2)}) collective-permute-start(bf16[128,3840]{1,0:T(8,128)(2,1)S(1)} %get-tuple-element.65), channel_id=1, source_target_pairs={{0,1},{1,0},{2,3},{3,2},{4,5},{5,4},{6,7},{7,6},{8,9},{9,8},{10,11... | collective-permute-start | bytes 2949128 | tf_op jit(solution)/shard_map/ppermute | solution.py:65
  13.7 2.0 %convolution_convert_fusion = bf16[512,3328]{1,0:T(8,128)(2,1)S(1)} fusion(bf16[512,11008]{1,0:T(8,128)(2,1)S(1)} %copy-done.2, bf16[512,1536]{1,0:T(8,128)(2,1)S(1)} %get-tuple-element.32), kind=kOutput, calls=%fused_computation | convolution fusion | flops 1746534400 | bytes 7340032 | tf_op jit(solution)/shard_map/dot_general | solution.py:182
  15.9 2.3 %convolution_convert_fusion.2 = bf16[512,3840]{1,0:T(8,128)(2,1)S(1)} fusion(bf16[512,11008]{1,0:T(8,128)(2,1)S(1)} %copy-done.2, bf16[512,1536]{1,0:T(8,128)(2,1)S(1)} %get-tuple-element.32), kind=kOutput, calls=%fused_computation.2 | convolution fusion | flops 2015232000 | bytes 8388608 | tf_op jit(solution)/shard_map/dot_general | solution.py:182
  21.5 3.9 %collective-permute-start.7 = (bf16[128,3328]{1,0:T(8,128)(2,1)S(1)}, bf16[128,3328]{1,0:T(8,128)(2,1)S(1)}, u32[]{:S(2)}, u32[]{:S(2)}) collective-permute-start(bf16[128,3328]{1,0:T(8,128)(2,1)S(1)} %add_convert_fusion.2), channel_id=1, source_target_pairs={{0,4},{1,13},{4,0},{5,9},{8,12},{9,5},{12,8},{13,1},{16,20},{17,29... | collective-permute-start | bytes 2555912 | tf_op jit(solution)/shard_map/ppermute | solution.py:65
  25.5 2.8 %collective-permute-start.6 = (bf16[128,3840]{1,0:T(8,128)(2,1)S(1)}, bf16[128,3840]{1,0:T(8,128)(2,1)S(1)}, u32[]{:S(2)}, u32[]{:S(2)}) collective-permute-start(bf16[128,3840]{1,0:T(8,128)(2,1)S(1)} %add_convert_fusion), channel_id=1, source_target_pairs={{0,16},{1,19},{4,20},{5,23},{8,24},{9,27},{12,28},{13,31},{16,0},{... | collective-permute-start | bytes 2949128 | tf_op jit(solution)/shard_map/ppermute | solution.py:65
  28.3 2.5 %collective-permute-start.4 = (bf16[128,3840]{1,0:T(8,128)(2,1)S(1)}, bf16[128,3840]{1,0:T(8,128)(2,1)S(1)}, u32[]{:S(2)}, u32[]{:S(2)}) collective-permute-start(bf16[128,3840]{1,0:T(8,128)(2,1)S(1)} %add_convert_fusion.1), channel_id=1, source_target_pairs={{0,32},{1,97},{4,36},{5,101},{8,40},{9,105},{12,44},{13,109},{16,4... | collective-permute-start | bytes 2949128 | tf_op jit(solution)/shard_map/ppermute | solution.py:65
  30.8 4.7 %collective-permute-done.7 = bf16[128,3328]{1,0:T(8,128)(2,1)S(1)} collective-permute-done((bf16[128,3328]{1,0:T(8,128)(2,1)S(1)}, bf16[128,3328]{1,0:T(8,128)(2,1)S(1)}, u32[]{:S(2)}, u32[]{:S(2)}) %collective-permute-start.7) | collective-permute-done | bytes 852000 | tf_op jit(solution)/shard_map/ppermute | solution.py:65
  35.8 4.0 %collective-permute-done.6 = bf16[128,3840]{1,0:T(8,128)(2,1)S(1)} collective-permute-done((bf16[128,3840]{1,0:T(8,128)(2,1)S(1)}, bf16[128,3840]{1,0:T(8,128)(2,1)S(1)}, u32[]{:S(2)}, u32[]{:S(2)}) %collective-permute-start.6) | collective-permute-done | bytes 983072 | tf_op jit(solution)/shard_map/ppermute | solution.py:65
  40.2 2.3 %collective-permute-done.4 = bf16[128,3840]{1,0:T(8,128)(2,1)S(1)} collective-permute-done((bf16[128,3840]{1,0:T(8,128)(2,1)S(1)}, bf16[128,3840]{1,0:T(8,128)(2,1)S(1)}, u32[]{:S(2)}, u32[]{:S(2)}) %collective-permute-start.4) | collective-permute-done | bytes 983072 | tf_op jit(solution)/shard_map/ppermute | solution.py:65
  43.5 2.5 %collective-permute-start.9 = (bf16[64,3840]{1,0:T(8,128)(2,1)S(1)}, bf16[64,3840]{1,0:T(8,128)(2,1)S(1)}, u32[]{:S(2)}, u32[]{:S(2)}) collective-permute-start(bf16[64,3840]{1,0:T(8,128)(2,1)S(1)} %slice.286), channel_id=1, source_target_pairs={{0,32},{1,97},{4,36},{5,101},{8,40},{9,105},{12,44},{13,109},{16,4... | collective-permute-start | bytes 1474568 | tf_op jit(solution)/shard_map/ppermute | solution.py:65
  46.0 5.2 %collective-permute-done.10 = bf16[64,3328]{1,0:T(8,128)(2,1)S(1)} collective-permute-done((bf16[64,3328]{1,0:T(8,128)(2,1)S(1)}, bf16[64,3328]{1,0:T(8,128)(2,1)S(1)}, u32[]{:S(2)}, u32[]{:S(2)}) %collective-permute-start.10) | collective-permute-done | bytes 426016 | tf_op jit(solution)/shard_map/ppermute | solution.py:65
  52.5 2.3 %collective-permute-done.8 = bf16[64,3840]{1,0:T(8,128)(2,1)S(1)} collective-permute-done((bf16[64,3840]{1,0:T(8,128)(2,1)S(1)}, bf16[64,3840]{1,0:T(8,128)(2,1)S(1)}, u32[]{:S(2)}, u32[]{:S(2)}) %collective-permute-start.8) | collective-permute-done | bytes 491552 | tf_op jit(solution)/shard_map/ppermute | solution.py:65
  55.3 2.2 %collective-permute-start.11 = (bf16[32,3840]{1,0:T(8,128)(2,1)S(1)}, bf16[32,3840]{1,0:T(8,128)(2,1)}, u32[]{:S(2)}, u32[]{:S(2)}) collective-permute-start(bf16[32,3840]{1,0:T(8,128)(2,1)S(1)} %slice.290), channel_id=1, source_target_pairs={{0,16},{1,19},{4,20},{5,23},{8,24},{9,27},{12,28},{13,31},{16,0},{... | collective-permute-start | bytes 737288 | tf_op jit(solution)/shard_map/ppermute | solution.py:65
  57.5 3.4 %collective-permute-done.13 = bf16[32,3328]{1,0:T(8,128)(2,1)S(1)} collective-permute-done((bf16[32,3328]{1,0:T(8,128)(2,1)S(1)}, bf16[32,3328]{1,0:T(8,128)(2,1)S(1)}, u32[]{:S(2)}, u32[]{:S(2)}) %collective-permute-start.13) | collective-permute-done | bytes 213024 | tf_op jit(solution)/shard_map/ppermute | solution.py:65
  64.2 10.7 %all_to_all.10 = bf16[8,4,11008]{2,1,0:T(4,128)(2,1)S(1)} all-to-all(bf16[8,4,11008]{2,1,0:T(4,128)(2,1)S(1)} %pad_maximum_fusion.3), channel_id=1, replica_groups={{0,12,18,30,96,108,114,126},{1,5,17,21,33,37,49,53},{4,8,22,26,100,104,..., dimensions={0} | all-to-all | bytes 1409024 | tf_op jit(solution)/shard_map/all_to_all | solution.py:61
  76.4 10.4 %all_to_all.11 = bf16[8,4,11008]{2,1,0:T(4,128)(2,1)S(1)} all-to-all(bf16[8,4,11008]{2,1,0:T(4,128)(2,1)S(1)} %broadcast_in_dim.5), channel_id=1, replica_groups={{0,12,18,30,96,108,114,126},{1,5,17,21,33,37,49,53},{4,8,22,26,100,104,..., dimensions={0} | all-to-all | bytes 1409024 | tf_op jit(solution)/shard_map/all_to_all | solution.py:61
  87.0 1.8 %collective-permute-start.14 = (bf16[32,3328]{1,0:T(8,128)(2,1)S(1)}, bf16[32,3328]{1,0:T(8,128)(2,1)S(1)}, u32[]{:S(2)}, u32[]{:S(2)}) collective-permute-start(bf16[32,3328]{1,0:T(8,128)(2,1)S(1)} %slice.233), channel_id=1, source_target_pairs={{0,32},{1,97},{4,36},{5,101},{8,40},{9,105},{12,44},{13,109},{16,4... | collective-permute-start | bytes 638984 | tf_op jit(solution)/shard_map/ppermute | solution.py:65
  89.8 5.4 %collective-permute-done.14 = bf16[32,3328]{1,0:T(8,128)(2,1)S(1)} collective-permute-done((bf16[32,3328]{1,0:T(8,128)(2,1)S(1)}, bf16[32,3328]{1,0:T(8,128)(2,1)S(1)}, u32[]{:S(2)}, u32[]{:S(2)}) %collective-permute-start.14) | collective-permute-done | bytes 213024 | tf_op jit(solution)/shard_map/ppermute | solution.py:65
  95.2 2.3 %collective-permute-done.16 = bf16[32,3840]{1,0:T(8,128)(2,1)S(1)} collective-permute-done((bf16[32,3840]{1,0:T(8,128)(2,1)S(1)}, bf16[32,3840]{1,0:T(8,128)(2,1)S(1)}, u32[]{:S(2)}, u32[]{:S(2)}) %collective-permute-start.16) | collective-permute-done | bytes 245792 | tf_op jit(solution)/shard_map/ppermute | solution.py:65
  99.1 1.6 %collective-permute-start.17 = (bf16[64,3328]{1,0:T(8,128)(2,1)S(1)}, bf16[64,3328]{1,0:T(8,128)(2,1)S(1)}, u32[]{:S(2)}, u32[]{:S(2)}) collective-permute-start(bf16[64,3328]{1,0:T(8,128)(2,1)S(1)} %pad_maximum_fusion.6), channel_id=1, source_target_pairs={{0,16},{1,19},{4,20},{5,23},{8,24},{9,27},{12,28},{13,31},{16,0},{... | collective-permute-start | bytes 1277960 | tf_op jit(solution)/shard_map/ppermute | solution.py:65
  100.7 5.8 %collective-permute-done.18 = bf16[64,3840]{1,0:T(8,128)(2,1)S(1)} collective-permute-done((bf16[64,3840]{1,0:T(8,128)(2,1)S(1)}, bf16[64,3840]{1,0:T(8,128)(2,1)S(1)}, u32[]{:S(2)}, u32[]{:S(2)}) %collective-permute-start.18) | collective-permute-done | bytes 491552 | tf_op jit(solution)/shard_map/ppermute | solution.py:65
  107.0 6.5 %collective-permute-start.23 = (bf16[256,3840]{1,0:T(8,128)(2,1)S(1)}, bf16[256,3840]{1,0:T(8,128)(2,1)S(1)}, u32[]{:S(2)}, u32[]{:S(2)}) collective-permute-start(bf16[256,3840]{1,0:T(8,128)(2,1)S(1)} %constant_dynamic-update-slice_fusion.8), channel_id=1, source_target_pairs={{0,1},{1,0},{2,3},{3,2},{4,5},{5,4},{6,7},{7,6},{8,9},{9,8},{10,11... | collective-permute-start | bytes 5898248 | tf_op jit(solution)/shard_map/ppermute | solution.py:65
  113.7 1.7 %collective-permute-start.20 = (bf16[128,3840]{1,0:T(8,128)(2,1)S(1)}, bf16[128,3840]{1,0:T(8,128)(2,1)S(1)}, u32[]{:S(2)}, u32[]{:S(2)}) collective-permute-start(bf16[128,3840]{1,0:T(8,128)(2,1)S(1)} %pad_maximum_fusion.refs_0_), channel_id=1, source_target_pairs={{0,32},{1,97},{4,36},{5,101},{8,40},{9,105},{12,44},{13,109},{16,4... | collective-permute-start | bytes 2949128 | tf_op jit(solution)/shard_map/ppermute | solution.py:65
  119.7 10.7 %collective-permute-done.22.refs_2_ = bf16[128,3328]{1,0:T(8,128)(2,1)S(1)} collective-permute-done((bf16[128,3328]{1,0:T(8,128)(2,1)S(1)}, bf16[128,3328]{1,0:T(8,128)(2,1)S(1)}, u32[]{:S(2)}, u32[]{:S(2)}) %collective-permute-start.22) | collective-permute-done | bytes 852000 | tf_op jit(solution)/shard_map/ppermute | solution.py:65
  131.1 2.0 %collective-permute-done.27.refs_3_ = bf16[128,3840]{1,0:T(8,128)(2,1)S(1)} collective-permute-done((bf16[128,3840]{1,0:T(8,128)(2,1)S(1)}, bf16[128,3840]{1,0:T(8,128)(2,1)S(1)}, u32[]{:S(2)}, u32[]{:S(2)}) %collective-permute-start.27) | collective-permute-done | bytes 983072 | tf_op jit(solution)/shard_map/ppermute | solution.py:65
  133.1 2.2 %expand.3.refs_4_ = f32[128,11008]{1,0:T(8,128)} custom-call(bf16[128,1536]{1,0:T(8,128)(2,1)S(1)} %constant_dynamic-update-slice_fusion.basis_ref, bf16[128,3840]{1,0:T(8,128)(2,1)S(1)} %pad_maximum_fusion.refs_0_, bf16[256,3840]{1,0:T(8,128)(2,1)S(1)} %collective-permute-done.23.refs_1_, bf16[128,3840]{1,0:T(8,128)(2,1)S(1)} %collective-permute-done.20.refs_2_, ...), custom_call_target="tpu_custom_call" | custom-call | flops 503316480 | bytes 5898240 | tf_op jit(solution)/shard_map/expand/pallas_call | solution.py:152
  135.3 2.2 %expand.4.refs_4_ = f32[128,11008]{1,0:T(8,128)} custom-call(bf16[128,1536]{1,0:T(8,128)(2,1)S(1)} %constant_dynamic-update-slice_fusion.basis_ref, bf16[128,3840]{1,0:T(8,128)(2,1)S(1)} %pad_maximum_fusion.1.refs_0_, bf16[256,3840]{1,0:T(8,128)(2,1)S(1)} %collective-permute-done.23.refs_1_, ...), custom_call_target="tpu_custom_call", output_to_operand_aliasing={{}: (5, {})} | custom-call | flops 503316480 | bytes 5898240 | tf_op jit(solution)/shard_map/expand/pallas_call | solution.py:152
  137.5 2.3 %expand.5 = f32[128,11008]{1,0:T(8,128)} custom-call(bf16[128,1536]{1,0:T(8,128)(2,1)S(1)} %constant_dynamic-update-slice_fusion.basis_ref, bf16[128,3328]{1,0:T(8,128)(2,1)S(1)} %pad_maximum_fusion.2.refs_0_, bf16[128,3328]{1,0:T(8,128)(2,1)S(1)} %collective-permute-done.24.refs_1_, ...), custom_call_target="tpu_custom_call", output_to_operand_aliasing={{}: (5, {})} | custom-call | flops 436207616 | bytes 5111808 | tf_op jit(solution)/shard_map/expand/pallas_call | solution.py:152
  (100 shorter events, 20.3 us)
Async XLA Ops:
  0.8 2.2 %copy-start = (bf16[4096,512]{1,0:T(8,128)(2,1)S(1)}, bf16[4096,512]{1,0:T(8,128)(2,1)}, u32[]{:S(2)}) copy-start(bf16[4096,512]{1,0:T(8,128)(2,1)} %rows_ref.1) | copy-start | bytes 12582916
  5.2 4.6 %copy-start.2 = (bf16[512,11008]{1,0:T(8,128)(2,1)S(1)}, bf16[512,11008]{1,0:T(8,128)(2,1)}, u32[]{:S(2)}) copy-start(bf16[512,11008]{1,0:T(8,128)(2,1)} %param.6) | copy-start | bytes 33816580
  12.2 8.1 %collective-permute-start.2 = (bf16[128,3840]{1,0:T(8,128)(2,1)S(1)}, bf16[128,3840]{1,0:T(8,128)(2,1)S(1)}, u32[]{:S(2)}, u32[]{:S(2)}) collective-permute-start(bf16[128,3840]{1,0:T(8,128)(2,1)S(1)} %get-tuple-element.65), channel_id=1, source_target_pairs={{0,1},{1,0},{2,3},{3,2},{4,5},{5,4},{6,7},{7,6},{8,9},{9,8},{10,11... | collective-permute-start | bytes 2949128 | tf_op jit(solution)/shard_map/ppermute | solution.py:65
  15.8 5.5 %collective-permute-start.3 = (bf16[256,3328]{1,0:T(8,128)(2,1)S(1)}, bf16[256,3328]{1,0:T(8,128)(2,1)S(1)}, u32[]{:S(2)}, u32[]{:S(2)}) collective-permute-start(bf16[256,3328]{1,0:T(8,128)(2,1)S(1)} %slice.208), channel_id=1, source_target_pairs={{0,1},{1,0},{2,3},{3,2},{4,5},{5,4},{6,7},{7,6},{8,9},{9,8},{10,11... | collective-permute-start | bytes 5111816 | tf_op jit(solution)/shard_map/ppermute | solution.py:65
  18.3 2.8 %collective-permute-start.1 = (bf16[128,3840]{1,0:T(8,128)(2,1)S(1)}, bf16[128,3840]{1,0:T(8,128)(2,1)S(1)}, u32[]{:S(2)}, u32[]{:S(2)}) collective-permute-start(bf16[128,3840]{1,0:T(8,128)(2,1)S(1)} %get-tuple-element.67), channel_id=1, source_target_pairs={{0,1},{1,0},{2,3},{3,2},{4,5},{5,4},{6,7},{7,6},{8,9},{9,8},{10,11... | collective-permute-start | bytes 2949128 | tf_op jit(solution)/shard_map/ppermute | solution.py:65
  18.9 16.9 %collective-permute-start.5 = (bf16[128,3840]{1,0:T(8,128)(2,1)S(1)}, bf16[128,3840]{1,0:T(8,128)(2,1)S(1)}, u32[]{:S(2)}, u32[]{:S(2)}) collective-permute-start(bf16[128,3840]{1,0:T(8,128)(2,1)S(1)} %get-tuple-element.64), channel_id=1, source_target_pairs={{0,1},{1,0},{2,3},{3,2},{4,5},{5,4},{6,7},{7,6},{8,9},{9,8},{10,11... | collective-permute-start | bytes 2949128 | tf_op jit(solution)/shard_map/ppermute | solution.py:65
  19.0 21.2 %collective-permute-start = (bf16[128,3840]{1,0:T(8,128)(2,1)S(1)}, bf16[128,3840]{1,0:T(8,128)(2,1)S(1)}, u32[]{:S(2)}, u32[]{:S(2)}) collective-permute-start(bf16[128,3840]{1,0:T(8,128)(2,1)S(1)} %get-tuple-element.66), channel_id=1, source_target_pairs={{0,1},{1,0},{2,3},{3,2},{4,5},{5,4},{6,7},{7,6},{8,9},{9,8},{10,11... | collective-permute-start | bytes 2949128 | tf_op jit(solution)/shard_map/ppermute | solution.py:65
  21.5 14.0 %collective-permute-start.7 = (bf16[128,3328]{1,0:T(8,128)(2,1)S(1)}, bf16[128,3328]{1,0:T(8,128)(2,1)S(1)}, u32[]{:S(2)}, u32[]{:S(2)}) collective-permute-start(bf16[128,3328]{1,0:T(8,128)(2,1)S(1)} %add_convert_fusion.2), channel_id=1, source_target_pairs={{0,4},{1,13},{4,0},{5,9},{8,12},{9,5},{12,8},{13,1},{16,20},{17,29... | collective-permute-start | bytes 2555912 | tf_op jit(solution)/shard_map/ppermute | solution.py:65
  25.5 14.3 %collective-permute-start.6 = (bf16[128,3840]{1,0:T(8,128)(2,1)S(1)}, bf16[128,3840]{1,0:T(8,128)(2,1)S(1)}, u32[]{:S(2)}, u32[]{:S(2)}) collective-permute-start(bf16[128,3840]{1,0:T(8,128)(2,1)S(1)} %add_convert_fusion), channel_id=1, source_target_pairs={{0,16},{1,19},{4,20},{5,23},{8,24},{9,27},{12,28},{13,31},{16,0},{... | collective-permute-start | bytes 2949128 | tf_op jit(solution)/shard_map/ppermute | solution.py:65
  28.3 14.2 %collective-permute-start.4 = (bf16[128,3840]{1,0:T(8,128)(2,1)S(1)}, bf16[128,3840]{1,0:T(8,128)(2,1)S(1)}, u32[]{:S(2)}, u32[]{:S(2)}) collective-permute-start(bf16[128,3840]{1,0:T(8,128)(2,1)S(1)} %add_convert_fusion.1), channel_id=1, source_target_pairs={{0,32},{1,97},{4,36},{5,101},{8,40},{9,105},{12,44},{13,109},{16,4... | collective-permute-start | bytes 2949128 | tf_op jit(solution)/shard_map/ppermute | solution.py:65
  43.0 8.3 %collective-permute-start.10 = (bf16[64,3328]{1,0:T(8,128)(2,1)S(1)}, bf16[64,3328]{1,0:T(8,128)(2,1)S(1)}, u32[]{:S(2)}, u32[]{:S(2)}) collective-permute-start(bf16[64,3328]{1,0:T(8,128)(2,1)S(1)} %slice.288), channel_id=1, source_target_pairs={{0,16},{1,19},{4,20},{5,23},{8,24},{9,27},{12,28},{13,31},{16,0},{... | collective-permute-start | bytes 1277960 | tf_op jit(solution)/shard_map/ppermute | solution.py:65
  43.5 8.9 %collective-permute-start.9 = (bf16[64,3840]{1,0:T(8,128)(2,1)S(1)}, bf16[64,3840]{1,0:T(8,128)(2,1)S(1)}, u32[]{:S(2)}, u32[]{:S(2)}) collective-permute-start(bf16[64,3840]{1,0:T(8,128)(2,1)S(1)} %slice.286), channel_id=1, source_target_pairs={{0,32},{1,97},{4,36},{5,101},{8,40},{9,105},{12,44},{13,109},{16,4... | collective-permute-start | bytes 1474568 | tf_op jit(solution)/shard_map/ppermute | solution.py:65
  46.0 8.9 %collective-permute-start.8 = (bf16[64,3840]{1,0:T(8,128)(2,1)S(1)}, bf16[64,3840]{1,0:T(8,128)(2,1)S(1)}, u32[]{:S(2)}, u32[]{:S(2)}) collective-permute-start(bf16[64,3840]{1,0:T(8,128)(2,1)S(1)} %slice.287), channel_id=1, source_target_pairs={{0,4},{1,13},{4,0},{5,9},{8,12},{9,5},{12,8},{13,1},{16,20},{17,29... | collective-permute-start | bytes 1474568 | tf_op jit(solution)/shard_map/ppermute | solution.py:65
  55.0 6.0 %collective-permute-start.13 = (bf16[32,3328]{1,0:T(8,128)(2,1)S(1)}, bf16[32,3328]{1,0:T(8,128)(2,1)S(1)}, u32[]{:S(2)}, u32[]{:S(2)}) collective-permute-start(bf16[32,3328]{1,0:T(8,128)(2,1)S(1)} %slice.291), channel_id=1, source_target_pairs={{0,32},{1,97},{4,36},{5,101},{8,40},{9,105},{12,44},{13,109},{16,4... | collective-permute-start | bytes 638984 | tf_op jit(solution)/shard_map/ppermute | solution.py:65
  55.3 6.4 %collective-permute-start.11 = (bf16[32,3840]{1,0:T(8,128)(2,1)S(1)}, bf16[32,3840]{1,0:T(8,128)(2,1)}, u32[]{:S(2)}, u32[]{:S(2)}) collective-permute-start(bf16[32,3840]{1,0:T(8,128)(2,1)S(1)} %slice.290), channel_id=1, source_target_pairs={{0,16},{1,19},{4,20},{5,23},{8,24},{9,27},{12,28},{13,31},{16,0},{... | collective-permute-start | bytes 737288 | tf_op jit(solution)/shard_map/ppermute | solution.py:65
  57.5 6.3 %collective-permute-start.12 = (bf16[32,3840]{1,0:T(8,128)(2,1)S(1)}, bf16[32,3840]{1,0:T(8,128)(2,1)S(1)}, u32[]{:S(2)}, u32[]{:S(2)}) collective-permute-start(bf16[32,3840]{1,0:T(8,128)(2,1)S(1)} %slice.289), channel_id=1, source_target_pairs={{0,4},{1,13},{4,0},{5,9},{8,12},{9,5},{12,8},{13,1},{16,20},{17,29... | collective-permute-start | bytes 737288 | tf_op jit(solution)/shard_map/ppermute | solution.py:65
  63.9 11.3 %copy-start.3 = (f32[4,11008]{1,0:T(4,128)S(1)}, f32[4,11008]{1,0:T(4,128)}, u32[]{:S(2)}) copy-start(f32[4,11008]{1,0:T(4,128)} %param.8) | copy-start | bytes 528388
  63.9 11.3 %copy-start.4 = (f32[4,11008]{1,0:T(4,128)S(1)}, f32[4,11008]{1,0:T(4,128)}, u32[]{:S(2)}) copy-start(f32[4,11008]{1,0:T(4,128)} %param.9) | copy-start | bytes 528388
  87.0 8.2 %collective-permute-start.14 = (bf16[32,3328]{1,0:T(8,128)(2,1)S(1)}, bf16[32,3328]{1,0:T(8,128)(2,1)S(1)}, u32[]{:S(2)}, u32[]{:S(2)}) collective-permute-start(bf16[32,3328]{1,0:T(8,128)(2,1)S(1)} %slice.233), channel_id=1, source_target_pairs={{0,32},{1,97},{4,36},{5,101},{8,40},{9,105},{12,44},{13,109},{16,4... | collective-permute-start | bytes 638984 | tf_op jit(solution)/shard_map/ppermute | solution.py:65
  88.7 8.8 %collective-permute-start.15 = (bf16[32,3840]{1,0:T(8,128)(2,1)S(1)}, bf16[32,3840]{1,0:T(8,128)(2,1)S(1)}, u32[]{:S(2)}, u32[]{:S(2)}) collective-permute-start(bf16[32,3840]{1,0:T(8,128)(2,1)S(1)} %get-tuple-element.48), channel_id=1, source_target_pairs={{0,16},{1,19},{4,20},{5,23},{8,24},{9,27},{12,28},{13,31},{16,0},{... | collective-permute-start | bytes 737288 | tf_op jit(solution)/shard_map/ppermute | solution.py:65
  89.8 7.7 %collective-permute-start.16 = (bf16[32,3840]{1,0:T(8,128)(2,1)S(1)}, bf16[32,3840]{1,0:T(8,128)(2,1)S(1)}, u32[]{:S(2)}, u32[]{:S(2)}) collective-permute-start(bf16[32,3840]{1,0:T(8,128)(2,1)S(1)} %get-tuple-element.49), channel_id=1, source_target_pairs={{0,4},{1,13},{4,0},{5,9},{8,12},{9,5},{12,8},{13,1},{16,20},{17,29... | collective-permute-start | bytes 737288 | tf_op jit(solution)/shard_map/ppermute | solution.py:65
  97.6 9.0 %collective-permute-start.18 = (bf16[64,3840]{1,0:T(8,128)(2,1)S(1)}, bf16[64,3840]{1,0:T(8,128)(2,1)S(1)}, u32[]{:S(2)}, u32[]{:S(2)}) collective-permute-start(bf16[64,3840]{1,0:T(8,128)(2,1)S(1)} %pad_maximum_fusion.4), channel_id=1, source_target_pairs={{0,4},{1,13},{4,0},{5,9},{8,12},{9,5},{12,8},{13,1},{16,20},{17,29... | collective-permute-start | bytes 1474568 | tf_op jit(solution)/shard_map/ppermute | solution.py:65
  98.1 8.9 %collective-permute-start.19 = (bf16[64,3840]{1,0:T(8,128)(2,1)S(1)}, bf16[64,3840]{1,0:T(8,128)(2,1)S(1)}, u32[]{:S(2)}, u32[]{:S(2)}) collective-permute-start(bf16[64,3840]{1,0:T(8,128)(2,1)S(1)} %pad_maximum_fusion.5), channel_id=1, source_target_pairs={{0,32},{1,97},{4,36},{5,101},{8,40},{9,105},{12,44},{13,109},{16,4... | collective-permute-start | bytes 1474568 | tf_op jit(solution)/shard_map/ppermute | solution.py:65
  99.1 14.4 %collective-permute-start.17 = (bf16[64,3328]{1,0:T(8,128)(2,1)S(1)}, bf16[64,3328]{1,0:T(8,128)(2,1)S(1)}, u32[]{:S(2)}, u32[]{:S(2)}) collective-permute-start(bf16[64,3328]{1,0:T(8,128)(2,1)S(1)} %pad_maximum_fusion.6), channel_id=1, source_target_pairs={{0,16},{1,19},{4,20},{5,23},{8,24},{9,27},{12,28},{13,31},{16,0},{... | collective-permute-start | bytes 1277960 | tf_op jit(solution)/shard_map/ppermute | solution.py:65
  107.0 23.5 %collective-permute-start.23 = (bf16[256,3840]{1,0:T(8,128)(2,1)S(1)}, bf16[256,3840]{1,0:T(8,128)(2,1)S(1)}, u32[]{:S(2)}, u32[]{:S(2)}) collective-permute-start(bf16[256,3840]{1,0:T(8,128)(2,1)S(1)} %constant_dynamic-update-slice_fusion.8), channel_id=1, source_target_pairs={{0,1},{1,0},{2,3},{3,2},{4,5},{5,4},{6,7},{7,6},{8,9},{9,8},{10,11... | collective-permute-start | bytes 5898248 | tf_op jit(solution)/shard_map/ppermute | solution.py:65
  113.7 16.7 %collective-permute-start.20 = (bf16[128,3840]{1,0:T(8,128)(2,1)S(1)}, bf16[128,3840]{1,0:T(8,128)(2,1)S(1)}, u32[]{:S(2)}, u32[]{:S(2)}) collective-permute-start(bf16[128,3840]{1,0:T(8,128)(2,1)S(1)} %pad_maximum_fusion.refs_0_), channel_id=1, source_target_pairs={{0,32},{1,97},{4,36},{5,101},{8,40},{9,105},{12,44},{13,109},{16,4... | collective-permute-start | bytes 2949128 | tf_op jit(solution)/shard_map/ppermute | solution.py:65
  115.4 15.0 %collective-permute-start.21 = (bf16[128,3840]{1,0:T(8,128)(2,1)S(1)}, bf16[128,3840]{1,0:T(8,128)(2,1)S(1)}, u32[]{:S(2)}, u32[]{:S(2)}) collective-permute-start(bf16[128,3840]{1,0:T(8,128)(2,1)S(1)} %pad_maximum_fusion.1.refs_0_), channel_id=1, source_target_pairs={{0,16},{1,19},{4,20},{5,23},{8,24},{9,27},{12,28},{13,31},{16,0},{... | collective-permute-start | bytes 2949128 | tf_op jit(solution)/shard_map/ppermute | solution.py:65
  116.5 3.2 %collective-permute-start.24 = (bf16[128,3328]{1,0:T(8,128)(2,1)S(1)}, bf16[128,3328]{1,0:T(8,128)(2,1)S(1)}, u32[]{:S(2)}, u32[]{:S(2)}) collective-permute-start(bf16[128,3328]{1,0:T(8,128)(2,1)S(1)} %pad_maximum_fusion.2.refs_0_), channel_id=1, source_target_pairs={{0,1},{1,0},{2,3},{3,2},{4,5},{5,4},{6,7},{7,6},{8,9},{9,8},{10,11... | collective-permute-start | bytes 2555912 | tf_op jit(solution)/shard_map/ppermute | solution.py:65
  117.7 12.8 %collective-permute-start.22 = (bf16[128,3328]{1,0:T(8,128)(2,1)S(1)}, bf16[128,3328]{1,0:T(8,128)(2,1)S(1)}, u32[]{:S(2)}, u32[]{:S(2)}) collective-permute-start(bf16[128,3328]{1,0:T(8,128)(2,1)S(1)} %pad_maximum_fusion.2.refs_0_), channel_id=1, source_target_pairs={{0,4},{1,13},{4,0},{5,9},{8,12},{9,5},{12,8},{13,1},{16,20},{17,29... | collective-permute-start | bytes 2555912 | tf_op jit(solution)/shard_map/ppermute | solution.py:65
  130.5 2.6 %collective-permute-start.27 = (bf16[128,3840]{1,0:T(8,128)(2,1)S(1)}, bf16[128,3840]{1,0:T(8,128)(2,1)S(1)}, u32[]{:S(2)}, u32[]{:S(2)}) collective-permute-start(bf16[128,3840]{1,0:T(8,128)(2,1)S(1)} %collective-permute-done.20.refs_2_), channel_id=1, source_target_pairs={{0,1},{1,0},{2,3},{3,2},{4,5},{5,4},{6,7},{7,6},{8,9},{9,8},{10,11... | collective-permute-start | bytes 2949128 | tf_op jit(solution)/shard_map/ppermute | solution.py:65
  130.6 4.7 %collective-permute-start.26 = (bf16[128,3840]{1,0:T(8,128)(2,1)S(1)}, bf16[128,3840]{1,0:T(8,128)(2,1)S(1)}, u32[]{:S(2)}, u32[]{:S(2)}) collective-permute-start(bf16[128,3840]{1,0:T(8,128)(2,1)S(1)} %collective-permute-done.21.refs_2_), channel_id=1, source_target_pairs={{0,1},{1,0},{2,3},{3,2},{4,5},{5,4},{6,7},{7,6},{8,9},{9,8},{10,11... | collective-permute-start | bytes 2949128 | tf_op jit(solution)/shard_map/ppermute | solution.py:65
  131.1 6.5 %collective-permute-start.25 = (bf16[128,3328]{1,0:T(8,128)(2,1)S(1)}, bf16[128,3328]{1,0:T(8,128)(2,1)S(1)}, u32[]{:S(2)}, u32[]{:S(2)}) collective-permute-start(bf16[128,3328]{1,0:T(8,128)(2,1)S(1)} %collective-permute-done.22.refs_2_), channel_id=1, source_target_pairs={{0,1},{1,0},{2,3},{3,2},{4,5},{5,4},{6,7},{7,6},{8,9},{9,8},{10,11... | collective-permute-start | bytes 2555912 | tf_op jit(solution)/shard_map/ppermute | solution.py:65
  (1 other events, 2.2 us)

commit v7 on v6

--- a/solution.py
+++ b/solution.py
@@ -222,7 +222,10 @@
         low = [jnp.concatenate([mine, theirs], axis=0) for mine, theirs in zip(low, got)]
     late = send_pieces(low, 0)
     pair, third = send(jnp.concatenate(low[:2], axis=0), SWAP), send(low[2], SWAP)
-    late, pair, third = lax.optimization_barrier((late, pair, third))
+    first, second, last = late
+    first, second, pair = lax.optimization_barrier((first, second, pair))
+    last, third = lax.optimization_barrier((last, third))
+    late = (first, second, last)
     blocks = [low, [pair, pair, third], late, [send(part, SWAP) for part in late]]
     done = ()
     for piece in range(3):

time: 140 us -> 139 us (level)
  transfers between devices with their start and end apart: 28 -> 28, of which waited for: 17 -> 18; matrix products, arithmetic and copies ran while one was open for 6% -> 6% of each run, Pallas kernels for 3% -> 3%
where the time goes in v7:
time: 139 us
  waiting for transfers between devices  51.6 us (37%)
  starting transfers between devices  35.8 us (26%)
  blocking collectives  21 us (15%)
  Pallas kernels  11.3 us (8%)
  matrix products  7.27 us (5%)
  local copies, waits for them, and re-layouts  5.83 us (4%)
  other arithmetic  5.01 us (4%)
    ppermute x28, waiting for transfers between devices, send(): return lax.ppermute(value, AXES, pairs)  51.6 us
    ppermute x28, starting transfers between devices, send(): return lax.ppermute(value, AXES, pairs)  35.8 us
    all_to_all x2, blocking collectives, swap_groups(): lax.all_to_all(value, AXES, 0, 0, axis_index_groups=groups(), tiled=True)  21 us
    pallas_call x3, Pallas kernels, expand(): pl.pallas_call(expand_kernel, grid=(pl.cdiv(size, WIDTH),), in_specs=[pl....  6.71 us
    dot_general x3, matrix products, shards(): lax.dot_general(projected[:, 512 * piece:512 * piece + 512], grad_out[:,...  6.52 us
    unnamed x24, local copies, waits for them, and re-layouts  4.63 us
    pallas_call x1, Pallas kernels, project(): pl.pallas_call(project_kernel, grid_spec=pltpu.PrefetchScalarGridSpec(num...  4.56 us
  transfers between devices with their start and end apart: 28, of which 18 were waited for; matrix products, arithmetic and copies ran while one was open for 6% of the time, Pallas kernels for 3%

profile of v7, /device:TPU:1, one launch (start us, length us, event | category | flops | bytes accessed | tf_op | source)
XLA Modules:
  0.0 138.9 jit_solution(17614088627567386656)
XLA Ops:
  0.8 2.2 %copy-done = bf16[4096,512]{1,0:T(8,128)(2,1)S(1)} copy-done((bf16[4096,512]{1,0:T(8,128)(2,1)S(1)}, bf16[4096,512]{1,0:T(8,128)(2,1)}, u32[]{:S(2)}) %copy-start) | copy-done | bytes 4194328
  3.0 2.2 %copy-done.1 = bf16[512,4096]{1,0:T(8,128)(2,1)S(1)} copy-done((bf16[512,4096]{1,0:T(8,128)(2,1)S(1)}, bf16[512,4096]{1,0:T(8,128)(2,1)}, u32[]{:S(2)}) %copy-start.1) | copy-done | bytes 4194328
  5.2 4.6 %project.1 = (bf16[512,1536]{1,0:T(8,128)(2,1)S(1)}, bf16[128,512]{1,0:T(8,128)(2,1)S(1)}) custom-call(s32[1]{0:T(128)} %bitcast.at_ref, s32[1,1536]{1,0:T(1,128)S(1)} %broadcast_in_dim.4.places_ref, bf16[512,4096]{1,0:T(8,128)(2,1)S(1)} %copy-done.1, bf16[4096,512]{1,0:T(8,128)(2,1)S(1)} %copy-done, bf16[4096,512]{1,0:T(8,128)(2,1)S(1)} %copy-done), custom_call_target="tpu_custom_call" | custom-call | flops 2952790016 | bytes 8388608 | tf_op jit(solution)/shard_map/project/pallas_call | solution.py:113
  9.8 2.3 %convolution_convert_fusion.1 = bf16[512,3840]{1,0:T(8,128)(2,1)S(1)} fusion(bf16[512,11008]{1,0:T(8,128)(2,1)S(1)} %copy-done.2, bf16[512,1536]{1,0:T(8,128)(2,1)S(1)} %get-tuple-element.32), kind=kOutput, calls=%fused_computation.1 | convolution fusion | flops 2015232000 | bytes 8388608 | tf_op jit(solution)/shard_map/dot_general | solution.py:182
  13.7 2.0 %convolution_convert_fusion = bf16[512,3328]{1,0:T(8,128)(2,1)S(1)} fusion(bf16[512,11008]{1,0:T(8,128)(2,1)S(1)} %copy-done.2, bf16[512,1536]{1,0:T(8,128)(2,1)S(1)} %get-tuple-element.32), kind=kOutput, calls=%fused_computation | convolution fusion | flops 1746534400 | bytes 7340032 | tf_op jit(solution)/shard_map/dot_general | solution.py:182
  15.9 2.3 %convolution_convert_fusion.2 = bf16[512,3840]{1,0:T(8,128)(2,1)S(1)} fusion(bf16[512,11008]{1,0:T(8,128)(2,1)S(1)} %copy-done.2, bf16[512,1536]{1,0:T(8,128)(2,1)S(1)} %get-tuple-element.32), kind=kOutput, calls=%fused_computation.2 | convolution fusion | flops 2015232000 | bytes 8388608 | tf_op jit(solution)/shard_map/dot_general | solution.py:182
  21.5 3.9 %collective-permute-start.7 = (bf16[128,3328]{1,0:T(8,128)(2,1)S(1)}, bf16[128,3328]{1,0:T(8,128)(2,1)S(1)}, u32[]{:S(2)}, u32[]{:S(2)}) collective-permute-start(bf16[128,3328]{1,0:T(8,128)(2,1)S(1)} %add_convert_fusion.2), channel_id=1, source_target_pairs={{0,4},{1,13},{4,0},{5,9},{8,12},{9,5},{12,8},{13,1},{16,20},{17,29... | collective-permute-start | bytes 2555912 | tf_op jit(solution)/shard_map/ppermute | solution.py:65
  25.5 2.8 %collective-permute-start.6 = (bf16[128,3840]{1,0:T(8,128)(2,1)S(1)}, bf16[128,3840]{1,0:T(8,128)(2,1)S(1)}, u32[]{:S(2)}, u32[]{:S(2)}) collective-permute-start(bf16[128,3840]{1,0:T(8,128)(2,1)S(1)} %add_convert_fusion), channel_id=1, source_target_pairs={{0,16},{1,19},{4,20},{5,23},{8,24},{9,27},{12,28},{13,31},{16,0},{... | collective-permute-start | bytes 2949128 | tf_op jit(solution)/shard_map/ppermute | solution.py:65
  28.3 2.5 %collective-permute-start.4 = (bf16[128,3840]{1,0:T(8,128)(2,1)S(1)}, bf16[128,3840]{1,0:T(8,128)(2,1)S(1)}, u32[]{:S(2)}, u32[]{:S(2)}) collective-permute-start(bf16[128,3840]{1,0:T(8,128)(2,1)S(1)} %add_convert_fusion.1), channel_id=1, source_target_pairs={{0,32},{1,97},{4,36},{5,101},{8,40},{9,105},{12,44},{13,109},{16,4... | collective-permute-start | bytes 2949128 | tf_op jit(solution)/shard_map/ppermute | solution.py:65
  30.8 4.7 %collective-permute-done.7 = bf16[128,3328]{1,0:T(8,128)(2,1)S(1)} collective-permute-done((bf16[128,3328]{1,0:T(8,128)(2,1)S(1)}, bf16[128,3328]{1,0:T(8,128)(2,1)S(1)}, u32[]{:S(2)}, u32[]{:S(2)}) %collective-permute-start.7) | collective-permute-done | bytes 852000 | tf_op jit(solution)/shard_map/ppermute | solution.py:65
  35.8 4.0 %collective-permute-done.6 = bf16[128,3840]{1,0:T(8,128)(2,1)S(1)} collective-permute-done((bf16[128,3840]{1,0:T(8,128)(2,1)S(1)}, bf16[128,3840]{1,0:T(8,128)(2,1)S(1)}, u32[]{:S(2)}, u32[]{:S(2)}) %collective-permute-start.6) | collective-permute-done | bytes 983072 | tf_op jit(solution)/shard_map/ppermute | solution.py:65
  40.2 2.3 %collective-permute-done.4 = bf16[128,3840]{1,0:T(8,128)(2,1)S(1)} collective-permute-done((bf16[128,3840]{1,0:T(8,128)(2,1)S(1)}, bf16[128,3840]{1,0:T(8,128)(2,1)S(1)}, u32[]{:S(2)}, u32[]{:S(2)}) %collective-permute-start.4) | collective-permute-done | bytes 983072 | tf_op jit(solution)/shard_map/ppermute | solution.py:65
  43.5 2.5 %collective-permute-start.9 = (bf16[64,3840]{1,0:T(8,128)(2,1)S(1)}, bf16[64,3840]{1,0:T(8,128)(2,1)S(1)}, u32[]{:S(2)}, u32[]{:S(2)}) collective-permute-start(bf16[64,3840]{1,0:T(8,128)(2,1)S(1)} %slice.286), channel_id=1, source_target_pairs={{0,32},{1,97},{4,36},{5,101},{8,40},{9,105},{12,44},{13,109},{16,4... | collective-permute-start | bytes 1474568 | tf_op jit(solution)/shard_map/ppermute | solution.py:65
  46.0 5.2 %collective-permute-done.10 = bf16[64,3328]{1,0:T(8,128)(2,1)S(1)} collective-permute-done((bf16[64,3328]{1,0:T(8,128)(2,1)S(1)}, bf16[64,3328]{1,0:T(8,128)(2,1)S(1)}, u32[]{:S(2)}, u32[]{:S(2)}) %collective-permute-start.10) | collective-permute-done | bytes 426016 | tf_op jit(solution)/shard_map/ppermute | solution.py:65
  52.5 2.3 %collective-permute-done.8 = bf16[64,3840]{1,0:T(8,128)(2,1)S(1)} collective-permute-done((bf16[64,3840]{1,0:T(8,128)(2,1)S(1)}, bf16[64,3840]{1,0:T(8,128)(2,1)S(1)}, u32[]{:S(2)}, u32[]{:S(2)}) %collective-permute-start.8) | collective-permute-done | bytes 491552 | tf_op jit(solution)/shard_map/ppermute | solution.py:65
  55.3 2.2 %collective-permute-start.11 = (bf16[32,3840]{1,0:T(8,128)(2,1)S(1)}, bf16[32,3840]{1,0:T(8,128)(2,1)}, u32[]{:S(2)}, u32[]{:S(2)}) collective-permute-start(bf16[32,3840]{1,0:T(8,128)(2,1)S(1)} %slice.290), channel_id=1, source_target_pairs={{0,16},{1,19},{4,20},{5,23},{8,24},{9,27},{12,28},{13,31},{16,0},{... | collective-permute-start | bytes 737288 | tf_op jit(solution)/shard_map/ppermute | solution.py:65
  57.5 3.4 %collective-permute-done.13 = bf16[32,3328]{1,0:T(8,128)(2,1)S(1)} collective-permute-done((bf16[32,3328]{1,0:T(8,128)(2,1)S(1)}, bf16[32,3328]{1,0:T(8,128)(2,1)S(1)}, u32[]{:S(2)}, u32[]{:S(2)}) %collective-permute-start.13) | collective-permute-done | bytes 213024 | tf_op jit(solution)/shard_map/ppermute | solution.py:65
  64.2 10.7 %all_to_all.10 = bf16[8,4,11008]{2,1,0:T(4,128)(2,1)S(1)} all-to-all(bf16[8,4,11008]{2,1,0:T(4,128)(2,1)S(1)} %pad_maximum_fusion.3), channel_id=1, replica_groups={{0,12,18,30,96,108,114,126},{1,5,17,21,33,37,49,53},{4,8,22,26,100,104,..., dimensions={0} | all-to-all | bytes 1409024 | tf_op jit(solution)/shard_map/all_to_all | solution.py:61
  76.4 10.4 %all_to_all.11 = bf16[8,4,11008]{2,1,0:T(4,128)(2,1)S(1)} all-to-all(bf16[8,4,11008]{2,1,0:T(4,128)(2,1)S(1)} %broadcast_in_dim.5), channel_id=1, replica_groups={{0,12,18,30,96,108,114,126},{1,5,17,21,33,37,49,53},{4,8,22,26,100,104,..., dimensions={0} | all-to-all | bytes 1409024 | tf_op jit(solution)/shard_map/all_to_all | solution.py:61
  87.0 1.8 %collective-permute-start.14 = (bf16[32,3328]{1,0:T(8,128)(2,1)S(1)}, bf16[32,3328]{1,0:T(8,128)(2,1)S(1)}, u32[]{:S(2)}, u32[]{:S(2)}) collective-permute-start(bf16[32,3328]{1,0:T(8,128)(2,1)S(1)} %slice.233), channel_id=1, source_target_pairs={{0,32},{1,97},{4,36},{5,101},{8,40},{9,105},{12,44},{13,109},{16,4... | collective-permute-start | bytes 638984 | tf_op jit(solution)/shard_map/ppermute | solution.py:65
  89.8 5.4 %collective-permute-done.14 = bf16[32,3328]{1,0:T(8,128)(2,1)S(1)} collective-permute-done((bf16[32,3328]{1,0:T(8,128)(2,1)S(1)}, bf16[32,3328]{1,0:T(8,128)(2,1)S(1)}, u32[]{:S(2)}, u32[]{:S(2)}) %collective-permute-start.14) | collective-permute-done | bytes 213024 | tf_op jit(solution)/shard_map/ppermute | solution.py:65
  95.2 2.3 %collective-permute-done.16 = bf16[32,3840]{1,0:T(8,128)(2,1)S(1)} collective-permute-done((bf16[32,3840]{1,0:T(8,128)(2,1)S(1)}, bf16[32,3840]{1,0:T(8,128)(2,1)S(1)}, u32[]{:S(2)}, u32[]{:S(2)}) %collective-permute-start.16) | collective-permute-done | bytes 245792 | tf_op jit(solution)/shard_map/ppermute | solution.py:65
  99.1 1.6 %collective-permute-start.17 = (bf16[64,3328]{1,0:T(8,128)(2,1)S(1)}, bf16[64,3328]{1,0:T(8,128)(2,1)S(1)}, u32[]{:S(2)}, u32[]{:S(2)}) collective-permute-start(bf16[64,3328]{1,0:T(8,128)(2,1)S(1)} %pad_maximum_fusion.6), channel_id=1, source_target_pairs={{0,16},{1,19},{4,20},{5,23},{8,24},{9,27},{12,28},{13,31},{16,0},{... | collective-permute-start | bytes 1277960 | tf_op jit(solution)/shard_map/ppermute | solution.py:65
  100.7 5.8 %collective-permute-done.18 = bf16[64,3840]{1,0:T(8,128)(2,1)S(1)} collective-permute-done((bf16[64,3840]{1,0:T(8,128)(2,1)S(1)}, bf16[64,3840]{1,0:T(8,128)(2,1)S(1)}, u32[]{:S(2)}, u32[]{:S(2)}) %collective-permute-start.18) | collective-permute-done | bytes 491552 | tf_op jit(solution)/shard_map/ppermute | solution.py:65
  107.0 6.5 %collective-permute-start.25 = (bf16[256,3840]{1,0:T(8,128)(2,1)S(1)}, bf16[256,3840]{1,0:T(8,128)(2,1)S(1)}, u32[]{:S(2)}, u32[]{:S(2)}) collective-permute-start(bf16[256,3840]{1,0:T(8,128)(2,1)S(1)} %constant_dynamic-update-slice_fusion.8), channel_id=1, source_target_pairs={{0,1},{1,0},{2,3},{3,2},{4,5},{5,4},{6,7},{7,6},{8,9},{9,8},{10,11... | collective-permute-start | bytes 5898248 | tf_op jit(solution)/shard_map/ppermute | solution.py:65
  113.7 1.7 %collective-permute-start.23 = (bf16[128,3840]{1,0:T(8,128)(2,1)S(1)}, bf16[128,3840]{1,0:T(8,128)(2,1)S(1)}, u32[]{:S(2)}, u32[]{:S(2)}) collective-permute-start(bf16[128,3840]{1,0:T(8,128)(2,1)S(1)} %pad_maximum_fusion.refs_0_), channel_id=1, source_target_pairs={{0,32},{1,97},{4,36},{5,101},{8,40},{9,105},{12,44},{13,109},{16,4... | collective-permute-start | bytes 2949128 | tf_op jit(solution)/shard_map/ppermute | solution.py:65
  119.1 8.9 %collective-permute-done.23.refs_2_ = bf16[128,3840]{1,0:T(8,128)(2,1)S(1)} collective-permute-done((bf16[128,3840]{1,0:T(8,128)(2,1)S(1)}, bf16[128,3840]{1,0:T(8,128)(2,1)S(1)}, u32[]{:S(2)}, u32[]{:S(2)}) %collective-permute-start.23) | collective-permute-done | bytes 983072 | tf_op jit(solution)/shard_map/ppermute | solution.py:65
  128.0 1.6 %collective-permute-done.24.refs_2_ = bf16[128,3840]{1,0:T(8,128)(2,1)S(1)} collective-permute-done((bf16[128,3840]{1,0:T(8,128)(2,1)S(1)}, bf16[128,3840]{1,0:T(8,128)(2,1)S(1)}, u32[]{:S(2)}, u32[]{:S(2)}) %collective-permute-start.24) | collective-permute-done | bytes 983072 | tf_op jit(solution)/shard_map/ppermute | solution.py:65
  130.5 1.7 %collective-permute-done.27.refs_3_ = bf16[128,3840]{1,0:T(8,128)(2,1)S(1)} collective-permute-done((bf16[128,3840]{1,0:T(8,128)(2,1)S(1)}, bf16[128,3840]{1,0:T(8,128)(2,1)S(1)}, u32[]{:S(2)}, u32[]{:S(2)}) %collective-permute-start.27) | collective-permute-done | bytes 983072 | tf_op jit(solution)/shard_map/ppermute | solution.py:65
  132.2 2.2 %expand.3.refs_4_ = f32[128,11008]{1,0:T(8,128)} custom-call(bf16[128,1536]{1,0:T(8,128)(2,1)S(1)} %constant_dynamic-update-slice_fusion.basis_ref, bf16[128,3840]{1,0:T(8,128)(2,1)S(1)} %pad_maximum_fusion.refs_0_, bf16[256,3840]{1,0:T(8,128)(2,1)S(1)} %collective-permute-done.25.refs_1_, bf16[128,3840]{1,0:T(8,128)(2,1)S(1)} %collective-permute-done.23.refs_2_, ...), custom_call_target="tpu_custom_call" | custom-call | flops 503316480 | bytes 5898240 | tf_op jit(solution)/shard_map/expand/pallas_call | solution.py:152
  134.4 2.2 %expand.4.refs_4_ = f32[128,11008]{1,0:T(8,128)} custom-call(bf16[128,1536]{1,0:T(8,128)(2,1)S(1)} %constant_dynamic-update-slice_fusion.basis_ref, bf16[128,3840]{1,0:T(8,128)(2,1)S(1)} %pad_maximum_fusion.1.refs_0_, bf16[256,3840]{1,0:T(8,128)(2,1)S(1)} %collective-permute-done.25.refs_1_, ...), custom_call_target="tpu_custom_call", output_to_operand_aliasing={{}: (5, {})} | custom-call | flops 503316480 | bytes 5898240 | tf_op jit(solution)/shard_map/expand/pallas_call | solution.py:152
  136.6 2.3 %expand.5 = f32[128,11008]{1,0:T(8,128)} custom-call(bf16[128,1536]{1,0:T(8,128)(2,1)S(1)} %constant_dynamic-update-slice_fusion.basis_ref, bf16[128,3328]{1,0:T(8,128)(2,1)S(1)} %pad_maximum_fusion.2.refs_0_, bf16[128,3328]{1,0:T(8,128)(2,1)S(1)} %collective-permute-done.21.refs_1_, ...), custom_call_target="tpu_custom_call", output_to_operand_aliasing={{}: (5, {})} | custom-call | flops 436207616 | bytes 5111808 | tf_op jit(solution)/shard_map/expand/pallas_call | solution.py:152
  (100 shorter events, 21.3 us)
Async XLA Ops:
  0.8 2.2 %copy-start = (bf16[4096,512]{1,0:T(8,128)(2,1)S(1)}, bf16[4096,512]{1,0:T(8,128)(2,1)}, u32[]{:S(2)}) copy-start(bf16[4096,512]{1,0:T(8,128)(2,1)} %rows_ref.1) | copy-start | bytes 12582916
  5.2 4.6 %copy-start.2 = (bf16[512,11008]{1,0:T(8,128)(2,1)S(1)}, bf16[512,11008]{1,0:T(8,128)(2,1)}, u32[]{:S(2)}) copy-start(bf16[512,11008]{1,0:T(8,128)(2,1)} %param.6) | copy-start | bytes 33816580
  12.2 8.1 %collective-permute-start.2 = (bf16[128,3840]{1,0:T(8,128)(2,1)S(1)}, bf16[128,3840]{1,0:T(8,128)(2,1)S(1)}, u32[]{:S(2)}, u32[]{:S(2)}) collective-permute-start(bf16[128,3840]{1,0:T(8,128)(2,1)S(1)} %get-tuple-element.65), channel_id=1, source_target_pairs={{0,1},{1,0},{2,3},{3,2},{4,5},{5,4},{6,7},{7,6},{8,9},{9,8},{10,11... | collective-permute-start | bytes 2949128 | tf_op jit(solution)/shard_map/ppermute | solution.py:65
  15.8 5.5 %collective-permute-start.3 = (bf16[256,3328]{1,0:T(8,128)(2,1)S(1)}, bf16[256,3328]{1,0:T(8,128)(2,1)S(1)}, u32[]{:S(2)}, u32[]{:S(2)}) collective-permute-start(bf16[256,3328]{1,0:T(8,128)(2,1)S(1)} %slice.208), channel_id=1, source_target_pairs={{0,1},{1,0},{2,3},{3,2},{4,5},{5,4},{6,7},{7,6},{8,9},{9,8},{10,11... | collective-permute-start | bytes 5111816 | tf_op jit(solution)/shard_map/ppermute | solution.py:65
  18.3 2.8 %collective-permute-start.1 = (bf16[128,3840]{1,0:T(8,128)(2,1)S(1)}, bf16[128,3840]{1,0:T(8,128)(2,1)S(1)}, u32[]{:S(2)}, u32[]{:S(2)}) collective-permute-start(bf16[128,3840]{1,0:T(8,128)(2,1)S(1)} %get-tuple-element.67), channel_id=1, source_target_pairs={{0,1},{1,0},{2,3},{3,2},{4,5},{5,4},{6,7},{7,6},{8,9},{9,8},{10,11... | collective-permute-start | bytes 2949128 | tf_op jit(solution)/shard_map/ppermute | solution.py:65
  18.9 16.9 %collective-permute-start.5 = (bf16[128,3840]{1,0:T(8,128)(2,1)S(1)}, bf16[128,3840]{1,0:T(8,128)(2,1)S(1)}, u32[]{:S(2)}, u32[]{:S(2)}) collective-permute-start(bf16[128,3840]{1,0:T(8,128)(2,1)S(1)} %get-tuple-element.64), channel_id=1, source_target_pairs={{0,1},{1,0},{2,3},{3,2},{4,5},{5,4},{6,7},{7,6},{8,9},{9,8},{10,11... | collective-permute-start | bytes 2949128 | tf_op jit(solution)/shard_map/ppermute | solution.py:65
  19.0 21.2 %collective-permute-start = (bf16[128,3840]{1,0:T(8,128)(2,1)S(1)}, bf16[128,3840]{1,0:T(8,128)(2,1)S(1)}, u32[]{:S(2)}, u32[]{:S(2)}) collective-permute-start(bf16[128,3840]{1,0:T(8,128)(2,1)S(1)} %get-tuple-element.66), channel_id=1, source_target_pairs={{0,1},{1,0},{2,3},{3,2},{4,5},{5,4},{6,7},{7,6},{8,9},{9,8},{10,11... | collective-permute-start | bytes 2949128 | tf_op jit(solution)/shard_map/ppermute | solution.py:65
  21.5 14.0 %collective-permute-start.7 = (bf16[128,3328]{1,0:T(8,128)(2,1)S(1)}, bf16[128,3328]{1,0:T(8,128)(2,1)S(1)}, u32[]{:S(2)}, u32[]{:S(2)}) collective-permute-start(bf16[128,3328]{1,0:T(8,128)(2,1)S(1)} %add_convert_fusion.2), channel_id=1, source_target_pairs={{0,4},{1,13},{4,0},{5,9},{8,12},{9,5},{12,8},{13,1},{16,20},{17,29... | collective-permute-start | bytes 2555912 | tf_op jit(solution)/shard_map/ppermute | solution.py:65
  25.5 14.3 %collective-permute-start.6 = (bf16[128,3840]{1,0:T(8,128)(2,1)S(1)}, bf16[128,3840]{1,0:T(8,128)(2,1)S(1)}, u32[]{:S(2)}, u32[]{:S(2)}) collective-permute-start(bf16[128,3840]{1,0:T(8,128)(2,1)S(1)} %add_convert_fusion), channel_id=1, source_target_pairs={{0,16},{1,19},{4,20},{5,23},{8,24},{9,27},{12,28},{13,31},{16,0},{... | collective-permute-start | bytes 2949128 | tf_op jit(solution)/shard_map/ppermute | solution.py:65
  28.3 14.2 %collective-permute-start.4 = (bf16[128,3840]{1,0:T(8,128)(2,1)S(1)}, bf16[128,3840]{1,0:T(8,128)(2,1)S(1)}, u32[]{:S(2)}, u32[]{:S(2)}) collective-permute-start(bf16[128,3840]{1,0:T(8,128)(2,1)S(1)} %add_convert_fusion.1), channel_id=1, source_target_pairs={{0,32},{1,97},{4,36},{5,101},{8,40},{9,105},{12,44},{13,109},{16,4... | collective-permute-start | bytes 2949128 | tf_op jit(solution)/shard_map/ppermute | solution.py:65
  43.0 8.3 %collective-permute-start.10 = (bf16[64,3328]{1,0:T(8,128)(2,1)S(1)}, bf16[64,3328]{1,0:T(8,128)(2,1)S(1)}, u32[]{:S(2)}, u32[]{:S(2)}) collective-permute-start(bf16[64,3328]{1,0:T(8,128)(2,1)S(1)} %slice.288), channel_id=1, source_target_pairs={{0,16},{1,19},{4,20},{5,23},{8,24},{9,27},{12,28},{13,31},{16,0},{... | collective-permute-start | bytes 1277960 | tf_op jit(solution)/shard_map/ppermute | solution.py:65
  43.5 8.9 %collective-permute-start.9 = (bf16[64,3840]{1,0:T(8,128)(2,1)S(1)}, bf16[64,3840]{1,0:T(8,128)(2,1)S(1)}, u32[]{:S(2)}, u32[]{:S(2)}) collective-permute-start(bf16[64,3840]{1,0:T(8,128)(2,1)S(1)} %slice.286), channel_id=1, source_target_pairs={{0,32},{1,97},{4,36},{5,101},{8,40},{9,105},{12,44},{13,109},{16,4... | collective-permute-start | bytes 1474568 | tf_op jit(solution)/shard_map/ppermute | solution.py:65
  46.0 8.9 %collective-permute-start.8 = (bf16[64,3840]{1,0:T(8,128)(2,1)S(1)}, bf16[64,3840]{1,0:T(8,128)(2,1)S(1)}, u32[]{:S(2)}, u32[]{:S(2)}) collective-permute-start(bf16[64,3840]{1,0:T(8,128)(2,1)S(1)} %slice.287), channel_id=1, source_target_pairs={{0,4},{1,13},{4,0},{5,9},{8,12},{9,5},{12,8},{13,1},{16,20},{17,29... | collective-permute-start | bytes 1474568 | tf_op jit(solution)/shard_map/ppermute | solution.py:65
  55.0 6.0 %collective-permute-start.13 = (bf16[32,3328]{1,0:T(8,128)(2,1)S(1)}, bf16[32,3328]{1,0:T(8,128)(2,1)S(1)}, u32[]{:S(2)}, u32[]{:S(2)}) collective-permute-start(bf16[32,3328]{1,0:T(8,128)(2,1)S(1)} %slice.291), channel_id=1, source_target_pairs={{0,32},{1,97},{4,36},{5,101},{8,40},{9,105},{12,44},{13,109},{16,4... | collective-permute-start | bytes 638984 | tf_op jit(solution)/shard_map/ppermute | solution.py:65
  55.3 6.4 %collective-permute-start.11 = (bf16[32,3840]{1,0:T(8,128)(2,1)S(1)}, bf16[32,3840]{1,0:T(8,128)(2,1)}, u32[]{:S(2)}, u32[]{:S(2)}) collective-permute-start(bf16[32,3840]{1,0:T(8,128)(2,1)S(1)} %slice.290), channel_id=1, source_target_pairs={{0,16},{1,19},{4,20},{5,23},{8,24},{9,27},{12,28},{13,31},{16,0},{... | collective-permute-start | bytes 737288 | tf_op jit(solution)/shard_map/ppermute | solution.py:65
  57.5 6.3 %collective-permute-start.12 = (bf16[32,3840]{1,0:T(8,128)(2,1)S(1)}, bf16[32,3840]{1,0:T(8,128)(2,1)S(1)}, u32[]{:S(2)}, u32[]{:S(2)}) collective-permute-start(bf16[32,3840]{1,0:T(8,128)(2,1)S(1)} %slice.289), channel_id=1, source_target_pairs={{0,4},{1,13},{4,0},{5,9},{8,12},{9,5},{12,8},{13,1},{16,20},{17,29... | collective-permute-start | bytes 737288 | tf_op jit(solution)/shard_map/ppermute | solution.py:65
  63.9 11.3 %copy-start.3 = (f32[4,11008]{1,0:T(4,128)S(1)}, f32[4,11008]{1,0:T(4,128)}, u32[]{:S(2)}) copy-start(f32[4,11008]{1,0:T(4,128)} %param.8) | copy-start | bytes 528388
  63.9 11.3 %copy-start.4 = (f32[4,11008]{1,0:T(4,128)S(1)}, f32[4,11008]{1,0:T(4,128)}, u32[]{:S(2)}) copy-start(f32[4,11008]{1,0:T(4,128)} %param.9) | copy-start | bytes 528388
  87.0 8.2 %collective-permute-start.14 = (bf16[32,3328]{1,0:T(8,128)(2,1)S(1)}, bf16[32,3328]{1,0:T(8,128)(2,1)S(1)}, u32[]{:S(2)}, u32[]{:S(2)}) collective-permute-start(bf16[32,3328]{1,0:T(8,128)(2,1)S(1)} %slice.233), channel_id=1, source_target_pairs={{0,32},{1,97},{4,36},{5,101},{8,40},{9,105},{12,44},{13,109},{16,4... | collective-permute-start | bytes 638984 | tf_op jit(solution)/shard_map/ppermute | solution.py:65
  88.7 8.8 %collective-permute-start.15 = (bf16[32,3840]{1,0:T(8,128)(2,1)S(1)}, bf16[32,3840]{1,0:T(8,128)(2,1)S(1)}, u32[]{:S(2)}, u32[]{:S(2)}) collective-permute-start(bf16[32,3840]{1,0:T(8,128)(2,1)S(1)} %get-tuple-element.48), channel_id=1, source_target_pairs={{0,16},{1,19},{4,20},{5,23},{8,24},{9,27},{12,28},{13,31},{16,0},{... | collective-permute-start | bytes 737288 | tf_op jit(solution)/shard_map/ppermute | solution.py:65
  89.8 7.7 %collective-permute-start.16 = (bf16[32,3840]{1,0:T(8,128)(2,1)S(1)}, bf16[32,3840]{1,0:T(8,128)(2,1)S(1)}, u32[]{:S(2)}, u32[]{:S(2)}) collective-permute-start(bf16[32,3840]{1,0:T(8,128)(2,1)S(1)} %get-tuple-element.49), channel_id=1, source_target_pairs={{0,4},{1,13},{4,0},{5,9},{8,12},{9,5},{12,8},{13,1},{16,20},{17,29... | collective-permute-start | bytes 737288 | tf_op jit(solution)/shard_map/ppermute | solution.py:65
  97.6 9.0 %collective-permute-start.18 = (bf16[64,3840]{1,0:T(8,128)(2,1)S(1)}, bf16[64,3840]{1,0:T(8,128)(2,1)S(1)}, u32[]{:S(2)}, u32[]{:S(2)}) collective-permute-start(bf16[64,3840]{1,0:T(8,128)(2,1)S(1)} %pad_maximum_fusion.4), channel_id=1, source_target_pairs={{0,4},{1,13},{4,0},{5,9},{8,12},{9,5},{12,8},{13,1},{16,20},{17,29... | collective-permute-start | bytes 1474568 | tf_op jit(solution)/shard_map/ppermute | solution.py:65
  98.1 8.9 %collective-permute-start.19 = (bf16[64,3840]{1,0:T(8,128)(2,1)S(1)}, bf16[64,3840]{1,0:T(8,128)(2,1)S(1)}, u32[]{:S(2)}, u32[]{:S(2)}) collective-permute-start(bf16[64,3840]{1,0:T(8,128)(2,1)S(1)} %pad_maximum_fusion.5), channel_id=1, source_target_pairs={{0,32},{1,97},{4,36},{5,101},{8,40},{9,105},{12,44},{13,109},{16,4... | collective-permute-start | bytes 1474568 | tf_op jit(solution)/shard_map/ppermute | solution.py:65
  99.1 14.4 %collective-permute-start.17 = (bf16[64,3328]{1,0:T(8,128)(2,1)S(1)}, bf16[64,3328]{1,0:T(8,128)(2,1)S(1)}, u32[]{:S(2)}, u32[]{:S(2)}) collective-permute-start(bf16[64,3328]{1,0:T(8,128)(2,1)S(1)} %pad_maximum_fusion.6), channel_id=1, source_target_pairs={{0,16},{1,19},{4,20},{5,23},{8,24},{9,27},{12,28},{13,31},{16,0},{... | collective-permute-start | bytes 1277960 | tf_op jit(solution)/shard_map/ppermute | solution.py:65
  107.0 22.6 %collective-permute-start.25 = (bf16[256,3840]{1,0:T(8,128)(2,1)S(1)}, bf16[256,3840]{1,0:T(8,128)(2,1)S(1)}, u32[]{:S(2)}, u32[]{:S(2)}) collective-permute-start(bf16[256,3840]{1,0:T(8,128)(2,1)S(1)} %constant_dynamic-update-slice_fusion.8), channel_id=1, source_target_pairs={{0,1},{1,0},{2,3},{3,2},{4,5},{5,4},{6,7},{7,6},{8,9},{9,8},{10,11... | collective-permute-start | bytes 5898248 | tf_op jit(solution)/shard_map/ppermute | solution.py:65
  113.7 14.2 %collective-permute-start.23 = (bf16[128,3840]{1,0:T(8,128)(2,1)S(1)}, bf16[128,3840]{1,0:T(8,128)(2,1)S(1)}, u32[]{:S(2)}, u32[]{:S(2)}) collective-permute-start(bf16[128,3840]{1,0:T(8,128)(2,1)S(1)} %pad_maximum_fusion.refs_0_), channel_id=1, source_target_pairs={{0,32},{1,97},{4,36},{5,101},{8,40},{9,105},{12,44},{13,109},{16,4... | collective-permute-start | bytes 2949128 | tf_op jit(solution)/shard_map/ppermute | solution.py:65
  115.4 14.2 %collective-permute-start.24 = (bf16[128,3840]{1,0:T(8,128)(2,1)S(1)}, bf16[128,3840]{1,0:T(8,128)(2,1)S(1)}, u32[]{:S(2)}, u32[]{:S(2)}) collective-permute-start(bf16[128,3840]{1,0:T(8,128)(2,1)S(1)} %pad_maximum_fusion.1.refs_0_), channel_id=1, source_target_pairs={{0,16},{1,19},{4,20},{5,23},{8,24},{9,27},{12,28},{13,31},{16,0},{... | collective-permute-start | bytes 2949128 | tf_op jit(solution)/shard_map/ppermute | solution.py:65
  116.5 13.6 %collective-permute-start.21 = (bf16[128,3328]{1,0:T(8,128)(2,1)S(1)}, bf16[128,3328]{1,0:T(8,128)(2,1)S(1)}, u32[]{:S(2)}, u32[]{:S(2)}) collective-permute-start(bf16[128,3328]{1,0:T(8,128)(2,1)S(1)} %pad_maximum_fusion.2.refs_0_), channel_id=1, source_target_pairs={{0,1},{1,0},{2,3},{3,2},{4,5},{5,4},{6,7},{7,6},{8,9},{9,8},{10,11... | collective-permute-start | bytes 2555912 | tf_op jit(solution)/shard_map/ppermute | solution.py:65
  117.7 12.8 %collective-permute-start.20 = (bf16[128,3328]{1,0:T(8,128)(2,1)S(1)}, bf16[128,3328]{1,0:T(8,128)(2,1)S(1)}, u32[]{:S(2)}, u32[]{:S(2)}) collective-permute-start(bf16[128,3328]{1,0:T(8,128)(2,1)S(1)} %pad_maximum_fusion.2.refs_0_), channel_id=1, source_target_pairs={{0,4},{1,13},{4,0},{5,9},{8,12},{9,5},{12,8},{13,1},{16,20},{17,29... | collective-permute-start | bytes 2555912 | tf_op jit(solution)/shard_map/ppermute | solution.py:65
  129.6 2.6 %collective-permute-start.27 = (bf16[128,3840]{1,0:T(8,128)(2,1)S(1)}, bf16[128,3840]{1,0:T(8,128)(2,1)S(1)}, u32[]{:S(2)}, u32[]{:S(2)}) collective-permute-start(bf16[128,3840]{1,0:T(8,128)(2,1)S(1)} %collective-permute-done.23.refs_2_), channel_id=1, source_target_pairs={{0,1},{1,0},{2,3},{3,2},{4,5},{5,4},{6,7},{7,6},{8,9},{9,8},{10,11... | collective-permute-start | bytes 2949128 | tf_op jit(solution)/shard_map/ppermute | solution.py:65
  129.8 4.6 %collective-permute-start.26 = (bf16[128,3840]{1,0:T(8,128)(2,1)S(1)}, bf16[128,3840]{1,0:T(8,128)(2,1)S(1)}, u32[]{:S(2)}, u32[]{:S(2)}) collective-permute-start(bf16[128,3840]{1,0:T(8,128)(2,1)S(1)} %collective-permute-done.24.refs_2_), channel_id=1, source_target_pairs={{0,1},{1,0},{2,3},{3,2},{4,5},{5,4},{6,7},{7,6},{8,9},{9,8},{10,11... | collective-permute-start | bytes 2949128 | tf_op jit(solution)/shard_map/ppermute | solution.py:65
  130.4 6.1 %collective-permute-start.22 = (bf16[128,3328]{1,0:T(8,128)(2,1)S(1)}, bf16[128,3328]{1,0:T(8,128)(2,1)S(1)}, u32[]{:S(2)}, u32[]{:S(2)}) collective-permute-start(bf16[128,3328]{1,0:T(8,128)(2,1)S(1)} %collective-permute-done.20.refs_2_), channel_id=1, source_target_pairs={{0,1},{1,0},{2,3},{3,2},{4,5},{5,4},{6,7},{7,6},{8,9},{9,8},{10,11... | collective-permute-start | bytes 2555912 | tf_op jit(solution)/shard_map/ppermute | solution.py:65
  (1 other events, 2.2 us)
